TPU v7x, 256 devices: a whole 4x4x8 slice. The times are simulated.
256 devices in a mesh: rows: 64 (over z, x, core), cols: 4 (over y).
Axes of the slice: x: 4, y: 4, z: 8, core: 2. Of those that a mesh axis runs over, the one named last changes fastest.
Arguments:
- activations: bfloat16 [131072, 8192], P('rows', 'cols'), may hold values from -120 to 120
- sketch: bfloat16 [8192, 256], P('cols'), may hold values from -0.0625 to 0.0625
Outputs:
- basis: bfloat16 [131072, 256], P(('rows', 'cols'))
- projected: float32 [256, 8192], P(None, 'cols')
All inputs are finite; a program needn't handle non-finite values.
Results may differ from a plain program's by a relative error of at most 0.0051.
Values may be sent and summed in bfloat16 or wider, within the bound.
No kernel may reach another device: no remote copies, remote signals or barrier semaphores. Data moves between devices by JAX's collectives and lax.ppermute only.
A program may use at most 64 MiB of HBM per device.

v0:
```python
import math

import jax
import jax.numpy as jnp
from jax import lax
from jax.sharding import PartitionSpec as P


def per_device(activations, sketch):
    rows_here, width_here = activations.shape
    token_count = rows_here * lax.axis_size("rows")
    inverse_root = 1.0 / math.sqrt(token_count)
    row_block = activations
    image_part = lax.psum_scatter(
        jnp.dot(row_block, sketch, preferred_element_type=jnp.float32),
        "cols",
        scatter_dimension=0,
        tiled=True,
    )
    image_low = image_part.astype(jnp.bfloat16)
    row_block = activations
    back_part = lax.dot_general(
        row_block,
        lax.all_gather(image_low, "cols", axis=0, tiled=True),
        (((0,), (0,)), ((), ())),
        preferred_element_type=jnp.float32,
    )
    back_image = lax.psum(back_part, "rows").astype(jnp.bfloat16)
    row_block = activations
    power_image = lax.psum_scatter(
        jnp.dot(row_block, back_image, preferred_element_type=jnp.float32),
        "cols",
        scatter_dimension=0,
        tiled=True,
    )
    gram_local = jnp.dot(
        power_image.T,
        power_image,
        precision=lax.Precision.HIGHEST,
        preferred_element_type=jnp.float32,
    )
    gram_matrix = lax.psum(gram_local, ("rows", "cols"))
    gram_matrix = gram_matrix / token_count
    factor = jnp.linalg.cholesky(gram_matrix)
    solved = jax.scipy.linalg.solve_triangular(factor, power_image.T, lower=True)
    basis = solved.T.astype(jnp.bfloat16)
    row_block = activations
    projection_part = lax.dot_general(
        lax.all_gather(basis, "cols", axis=0, tiled=True),
        row_block,
        (((0,), (0,)), ((), ())),
        preferred_element_type=jnp.float32,
    )
    projected = lax.psum(projection_part, "rows") * inverse_root
    return (basis, projected)


def solution(mesh):
    placed = (P("rows", "cols"), P("cols", None))
    return jax.shard_map(
        per_device,
        mesh=mesh,
        in_specs=placed,
        out_specs=(P(("rows", "cols"), None), P(None, "cols")),
        check_vma=False,
    )
```

profile of v0, /device:TPU:1, one launch (start us, length us, event | category | flops | bytes accessed | tf_op | source)
XLA Modules:
  0.0 945.6 jit_solution(11068070381292719362)
XLA Ops:
  7.2 1.2 copy-done
  8.4 7.1 fusion.10
  15.5 36.2 %reduce-scatter.3.cloned.1.call-done = f32[512,256]{1,0:T(8,128)} async-done(((f32[2048,256]{1,0:T(8,128)}), f32[512,256]{1,0:T(8,128)}) %reduce-scatter.3.cloned.1.call-update) | async-done | bytes 524304 | tf_op jit(solution)/shard_map/reduce_scatter | solution.py:14
  51.7 1.8 convert_element_type.10
  53.6 26.0 %all-gather.3.cloned.1.call-done = bf16[2048,256]{1,0:T(8,128)(2,1)} async-done(((bf16[512,256]{1,0:T(8,128)(2,1)}), bf16[2048,256]{1,0:T(8,128)(2,1)}) %all-gather.3.cloned.1.call-update) | async-done | bytes 1048592 | tf_op jit(solution)/shard_map/all_gather | solution.py:24
  79.6 6.1 convolution_bitcast_fusion.1
  85.7 267.0 %all-reduce.8 = bf16[2048,256]{0,1:T(8,128)(2,1)} all-reduce(f32[2048,256]{0,1:T(8,128)S(1)} %convolution_bitcast_fusion.1), channel_id=1, replica_groups=mesh['rows'=64,'cols'=4] {'rows'}, use_global_device_ids=true, to_apply=%region_1.0 | all-reduce | flops 524288 | bytes 3145728 | tf_op jit(solution)/shard_map/psum | solution.py:28
  352.7 7.4 convolution_bitcast_fusion
  360.2 32.7 %reduce-scatter.5.cloned.1.call-done = f32[512,256]{0,1:T(8,128)} async-done(((f32[2048,256]{0,1:T(8,128)}), f32[512,256]{0,1:T(8,128)}) %reduce-scatter.5.cloned.1.call-update) | async-done | bytes 524304 | tf_op jit(solution)/shard_map/reduce_scatter | solution.py:30
  392.9 2.5 fusion.11
  395.6 251.6 %all-reduce.5.cloned.1.call-done = f32[256,256]{0,1:T(8,128)} async-done(((f32[256,256]{0,1:T(8,128)}), f32[256,256]{0,1:T(8,128)}) %all-reduce.5.cloned.1.call-update) | async-done | bytes 262160 | tf_op jit(solution)/shard_map/psum | solution.py:42
  647.3 1.0 broadcast_multiply_fusion.1
  648.4 1.0 fusion.3
  649.4 11.7 %cholesky.50 = f32[128,128]{1,0:T(8,128)S(1)} custom-call(f32[128,128]{1,0:T(8,128)S(1)} %cholesky.118), custom_call_target="Cholesky" | custom-call | tf_op jit(solution)/shard_map/jit(cholesky)/cholesky | solution.py:44
  661.1 9.8 %custom-call.15 = f32[1,128,128]{1,2,0:T(8,128)S(1)} custom-call(f32[1,128,128]{2,1,0:T(8,128)S(1)} %get-tuple-element.25), custom_call_target="InvertDiagBlocksLowerTriangular" | custom-call | tf_op jit(solution)/shard_map/jit(cholesky)/cholesky | solution.py:44
  671.4 11.7 %cholesky.105 = f32[128,128]{1,0:T(8,128)S(1)} custom-call(f32[128,128]{1,0:T(8,128)S(1)} %convolution_subtract_fusion.1), custom_call_target="Cholesky" | custom-call | tf_op jit(solution)/shard_map/jit(cholesky)/cholesky | solution.py:44
  683.2 0.6 compare_reduce_fusion
  685.2 4.0 while.1
  685.4 0.6 fusion.28
  685.9 1.3 bitcast_dynamic-update-slice_fusion.2
  687.3 0.6 fusion.28
  687.9 1.3 bitcast_dynamic-update-slice_fusion.2
  689.2 19.7 %custom-call.16 = f32[2,128,128]{1,2,0:T(8,128)S(1)} custom-call(f32[2,128,128]{2,1,0:T(8,128)S(1)} %get-tuple-element.9), custom_call_target="InvertDiagBlocksLowerTriangular" | custom-call | tf_op jit(solution)/shard_map/jit(_solve_triangular)/triangular_solve | solution.py:45
  708.9 1.4 fusion.9
  710.2 1.3 convolution_subtract_fusion
  711.6 0.4 convolution_convert_fusion
  712.0 0.7 maximum_bitcast_fusion
  712.8 25.8 %all-gather.5.cloned.1.call-done = bf16[2048,256]{0,1:T(8,128)(2,1)} async-done(((bf16[512,256]{0,1:T(8,128)(2,1)}), bf16[2048,256]{0,1:T(8,128)(2,1)}) %all-gather.5.cloned.1.call-update) | async-done | bytes 1048592 | tf_op jit(solution)/shard_map/all_gather | solution.py:49
  738.6 7.4 fusion.12
  746.0 0.8 copy.6
  746.9 188.6 %all-reduce.7.cloned.1.call-done = f32[256,2048]{1,0:T(8,128)} async-done(((f32[256,2048]{1,0:T(8,128)}), f32[256,2048]{1,0:T(8,128)}) %all-reduce.7.cloned.1.call-update) | async-done | bytes 2097168 | tf_op jit(solution)/shard_map/psum | solution.py:54
  935.5 3.2 broadcast_multiply_fusion
  (28 shorter events, 1.4 us)
Async XLA Ops:
  7.2 1.2 copy-start
  7.2 44.5 %reduce-scatter.3.cloned.1.call-start = ((), (), s32[]{:S(2)}) async-start(), calls=%async_computation.2 | async-start | bytes 2621440 | tf_op jit(solution)/shard_map/reduce_scatter | solution.py:14
  15.5 64.1 %all-gather.3.cloned.1.call-start = ((), (), s32[]{:S(2)}) async-start(), calls=%async_computation.3 | async-start | bytes 1310720 | tf_op jit(solution)/shard_map/all_gather | solution.py:24
  53.5 339.3 %reduce-scatter.5.cloned.1.call-start = ((), (), s32[]{:S(2)}) async-start(), calls=%async_computation.4 | async-start | bytes 2621440 | tf_op jit(solution)/shard_map/reduce_scatter | solution.py:30
  360.1 287.2 %all-reduce.5.cloned.1.call-start = ((), (), s32[]{:S(2)}) async-start(), calls=%async_computation.5 | async-start | bytes 524288 | tf_op jit(solution)/shard_map/psum | solution.py:42
  395.4 343.2 %all-gather.5.cloned.1.call-start = ((), (), s32[]{:S(2)}) async-start(), calls=%async_computation.6 | async-start | bytes 1310720 | tf_op jit(solution)/shard_map/all_gather | solution.py:49
  712.7 33.3 %copy-start.1 = (bf16[512,256]{0,1:T(8,128)(2,1)S(1)}, bf16[512,256]{0,1:T(8,128)(2,1)}, u32[]{:S(2)}) copy-start(bf16[512,256]{0,1:T(8,128)(2,1)} %maximum_bitcast_fusion) | copy-start | bytes 786436
  712.8 222.8 %all-reduce.7.cloned.1.call-start = ((), (), s32[]{:S(2)}) async-start(), calls=%async_computation.7 | async-start | bytes 4194304 | tf_op jit(solution)/shard_map/psum | solution.py:54
Sparse Core Ops, SparseCore 0:
  15.6 36.0 reduce-scatter.2
  54.2 25.3 all-gather.2
  360.2 32.5 reduce-scatter.4
  398.7 248.4 all-reduce.4
  712.9 25.7 all-gather.4
  746.1 189.3 all-reduce.6
where the time goes:
time: 947 us; the launch traced here: 946 us
  waiting for transfers between devices  561 us (59%)
  blocking collectives  267 us (28%)
  other arithmetic  61.3 us (6%)
  matrix products  34 us (4%)
  between operations  15.5 us (2%)
    psum x1, blocking collectives, per_device(): back_image = lax.psum(back_part, 'rows').astype(jnp.bfloat16)  267 us
    psum x1, waiting for transfers between devices, per_device(): gram_matrix = lax.psum(gram_local, ('rows', 'cols'))  252 us
    psum x1, waiting for transfers between devices, per_device(): projected = lax.psum(projection_part, 'rows') * inverse_root  189 us
    reduce_scatter x1, waiting for transfers between devices, per_device(): lax.psum_scatter(jnp.dot(row_block, sketch, preferred_element_type=jnp.fl...  36.2 us
    another operation x6, other arithmetic, per_device(): factor = jnp.linalg.cholesky(gram_matrix)  33.9 us
    reduce_scatter x1, waiting for transfers between devices, per_device(): lax.psum_scatter(jnp.dot(row_block, back_image, preferred_element_type=jn...  32.7 us
    all_gather x1, waiting for transfers between devices, per_device(): lax.all_gather(image_low, 'cols', axis=0, tiled=True)  26 us
    all_gather x1, waiting for transfers between devices, per_device(): lax.all_gather(basis, 'cols', axis=0, tiled=True)  25.8 us
  transfers between devices with their start and end apart: 6, of which 6 were waited for; matrix products, arithmetic and copies ran while one was open for 0% of the time, Pallas kernels for 0%

commit v1 on v0

v1 whole, which is shorter than its diff:
```python
import math

import jax
import jax.numpy as jnp
from jax import lax
from jax.experimental import pallas as pl
from jax.experimental.pallas import tpu as pltpu
from jax.sharding import PartitionSpec as P

NZ, NX, NC, NY = 8, 4, 2, 4
PLANE = NZ * NX
F32, BF16 = jnp.float32, jnp.bfloat16
EXACT = lax.Precision.HIGHEST
FIRST = (((0,), (0,)), ((), ()))
LAST = (((1,), (1,)), ((), ()))
PARAMS = pltpu.CompilerParams(vmem_limit_bytes=48 * 2**20)


def row_index(z, x, c):
    return (z * NX + x) * NC + c


Y_SHIFT = {k: [(i, (i + k) % NY) for i in range(NY)] for k in range(1, NY)}
CORE_SWAP = [(i, i ^ 1) for i in range(NZ * NX * NC)]
PLANES = [[row_index(z, x, c) for z in range(NZ) for x in range(NX)] for c in range(NC)]


def from_y(value, k):
    return lax.ppermute(value, "cols", Y_SHIFT[k])


def from_core(value):
    return lax.ppermute(value, "rows", CORE_SWAP)


def exchange(value):
    return lax.all_to_all(value, "rows", 0, 0, tiled=True, axis_index_groups=PLANES)


def forward_kernel(place, a, b, one, two, three, own):
    step = pl.program_id(0)
    part = jnp.dot(a[...], b[...], preferred_element_type=F32)
    store_quarter(step, part, one, two, three, own)


def forward_halves_kernel(place, a, mine, other, one, two, three, own):
    step = pl.program_id(0)
    half = mine.shape[1]
    here = pl.multiple_of(place[1] * half, half)
    there = pl.multiple_of((1 - place[1]) * half, half)
    part = lax.dot_general(a[:, pl.ds(here, half)], mine[...], LAST, preferred_element_type=F32)
    part += lax.dot_general(a[:, pl.ds(there, half)], other[...], LAST, preferred_element_type=F32)
    store_quarter(step, part, one, two, three, own)


def store_quarter(step, part, one, two, three, own):
    for k, out in enumerate((one, two, three)):
        @pl.when(step == k)
        def _(out=out):
            out[...] = part.astype(BF16)

    @pl.when(step == NY - 1)
    def _():
        own[...] = part


def whole(shape):
    return pl.BlockSpec(shape, lambda s, place: (0,) * len(shape))


def forward(place, activations, *right):
    rows, width = activations.shape
    m, rank = rows // NY, 256
    kernel = forward_kernel if len(right) == 1 else forward_halves_kernel
    return pl.pallas_call(
        kernel,
        grid_spec=pltpu.PrefetchScalarGridSpec(
            num_scalar_prefetch=1,
            grid=(NY,),
            in_specs=[pl.BlockSpec((m, width), lambda s, place: (lax.rem(place[0] + s + 1, NY), 0))]
            + [whole(r.shape) for r in right],
            out_specs=[whole((m, rank))] * NY,
        ),
        out_shape=[jax.ShapeDtypeStruct((m, rank), BF16)] * (NY - 1)
        + [jax.ShapeDtypeStruct((m, rank), F32)],
        compiler_params=PARAMS,
        cost_estimate=pl.CostEstimate(
            flops=2 * rows * width * rank, bytes_accessed=rows * width * 2, transcendentals=0
        ),
    )(place, activations, *right)


def back_kernel(place, a, i0, i1, i2, i3, mine, other, total):
    accumulate(place, a, (i0, i1, i2, i3), total, None)
    finish(place, total, mine, other)


def back_gram_kernel(place, a, i0, i1, i2, i3, mine, other, gram, total, square):
    accumulate(place, a, (i0, i1, i2, i3), total, square)
    finish(place, total, mine, other)

    @pl.when(pl.program_id(0) == NY - 1)
    def _():
        width = square.shape[1] // NY
        turned = pltpu.roll(square[...], lax.rem((NY - place[0]) * width, NY * width), 1)
        gram[...] = turned[:, : gram.shape[1]]


def accumulate(place, a, images, total, square):
    step = pl.program_id(0)
    for k, image in enumerate(images):
        @pl.when(step == k)
        def _(k=k, image=image):
            part = lax.dot_general(image[...], a[...], FIRST, preferred_element_type=F32)
            total[...] = part if k == 0 else total[...] + part
            if square is not None:
                part = lax.dot_general(image[...], image[...], FIRST, preferred_element_type=F32)
                square[...] = part if k == 0 else square[...] + part


def finish(place, total, mine, other):
    @pl.when(pl.program_id(0) == NY - 1)
    def _():
        half = mine.shape[1]
        mine[...] = total[:, pl.ds(pl.multiple_of(place[1] * half, half), half)]
        there = pl.multiple_of((1 - place[1]) * half, half)
        other[...] = total[:, pl.ds(there, half)].astype(BF16)


def back(place, activations, images, with_gram):
    rows, width = activations.shape
    m, rank = images[0].shape
    half = width // NC
    out_specs = [whole((rank, half)), whole((rank, half))]
    out_shape = [
        jax.ShapeDtypeStruct((rank, half), F32),
        jax.ShapeDtypeStruct((rank, half), BF16),
    ]
    scratch = [pltpu.VMEM((rank, width), F32)]
    if with_gram:
        out_specs.append(whole((rank, 128)))
        out_shape.append(jax.ShapeDtypeStruct((rank, 128), F32))
        scratch.append(pltpu.VMEM((rank, rank), F32))
    return pl.pallas_call(
        back_gram_kernel if with_gram else back_kernel,
        grid_spec=pltpu.PrefetchScalarGridSpec(
            num_scalar_prefetch=1,
            grid=(NY,),
            in_specs=[pl.BlockSpec((m, width), lambda s, place: (lax.rem(place[0] + s, NY), 0))]
            + [whole((m, rank))] * NY,
            out_specs=out_specs,
            scratch_shapes=scratch,
        ),
        out_shape=out_shape,
        compiler_params=PARAMS,
        cost_estimate=pl.CostEstimate(
            flops=2 * rows * width * rank, bytes_accessed=rows * width * 2, transcendentals=0
        ),
    )(place, activations, *images)


def small_inverse(block, block_at):
    rows = lax.broadcasted_iota(jnp.int32, (8, 128), 0)
    e = list(block)
    for group in range(4):
        c = {}
        for j in range(8):
            lane = block_at + 8 * group + j
            for g in range(group, 4):
                c[j, g] = jnp.broadcast_to(e[g][:, lane : lane + 1], (8, 128))
        for k in range(8):
            root = lax.rsqrt(jnp.broadcast_to(c[k, group][k : k + 1, :], (8, 128)))
            col = {g: c[k, g] * root for g in range(group, 4)}
            row = jnp.broadcast_to(e[group][k : k + 1, :], (8, 128)) * root
            below = jnp.where(rows > k, col[group], 0.0)
            for j in range(k + 1, 8):
                times = jnp.broadcast_to(col[group][j : j + 1, :], (8, 128))
                c[j, group] = c[j, group] - below * times
                for g in range(group + 1, 4):
                    c[j, g] = c[j, g] - col[g] * times
            e[group] = jnp.where(rows == k, row, e[group] - below * row)
            for g in range(group + 1, 4):
                e[g] = e[g] - col[g] * row
    return e


def eliminate(m, n):
    lanes = lax.broadcasted_iota(jnp.int32, (8, 128), 1)
    rows = lax.broadcasted_iota(jnp.int32, (8, 128), 0)
    wide = lax.broadcasted_iota(jnp.int32, (32, 128), 1)
    for k0 in range(0, n, 32):
        tile = 128 * (k0 // 128)
        off = k0 - tile
        at = (off + 32) % 128
        groups = []
        for g in range(4):
            v = pltpu.roll(m[k0 + 8 * g : k0 + 8 * g + 8, tile : tile + 128], 32, 1)
            eye = jnp.where(lanes - off == rows + 8 * g, 1.0, 0.0)
            groups.append(jnp.where((lanes >= at) & (lanes < at + 32), v, eye))
        e = jnp.concatenate(small_inverse(groups, at), axis=0)
        e = jnp.where((wide >= off) & (wide < off + 32), e, 0.0)
        lo, hi = (0, n + 128) if k0 < 128 else (128, 2 * n)
        panel = jnp.dot(e, m[tile : tile + 128, lo:hi], precision=EXACT, preferred_element_type=F32)
        m[k0 : k0 + 32, lo:hi] = panel
        done = k0 + 32
        if done < n:
            first = 0 if done < 128 else 128
            left = panel[:, first - lo : n - lo]
            update = lax.dot_general(left, panel, FIRST, precision=EXACT, preferred_element_type=F32)
            m[done:, lo:hi] = m[done:, lo:hi] - update[done - first :]


def inverse_kernel(scale, high, low, out, m):
    n = out.shape[0]
    m[:, :n] = (high[...].astype(F32) + low[...].astype(F32)) * scale
    r = lax.broadcasted_iota(jnp.int32, (n, n), 0)
    c = lax.broadcasted_iota(jnp.int32, (n, n), 1)
    m[:, n:] = jnp.where(r == c, 1.0, 0.0)
    eliminate(m, n)
    out[...] = m[:, n:]


def factor_inverse(gathered, start, scale):
    n = gathered.shape[0]
    at = start // n
    return pl.pallas_call(
        lambda *refs: inverse_kernel(scale, *refs),
        grid=(1,),
        in_specs=[pl.BlockSpec((n, n), lambda s: (0, at)), pl.BlockSpec((n, n), lambda s: (0, at + 1))],
        out_specs=pl.BlockSpec((n, n), lambda s: (0, 0)),
        out_shape=jax.ShapeDtypeStruct((n, n), F32),
        scratch_shapes=[pltpu.VMEM((n, 2 * n), F32)],
        compiler_params=PARAMS,
        cost_estimate=pl.CostEstimate(flops=2 * 10**10, bytes_accessed=2**20, transcendentals=0),
    )(gathered, gathered)


def last_kernel(inverse_root, place, inverse, power, mine, other, basis, projected):
    basis[...] = lax.dot_general(
        power[...], inverse[...], LAST, precision=EXACT, preferred_element_type=F32
    ).astype(BF16)
    scaled = inverse[...] * inverse_root
    high = scaled.astype(BF16)
    low = (scaled - high.astype(F32)).astype(BF16)
    half = other.shape[1]
    for at, value in ((place[1], mine[...]), (1 - place[1], other[...])):
        projected[:, pl.ds(pl.multiple_of(at * half, half), half)] = jnp.dot(
            high, value, preferred_element_type=F32
        ) + jnp.dot(low, value, preferred_element_type=F32)


def last(place, inverse, power, gathered, other, inverse_root):
    m, rank = power.shape
    half = other.shape[1]
    return pl.pallas_call(
        lambda *refs: last_kernel(inverse_root, *refs),
        grid_spec=pltpu.PrefetchScalarGridSpec(
            num_scalar_prefetch=1,
            grid=(1,),
            in_specs=[whole((rank, rank)), whole((m, rank)), whole((rank, half)), whole((rank, half))],
            out_specs=[whole((m, rank)), whole((rank, NC * half))],
        ),
        out_shape=[
            jax.ShapeDtypeStruct((m, rank), BF16),
            jax.ShapeDtypeStruct((rank, NC * half), F32),
        ],
        compiler_params=PARAMS,
    )(place, inverse, power, gathered, other)


def sum_over_y(one, two, three, own):
    got = [from_y(two, 2), from_y(one, 1), from_y(three, 3)]
    return own + got[0].astype(F32) + got[1].astype(F32) + got[2].astype(F32)


def gather_over_y(mine):
    far, on, behind = from_y(mine, 2), from_y(mine, 3), from_y(mine, 1)
    return mine, on, far, behind


def sum_over_plane(value):
    rows, width = value.shape
    got = exchange(value)
    return jnp.sum(got.reshape(PLANE, rows // PLANE, width).astype(F32), axis=0)


def gather_over_plane(mine):
    return exchange(jnp.tile(mine, (PLANE, 1)))


def split(value):
    high = value.astype(BF16)
    return high, (value - high.astype(F32)).astype(BF16)


def per_device(activations, sketch):
    token_count = activations.shape[0] * lax.axis_size("rows")
    rank = sketch.shape[1]
    quarter = rank // NY
    y = lax.axis_index("cols")
    place = jnp.stack([y, lax.axis_index("rows") % NC]).astype(jnp.int32)

    image = sum_over_y(*forward(place, activations, sketch)).astype(BF16)
    mine, other = back(place, activations, gather_over_y(image), False)
    back_image = sum_over_plane((mine + from_core(other).astype(F32)).astype(BF16))
    back_image = gather_over_plane(back_image.astype(BF16))

    power = sum_over_y(*forward(place, activations, back_image, from_core(back_image)))
    mine, other, gram = back(place, activations, gather_over_y(power.astype(BF16)), True)
    mine = (mine + from_core(other).astype(F32)).astype(BF16)
    gram = gram + from_core(gram)
    slab = sum_over_plane(jnp.concatenate([mine, *split(gram[:, :quarter])], axis=1))
    half = mine.shape[1]
    gram = slab[:, half : half + quarter] + slab[:, half + quarter :]
    lanes = lax.broadcasted_iota(jnp.int32, (slab.shape[0], rank), 1)
    gram = jnp.where(lanes // quarter == y, jnp.tile(gram, (1, NY)), 0.0)
    gram = (gram + from_y(gram, 2)) + (from_y(gram, 1) + from_y(gram, 3))
    gathered = gather_over_plane(
        jnp.concatenate([slab[:, :half].astype(BF16), *split(gram)], axis=1)
    )
    other = from_core(gathered[:, :half])
    inverse = factor_inverse(gathered, half, 1.0 / token_count)
    return last(place, inverse, power, gathered, other, 1.0 / math.sqrt(token_count))


def solution(mesh):
    placed = (P("rows", "cols"), P("cols", None))
    return jax.shard_map(
        per_device,
        mesh=mesh,
        in_specs=placed,
        out_specs=(P(("rows", "cols"), None), P(None, "cols")),
        check_vma=False,
    )
```

time: 947 us -> 223 us (0.24)
  waiting for transfers between devices: 561 us -> 69.2 us
  blocking collectives: 267 us -> 70.9 us
  other arithmetic: 61.3 us -> 0.93 us
  Pallas kernels: 0 us -> 39.8 us
  starting transfers between devices: 0.43 us -> 39 us
  matrix products: 34 us -> 0 us
  between operations: 15.5 us -> 0.8 us
    psum x2 -> x0, waiting for transfers between devices: 440 us -> none  [the longest x1 252 us: per_device(): gram_matrix = lax.psum(gram_local, ('rows', 'cols'))]
    psum x1 -> x0, blocking collectives: 267 us -> none  [per_device(): back_image = lax.psum(back_part, 'rows').astype(jnp.bfloat16)]
    all_to_all x0 -> x3, blocking collectives: none -> 70.9 us  [exchange(): lax.all_to_all(value, 'rows', 0, 0, tiled=True, axis_index_groups=PLANES)]
    reduce_scatter x2 -> x0, waiting for transfers between devices: 68.9 us -> none  [the longest x1 36.2 us: per_device(): lax.psum_scatter(jnp.dot(row_block, sketch, preferred_element_type=jnp.fl...]
    another operation x9 -> x1, other arithmetic: 53.7 us -> 0.08 us  [per_device(): place = jnp.stack([y, lax.axis_index('rows') % NC]).astype(jnp.int32)]
    all_gather x2 -> x0, waiting for transfers between devices: 51.9 us -> none  [the longest x1 26 us: per_device(): lax.all_gather(image_low, 'cols', axis=0, tiled=True)]
    ppermute x0 -> x20, waiting for transfers between devices: none -> 51.6 us  [the longest x15 46.8 us: from_y(): return lax.ppermute(value, 'cols', Y_SHIFT[k])]
    pallas_call x0 -> x6, Pallas kernels: none -> 39.8 us  [the longest x2 12.9 us: back(): pl.pallas_call(back_gram_kernel if with_gram else back_kernel, grid_spec=...]
  transfers between devices with their start and end apart: 6 -> 21, of which waited for: 6 -> 16; matrix products, arithmetic and copies ran while one was open for 0% -> 0% of each run, Pallas kernels for 0% -> 5%
where the time goes in v1:
time: 223 us
  blocking collectives  70.9 us (32%)
  waiting for transfers between devices  69.2 us (31%)
  Pallas kernels  39.8 us (18%)
  starting transfers between devices  39 us (17%)
  local copies, waits for them, and re-layouts  2.44 us (1%)
    all_to_all x3, blocking collectives, exchange(): lax.all_to_all(value, 'rows', 0, 0, tiled=True, axis_index_groups=PLANES)  70.9 us
    ppermute x15, waiting for transfers between devices, from_y(): return lax.ppermute(value, 'cols', Y_SHIFT[k])  46.8 us
    ppermute x15, starting transfers between devices, from_y(): return lax.ppermute(value, 'cols', Y_SHIFT[k])  21.9 us
    all_to_all x1, waiting for transfers between devices, exchange(): lax.all_to_all(value, 'rows', 0, 0, tiled=True, axis_index_groups=PLANES)  17.6 us
    pallas_call x2, Pallas kernels, back(): pl.pallas_call(back_gram_kernel if with_gram else back_kernel, grid_spec=...  12.9 us
    ppermute x5, starting transfers between devices, from_core(): return lax.ppermute(value, 'rows', CORE_SWAP)  12.8 us
    pallas_call x2, Pallas kernels, forward(): pl.pallas_call(kernel, grid_spec=pltpu.PrefetchScalarGridSpec(num_scalar_...  12.5 us
    pallas_call x1, Pallas kernels, factor_inverse(): pl.pallas_call(lambda *refs: inverse_kernel(scale, *refs), grid=(1,), in_...  11.4 us
  transfers between devices with their start and end apart: 21, of which 16 were waited for; matrix products, arithmetic and copies ran while one was open for 0% of the time, Pallas kernels for 5%

profile of v1, /device:TPU:1, one launch (start us, length us, event | category | flops | bytes accessed | tf_op | source)
XLA Modules:
  0.0 223.0 jit_solution(10298602078925788438)
XLA Ops:
  1.9 6.2 %shard_map.41 = (bf16[512,256]{1,0:T(8,128)(2,1)S(1)}, bf16[512,256]{1,0:T(8,128)(2,1)S(1)}, bf16[512,256]{1,0:T(8,128)(2,1)S(1)}, f32[512,256]{1,0:T(8,128)S(1)}) custom-call(s32[2]{0:T(128)S(1)} %pad_add_fusion.place.refs_0_, bf16[2048,2048]{1,0:T(8,128)(2,1)} %a.7, bf16[2048,256]{1,0:T(8,128)(2,1)S(1)} %copy-done), custom_call_target="tpu_custom_call" | custom-call | flops 2147483648 | bytes 8388608 | tf_op jit(solution)/shard_map/pallas_call | solution.py:75
  8.2 3.8 %collective-permute-start = (bf16[512,256]{1,0:T(8,128)(2,1)S(1)}, bf16[512,256]{1,0:T(8,128)(2,1)S(1)}, u32[]{:S(2)}, u32[]{:S(2)}) collective-permute-start(bf16[512,256]{1,0:T(8,128)(2,1)S(1)} %get-tuple-element.16), channel_id=1, source_target_pairs={{0,2},{1,3},{2,0},{3,1},{4,6},{5,7},{6,4},{7,5},{8,10},{9,11},{10,... | collective-permute-start | bytes 786440 | tf_op jit(solution)/shard_map/ppermute | solution.py:29
  12.4 2.3 %collective-permute-start.2 = (bf16[512,256]{1,0:T(8,128)(2,1)S(1)}, bf16[512,256]{1,0:T(8,128)(2,1)S(1)}, u32[]{:S(2)}, u32[]{:S(2)}) collective-permute-start(bf16[512,256]{1,0:T(8,128)(2,1)S(1)} %get-tuple-element.18), channel_id=1, source_target_pairs={{0,3},{1,0},{2,1},{3,2},{4,7},{5,4},{6,5},{7,6},{8,11},{9,8},{10,9... | collective-permute-start | bytes 786440 | tf_op jit(solution)/shard_map/ppermute | solution.py:29
  14.7 2.4 %collective-permute-done = bf16[512,256]{1,0:T(8,128)(2,1)S(1)} collective-permute-done((bf16[512,256]{1,0:T(8,128)(2,1)S(1)}, bf16[512,256]{1,0:T(8,128)(2,1)S(1)}, u32[]{:S(2)}, u32[]{:S(2)}) %collective-permute-start) | collective-permute-done | bytes 262176 | tf_op jit(solution)/shard_map/ppermute | solution.py:29
  17.1 6.6 %collective-permute-done.1 = bf16[512,256]{1,0:T(8,128)(2,1)S(1)} collective-permute-done((bf16[512,256]{1,0:T(8,128)(2,1)S(1)}, bf16[512,256]{1,0:T(8,128)(2,1)S(1)}, u32[]{:S(2)}, u32[]{:S(2)}) %collective-permute-start.1) | collective-permute-done | bytes 262176 | tf_op jit(solution)/shard_map/ppermute | solution.py:29
  23.9 2.0 collective-permute-start.5
  25.9 2.6 %collective-permute-start.4 = (bf16[512,256]{1,0:T(8,128)(2,1)S(1)}, bf16[512,256]{1,0:T(8,128)(2,1)S(1)}, u32[]{:S(2)}, u32[]{:S(2)}) collective-permute-start(bf16[512,256]{1,0:T(8,128)(2,1)S(1)} %add_convert_fusion.2.i0), channel_id=1, source_target_pairs={{0,2},{1,3},{2,0},{3,1},{4,6},{5,7},{6,4},{7,5},{8,10},{9,11},{10,... | collective-permute-start | bytes 786440 | tf_op jit(solution)/shard_map/ppermute | solution.py:29
  28.6 4.4 %collective-permute-done.5.i3 = bf16[512,256]{1,0:T(8,128)(2,1)S(1)} collective-permute-done((bf16[512,256]{1,0:T(8,128)(2,1)S(1)}, bf16[512,256]{1,0:T(8,128)(2,1)S(1)}, u32[]{:S(2)}, u32[]{:S(2)}) %collective-permute-start.5) | collective-permute-done | bytes 262176 | tf_op jit(solution)/shard_map/ppermute | solution.py:29
  32.9 7.2 %collective-permute-done.4.i2 = bf16[512,256]{1,0:T(8,128)(2,1)S(1)} collective-permute-done((bf16[512,256]{1,0:T(8,128)(2,1)S(1)}, bf16[512,256]{1,0:T(8,128)(2,1)S(1)}, u32[]{:S(2)}, u32[]{:S(2)}) %collective-permute-start.4) | collective-permute-done | bytes 262176 | tf_op jit(solution)/shard_map/ppermute | solution.py:29
  40.1 6.3 %shard_map.42 = (f32[256,1024]{1,0:T(8,128)S(1)}, bf16[256,1024]{1,0:T(8,128)(2,1)S(1)}) custom-call(s32[2]{0:T(128)S(1)} %pad_add_fusion.place.refs_0_, bf16[2048,2048]{1,0:T(8,128)(2,1)} %a.7, bf16[512,256]{1,0:T(8,128)(2,1)S(1)} %add_convert_fusion.2.i0, bf16[512,256]{1,0:T(8,128)(2,1)S(1)} %collective-permute-done.3.i1, ...), custom_call_target="tpu_custom_call" | custom-call | flops 2147483648 | bytes 8388608 | tf_op jit(solution)/shard_map/pallas_call | solution.py:144
  47.8 1.5 collective-permute-done.6
  49.5 27.4 %all_to_all.34 = bf16[32,8,1024]{2,1,0:T(8,128)(2,1)S(1)} all-to-all(bf16[32,8,1024]{2,1,0:T(8,128)(2,1)S(1)} %fusion), channel_id=1, replica_groups={{0,8,16,24,32,40,48,56,64,72,80,88,96,104,112,120,128,136,144,152,160,1..., dimensions={0} | all-to-all | bytes 1048576 | tf_op jit(solution)/shard_map/all_to_all | solution.py:37
  77.1 20.1 %all_to_all.35 = bf16[32,8,1024]{2,1,0:T(8,128)(2,1)S(1)} all-to-all(bf16[32,8,1024]{2,1,0:T(8,128)(2,1)S(1)} %tile.8), channel_id=1, replica_groups={{0,8,16,24,32,40,48,56,64,72,80,88,96,104,112,120,128,136,144,152,160,1..., dimensions={0} | all-to-all | bytes 1048576 | tf_op jit(solution)/shard_map/all_to_all | solution.py:37
  97.1 3.6 %collective-permute-start.7 = (bf16[256,1024]{1,0:T(8,128)(2,1)S(1)}, bf16[256,1024]{1,0:T(8,128)(2,1)S(1)}, u32[]{:S(2)}, u32[]{:S(2)}) collective-permute-start(bf16[256,1024]{1,0:T(8,128)(2,1)S(1)} %bitcast.11), channel_id=1, source_target_pairs={{0,4},{4,0},{8,12},{12,8},{16,20},{20,16},{24,28},{28,24},{32,36},... | collective-permute-start | bytes 1572872 | tf_op jit(solution)/shard_map/ppermute | solution.py:33
  100.7 1.5 collective-permute-done.7.other
  102.2 6.3 %shard_map.43 = (bf16[512,256]{1,0:T(8,128)(2,1)S(1)}, bf16[512,256]{1,0:T(8,128)(2,1)S(1)}, bf16[512,256]{1,0:T(8,128)(2,1)S(1)}, f32[512,256]{1,0:T(8,128)S(1)}) custom-call(s32[2]{0:T(128)S(1)} %pad_add_fusion.place.refs_0_, bf16[2048,2048]{1,0:T(8,128)(2,1)} %a.7, bf16[256,1024]{1,0:T(8,128)(2,1)S(1)} %bitcast.12, ...), custom_call_target="tpu_custom_call" | custom-call | flops 2147483648 | bytes 8388608 | tf_op jit(solution)/shard_map/pallas_call | solution.py:75
  112.4 5.3 %collective-permute-done.8 = bf16[512,256]{1,0:T(8,128)(2,1)S(1)} collective-permute-done((bf16[512,256]{1,0:T(8,128)(2,1)S(1)}, bf16[512,256]{1,0:T(8,128)(2,1)S(1)}, u32[]{:S(2)}, u32[]{:S(2)}) %collective-permute-start.8) | collective-permute-done | bytes 262176 | tf_op jit(solution)/shard_map/ppermute | solution.py:29
  117.7 6.3 %collective-permute-done.9 = bf16[512,256]{1,0:T(8,128)(2,1)S(1)} collective-permute-done((bf16[512,256]{1,0:T(8,128)(2,1)S(1)}, bf16[512,256]{1,0:T(8,128)(2,1)S(1)}, u32[]{:S(2)}, u32[]{:S(2)}) %collective-permute-start.9) | collective-permute-done | bytes 262176 | tf_op jit(solution)/shard_map/ppermute | solution.py:29
  124.6 2.6 %collective-permute-start.12 = (bf16[512,256]{1,0:T(8,128)(2,1)S(1)}, bf16[512,256]{1,0:T(8,128)(2,1)S(1)}, u32[]{:S(2)}, u32[]{:S(2)}) collective-permute-start(bf16[512,256]{1,0:T(8,128)(2,1)S(1)} %get-tuple-element.32.i0), channel_id=1, source_target_pairs={{0,2},{1,3},{2,0},{3,1},{4,6},{5,7},{6,4},{7,5},{8,10},{9,11},{10,... | collective-permute-start | bytes 786440 | tf_op jit(solution)/shard_map/ppermute | solution.py:29
  127.3 5.4 %collective-permute-done.13.i3 = bf16[512,256]{1,0:T(8,128)(2,1)S(1)} collective-permute-done((bf16[512,256]{1,0:T(8,128)(2,1)S(1)}, bf16[512,256]{1,0:T(8,128)(2,1)S(1)}, u32[]{:S(2)}, u32[]{:S(2)}) %collective-permute-start.13) | collective-permute-done | bytes 262176 | tf_op jit(solution)/shard_map/ppermute | solution.py:29
  132.8 6.0 %collective-permute-done.12.i2 = bf16[512,256]{1,0:T(8,128)(2,1)S(1)} collective-permute-done((bf16[512,256]{1,0:T(8,128)(2,1)S(1)}, bf16[512,256]{1,0:T(8,128)(2,1)S(1)}, u32[]{:S(2)}, u32[]{:S(2)}) %collective-permute-start.12) | collective-permute-done | bytes 262176 | tf_op jit(solution)/shard_map/ppermute | solution.py:29
  138.8 6.6 %shard_map.44 = (f32[256,1024]{1,0:T(8,128)S(1)}, bf16[256,1024]{1,0:T(8,128)(2,1)S(1)}, f32[256,128]{1,0:T(8,128)S(1)}) custom-call(s32[2]{0:T(128)S(1)} %pad_add_fusion.place.refs_0_, bf16[2048,2048]{1,0:T(8,128)(2,1)} %a.7, bf16[512,256]{1,0:T(8,128)(2,1)S(1)} %get-tuple-element.32.i0, bf16[512,256]{1,0:T(8,128)(2,1)S(1)} %collective-permute-done.11.i1, ...), custom_call_target="tpu_custom_call" | custom-call | flops 2147483648 | bytes 8388608 | tf_op jit(solution)/shard_map/pallas_call | solution.py:144
  145.4 1.6 collective-permute-start.14
  147.2 1.6 collective-permute-done.15
  150.0 4.3 %all-to-all-start.2 = ((bf16[32,8,1152]{2,1,0:T(8,128)(2,1)}), bf16[32,8,1152]{2,1,0:T(8,128)(2,1)S(1)}, u32[]{:S(2)}, u32[]{:S(2)}) async-start(bf16[32,8,1152]{2,1,0:T(8,128)(2,1)} %bitcast.4), calls=%async_computation.2 | async-start | bytes 1179648 | tf_op jit(solution)/shard_map/all_to_all | solution.py:37
  154.3 17.6 %all-to-all-done.2 = bf16[32,8,1152]{2,1,0:T(8,128)(2,1)S(1)} async-done(((bf16[32,8,1152]{2,1,0:T(8,128)(2,1)}), bf16[32,8,1152]{2,1,0:T(8,128)(2,1)S(1)}, u32[]{:S(2)}, u32[]{:S(2)}) %all-to-all-start.2) | async-done | bytes 589856 | tf_op jit(solution)/shard_map/all_to_all | solution.py:37
  172.6 2.2 %collective-permute-start.18 = (f32[8,256]{1,0:T(8,128)S(1)}, f32[8,256]{1,0:T(8,128)S(1)}, u32[]{:S(2)}, u32[]{:S(2)}) collective-permute-start(f32[8,256]{1,0:T(8,128)S(1)} %fusion.2), channel_id=1, source_target_pairs={{0,3},{1,0},{2,1},{3,2},{4,7},{5,4},{6,5},{7,6},{8,11},{9,8},{10,9... | collective-permute-start | bytes 24584 | tf_op jit(solution)/shard_map/ppermute | solution.py:29
  175.9 3.0 %collective-permute-done.16 = f32[8,256]{1,0:T(8,128)S(1)} collective-permute-done((f32[8,256]{1,0:T(8,128)S(1)}, f32[8,256]{1,0:T(8,128)S(1)}, u32[]{:S(2)}, u32[]{:S(2)}) %collective-permute-start.16) | collective-permute-done | bytes 8224 | tf_op jit(solution)/shard_map/ppermute | solution.py:29
  178.9 23.4 %all_to_all.36 = bf16[32,8,1536]{2,1,0:T(8,128)(2,1)S(1)} all-to-all(bf16[32,8,1536]{2,1,0:T(8,128)(2,1)S(1)} %tile.11), channel_id=1, replica_groups={{0,8,16,24,32,40,48,56,64,72,80,88,96,104,112,120,128,136,144,152,160,1..., dimensions={0} | all-to-all | bytes 1572864 | tf_op jit(solution)/shard_map/all_to_all | solution.py:37
  202.4 6.1 %collective-permute-start.19 = (bf16[256,1024]{1,0:T(8,128)(2,1)S(1)}, bf16[256,1024]{1,0:T(8,128)(2,1)S(1)}, u32[]{:S(2)}, u32[]{:S(2)}) collective-permute-start(bf16[256,1024]{1,0:T(8,128)(2,1)S(1)} %slice.26), channel_id=1, source_target_pairs={{0,4},{4,0},{8,12},{12,8},{16,20},{20,16},{24,28},{28,24},{32,36},... | collective-permute-start | bytes 1572872 | tf_op jit(solution)/shard_map/ppermute | solution.py:33
  208.5 11.4 %shard_map.45.refs_1_ = f32[256,256]{1,0:T(8,128)S(1)} custom-call(bf16[256,1536]{1,0:T(8,128)(2,1)S(1)} %bitcast.8, bf16[256,1536]{1,0:T(8,128)(2,1)S(1)} %bitcast.9), custom_call_target="tpu_custom_call" | custom-call | flops 20000000000 | bytes 1048576 | tf_op jit(solution)/shard_map/pallas_call | solution.py:226
  220.0 3.0 %shard_map.46 = (bf16[512,256]{1,0:T(8,128)(2,1)}, f32[256,2048]{1,0:T(8,128)}) custom-call(s32[2]{0:T(128)S(1)} %pad_add_fusion.place.refs_0_, f32[256,256]{1,0:T(8,128)S(1)} %shard_map.45.refs_1_, f32[512,256]{1,0:T(8,128)S(1)} %get-tuple-element.33.refs_2_, bf16[256,1536]{1,0:T(8,128)(2,1)S(1)} %bitcast.10, ...), custom_call_target="tpu_custom_call" | custom-call | tf_op jit(solution)/shard_map/pallas_call | solution.py:255
  (42 shorter events, 11.5 us)
Async XLA Ops:
  0.7 1.2 copy-start
  8.2 8.9 %collective-permute-start = (bf16[512,256]{1,0:T(8,128)(2,1)S(1)}, bf16[512,256]{1,0:T(8,128)(2,1)S(1)}, u32[]{:S(2)}, u32[]{:S(2)}) collective-permute-start(bf16[512,256]{1,0:T(8,128)(2,1)S(1)} %get-tuple-element.16), channel_id=1, source_target_pairs={{0,2},{1,3},{2,0},{3,1},{4,6},{5,7},{6,4},{7,5},{8,10},{9,11},{10,... | collective-permute-start | bytes 786440 | tf_op jit(solution)/shard_map/ppermute | solution.py:29
  12.0 11.7 %collective-permute-start.1 = (bf16[512,256]{1,0:T(8,128)(2,1)S(1)}, bf16[512,256]{1,0:T(8,128)(2,1)S(1)}, u32[]{:S(2)}, u32[]{:S(2)}) collective-permute-start(bf16[512,256]{1,0:T(8,128)(2,1)S(1)} %get-tuple-element.17), channel_id=1, source_target_pairs={{0,1},{1,2},{2,3},{3,0},{4,5},{5,6},{6,7},{7,4},{8,9},{9,10},{10,1... | collective-permute-start | bytes 786440 | tf_op jit(solution)/shard_map/ppermute | solution.py:29
  12.4 11.4 %collective-permute-start.2 = (bf16[512,256]{1,0:T(8,128)(2,1)S(1)}, bf16[512,256]{1,0:T(8,128)(2,1)S(1)}, u32[]{:S(2)}, u32[]{:S(2)}) collective-permute-start(bf16[512,256]{1,0:T(8,128)(2,1)S(1)} %get-tuple-element.18), channel_id=1, source_target_pairs={{0,3},{1,0},{2,1},{3,2},{4,7},{5,4},{6,5},{7,6},{8,11},{9,8},{10,9... | collective-permute-start | bytes 786440 | tf_op jit(solution)/shard_map/ppermute | solution.py:29
  23.9 9.0 %collective-permute-start.5 = (bf16[512,256]{1,0:T(8,128)(2,1)S(1)}, bf16[512,256]{1,0:T(8,128)(2,1)S(1)}, u32[]{:S(2)}, u32[]{:S(2)}) collective-permute-start(bf16[512,256]{1,0:T(8,128)(2,1)S(1)} %add_convert_fusion.2.i0), channel_id=1, source_target_pairs={{0,1},{1,2},{2,3},{3,0},{4,5},{5,6},{6,7},{7,4},{8,9},{9,10},{10,1... | collective-permute-start | bytes 786440 | tf_op jit(solution)/shard_map/ppermute | solution.py:29
  25.9 14.2 %collective-permute-start.4 = (bf16[512,256]{1,0:T(8,128)(2,1)S(1)}, bf16[512,256]{1,0:T(8,128)(2,1)S(1)}, u32[]{:S(2)}, u32[]{:S(2)}) collective-permute-start(bf16[512,256]{1,0:T(8,128)(2,1)S(1)} %add_convert_fusion.2.i0), channel_id=1, source_target_pairs={{0,2},{1,3},{2,0},{3,1},{4,6},{5,7},{6,4},{7,5},{8,10},{9,11},{10,... | collective-permute-start | bytes 786440 | tf_op jit(solution)/shard_map/ppermute | solution.py:29
  28.6 11.5 %collective-permute-start.3 = (bf16[512,256]{1,0:T(8,128)(2,1)S(1)}, bf16[512,256]{1,0:T(8,128)(2,1)S(1)}, u32[]{:S(2)}, u32[]{:S(2)}) collective-permute-start(bf16[512,256]{1,0:T(8,128)(2,1)S(1)} %add_convert_fusion.2.i0), channel_id=1, source_target_pairs={{0,3},{1,0},{2,1},{3,2},{4,7},{5,4},{6,5},{7,6},{8,11},{9,8},{10,9... | collective-permute-start | bytes 786440 | tf_op jit(solution)/shard_map/ppermute | solution.py:29
  46.4 3.0 %collective-permute-start.6 = (bf16[256,1024]{1,0:T(8,128)(2,1)S(1)}, bf16[256,1024]{1,0:T(8,128)(2,1)S(1)}, u32[]{:S(2)}, u32[]{:S(2)}) collective-permute-start(bf16[256,1024]{1,0:T(8,128)(2,1)S(1)} %get-tuple-element.20), channel_id=1, source_target_pairs={{0,4},{4,0},{8,12},{12,8},{16,20},{20,16},{24,28},{28,24},{32,36},... | collective-permute-start | bytes 1572872 | tf_op jit(solution)/shard_map/ppermute | solution.py:33
  97.1 5.1 %collective-permute-start.7 = (bf16[256,1024]{1,0:T(8,128)(2,1)S(1)}, bf16[256,1024]{1,0:T(8,128)(2,1)S(1)}, u32[]{:S(2)}, u32[]{:S(2)}) collective-permute-start(bf16[256,1024]{1,0:T(8,128)(2,1)S(1)} %bitcast.11), channel_id=1, source_target_pairs={{0,4},{4,0},{8,12},{12,8},{16,20},{20,16},{24,28},{28,24},{32,36},... | collective-permute-start | bytes 1572872 | tf_op jit(solution)/shard_map/ppermute | solution.py:33
  108.5 9.1 %collective-permute-start.8 = (bf16[512,256]{1,0:T(8,128)(2,1)S(1)}, bf16[512,256]{1,0:T(8,128)(2,1)S(1)}, u32[]{:S(2)}, u32[]{:S(2)}) collective-permute-start(bf16[512,256]{1,0:T(8,128)(2,1)S(1)} %get-tuple-element.22), channel_id=1, source_target_pairs={{0,2},{1,3},{2,0},{3,1},{4,6},{5,7},{6,4},{7,5},{8,10},{9,11},{10,... | collective-permute-start | bytes 786440 | tf_op jit(solution)/shard_map/ppermute | solution.py:29
  109.7 14.2 %collective-permute-start.9 = (bf16[512,256]{1,0:T(8,128)(2,1)S(1)}, bf16[512,256]{1,0:T(8,128)(2,1)S(1)}, u32[]{:S(2)}, u32[]{:S(2)}) collective-permute-start(bf16[512,256]{1,0:T(8,128)(2,1)S(1)} %get-tuple-element.23), channel_id=1, source_target_pairs={{0,1},{1,2},{2,3},{3,0},{4,5},{5,6},{6,7},{7,4},{8,9},{9,10},{10,1... | collective-permute-start | bytes 786440 | tf_op jit(solution)/shard_map/ppermute | solution.py:29
  111.1 12.9 %collective-permute-start.10 = (bf16[512,256]{1,0:T(8,128)(2,1)S(1)}, bf16[512,256]{1,0:T(8,128)(2,1)S(1)}, u32[]{:S(2)}, u32[]{:S(2)}) collective-permute-start(bf16[512,256]{1,0:T(8,128)(2,1)S(1)} %get-tuple-element.24), channel_id=1, source_target_pairs={{0,3},{1,0},{2,1},{3,2},{4,7},{5,4},{6,5},{7,6},{8,11},{9,8},{10,9... | collective-permute-start | bytes 786440 | tf_op jit(solution)/shard_map/ppermute | solution.py:29
  124.1 8.7 %collective-permute-start.13 = (bf16[512,256]{1,0:T(8,128)(2,1)S(1)}, bf16[512,256]{1,0:T(8,128)(2,1)S(1)}, u32[]{:S(2)}, u32[]{:S(2)}) collective-permute-start(bf16[512,256]{1,0:T(8,128)(2,1)S(1)} %get-tuple-element.32.i0), channel_id=1, source_target_pairs={{0,1},{1,2},{2,3},{3,0},{4,5},{5,6},{6,7},{7,4},{8,9},{9,10},{10,1... | collective-permute-start | bytes 786440 | tf_op jit(solution)/shard_map/ppermute | solution.py:29
  124.6 14.2 %collective-permute-start.12 = (bf16[512,256]{1,0:T(8,128)(2,1)S(1)}, bf16[512,256]{1,0:T(8,128)(2,1)S(1)}, u32[]{:S(2)}, u32[]{:S(2)}) collective-permute-start(bf16[512,256]{1,0:T(8,128)(2,1)S(1)} %get-tuple-element.32.i0), channel_id=1, source_target_pairs={{0,2},{1,3},{2,0},{3,1},{4,6},{5,7},{6,4},{7,5},{8,10},{9,11},{10,... | collective-permute-start | bytes 786440 | tf_op jit(solution)/shard_map/ppermute | solution.py:29
  127.2 11.5 %collective-permute-start.11 = (bf16[512,256]{1,0:T(8,128)(2,1)S(1)}, bf16[512,256]{1,0:T(8,128)(2,1)S(1)}, u32[]{:S(2)}, u32[]{:S(2)}) collective-permute-start(bf16[512,256]{1,0:T(8,128)(2,1)S(1)} %get-tuple-element.32.i0), channel_id=1, source_target_pairs={{0,3},{1,0},{2,1},{3,2},{4,7},{5,4},{6,5},{7,6},{8,11},{9,8},{10,9... | collective-permute-start | bytes 786440 | tf_op jit(solution)/shard_map/ppermute | solution.py:29
  145.4 3.4 %collective-permute-start.14 = (bf16[256,1024]{1,0:T(8,128)(2,1)S(1)}, bf16[256,1024]{1,0:T(8,128)(2,1)S(1)}, u32[]{:S(2)}, u32[]{:S(2)}) collective-permute-start(bf16[256,1024]{1,0:T(8,128)(2,1)S(1)} %get-tuple-element.26), channel_id=1, source_target_pairs={{0,4},{4,0},{8,12},{12,8},{16,20},{20,16},{24,28},{28,24},{32,36},... | collective-permute-start | bytes 1572872 | tf_op jit(solution)/shard_map/ppermute | solution.py:33
  147.1 1.7 collective-permute-start.15
  150.0 21.9 %all-to-all-start.2 = ((bf16[32,8,1152]{2,1,0:T(8,128)(2,1)}), bf16[32,8,1152]{2,1,0:T(8,128)(2,1)S(1)}, u32[]{:S(2)}, u32[]{:S(2)}) async-start(bf16[32,8,1152]{2,1,0:T(8,128)(2,1)} %bitcast.4), calls=%async_computation.2 | async-start | bytes 1179648 | tf_op jit(solution)/shard_map/all_to_all | solution.py:37
  172.1 3.8 %collective-permute-start.17 = (f32[8,256]{1,0:T(8,128)S(1)}, f32[8,256]{1,0:T(8,128)S(1)}, u32[]{:S(2)}, u32[]{:S(2)}) collective-permute-start(f32[8,256]{1,0:T(8,128)S(1)} %fusion.2), channel_id=1, source_target_pairs={{0,1},{1,2},{2,3},{3,0},{4,5},{5,6},{6,7},{7,4},{8,9},{9,10},{10,1... | collective-permute-start | bytes 24584 | tf_op jit(solution)/shard_map/ppermute | solution.py:29
  172.6 3.3 %collective-permute-start.18 = (f32[8,256]{1,0:T(8,128)S(1)}, f32[8,256]{1,0:T(8,128)S(1)}, u32[]{:S(2)}, u32[]{:S(2)}) collective-permute-start(f32[8,256]{1,0:T(8,128)S(1)} %fusion.2), channel_id=1, source_target_pairs={{0,3},{1,0},{2,1},{3,2},{4,7},{5,4},{6,5},{7,6},{8,11},{9,8},{10,9... | collective-permute-start | bytes 24584 | tf_op jit(solution)/shard_map/ppermute | solution.py:29
  174.9 4.0 %collective-permute-start.16 = (f32[8,256]{1,0:T(8,128)S(1)}, f32[8,256]{1,0:T(8,128)S(1)}, u32[]{:S(2)}, u32[]{:S(2)}) collective-permute-start(f32[8,256]{1,0:T(8,128)S(1)} %fusion.2), channel_id=1, source_target_pairs={{0,2},{1,3},{2,0},{3,1},{4,6},{5,7},{6,4},{7,5},{8,10},{9,11},{10,... | collective-permute-start | bytes 24584 | tf_op jit(solution)/shard_map/ppermute | solution.py:29
  202.4 17.6 %collective-permute-start.19 = (bf16[256,1024]{1,0:T(8,128)(2,1)S(1)}, bf16[256,1024]{1,0:T(8,128)(2,1)S(1)}, u32[]{:S(2)}, u32[]{:S(2)}) collective-permute-start(bf16[256,1024]{1,0:T(8,128)(2,1)S(1)} %slice.26), channel_id=1, source_target_pairs={{0,4},{4,0},{8,12},{12,8},{16,20},{20,16},{24,28},{28,24},{32,36},... | collective-permute-start | bytes 1572872 | tf_op jit(solution)/shard_map/ppermute | solution.py:33

commit v2 on v1

v2 whole, which is shorter than its diff:
```python
import functools
import math

import jax
import jax.numpy as jnp
from jax import lax
from jax.experimental import pallas as pl
from jax.experimental.pallas import tpu as pltpu
from jax.sharding import PartitionSpec as P

NZ, NX, NC, NY = 8, 4, 2, 4
PLANE = NZ * NX
F32, BF16 = jnp.float32, jnp.bfloat16
EXACT = lax.Precision.HIGHEST
FIRST = (((0,), (0,)), ((), ()))
LAST = (((1,), (1,)), ((), ()))
PRODUCT = pltpu.CompilerParams(vmem_limit_bytes=16 * 2**20)


def row_index(z, x, c):
    return (z * NX + x) * NC + c


Y_SHIFT = {k: [(i, (i + k) % NY) for i in range(NY)] for k in range(1, NY)}
CORE_SWAP = [(i, i ^ 1) for i in range(NZ * NX * NC)]
PLANES = [[row_index(z, x, c) for z in range(NZ) for x in range(NX)] for c in range(NC)]


def from_y(value, k):
    return lax.ppermute(value, "cols", Y_SHIFT[k])


def from_core(value):
    return lax.ppermute(value, "rows", CORE_SWAP)


def exchange(value):
    return lax.all_to_all(value, "rows", 0, 0, tiled=True, axis_index_groups=PLANES)


VMEM = pl.BlockSpec(memory_space=pltpu.VMEM)
SMEM = pl.BlockSpec(memory_space=pltpu.SMEM)
HBM = pl.BlockSpec(memory_space=pltpu.HBM)


def resident(value):
    return pltpu.with_memory_space_constraint(value, pltpu.VMEM)


def in_hbm(value):
    return pltpu.with_memory_space_constraint(value, pltpu.HBM)


def products(steps, rows, width, rank):
    return pl.CostEstimate(
        flops=2 * steps * rows * width * rank, bytes_accessed=steps * rows * width * 2, transcendentals=0
    )


def load_kernel(quarters, keep_right, place, a, right, *refs):
    count = len(quarters)
    outs, kept, refs = refs[:count], refs[count : 2 * count], refs[2 * count :]
    sems = refs[-1]
    m = outs[0].shape[0]
    copies = []
    if keep_right:
        copies.append(pltpu.make_async_copy(right, refs[0], sems.at[count]))
        right = refs[0]
    for i, k in enumerate(quarters):
        rows = pl.ds(pl.multiple_of(lax.rem(place[0] + k, NY) * m, m), m)
        copies.append(pltpu.make_async_copy(a.at[rows, :], kept[i], sems.at[i]))
    for copy in copies:
        copy.start()
    if keep_right:
        copies.pop(0).wait()
    for i, out in enumerate(outs):
        @pl.when(place[0] >= 0)
        def _(i=i, out=out):
            copies[i].wait()
            part = jnp.dot(kept[i][...], right[...], preferred_element_type=F32)
            out[...] = part.astype(out.dtype)


def load_part(place, activations, right, quarters, types, keep_right):
    rows, width = activations.shape
    count, m, rank = len(quarters), rows // NY, right.shape[1]
    return pl.pallas_call(
        functools.partial(load_kernel, quarters, keep_right),
        in_specs=[SMEM, HBM, HBM if keep_right else VMEM],
        out_specs=[VMEM] * (2 * count + keep_right),
        out_shape=[jax.ShapeDtypeStruct((m, rank), t) for t in types]
        + [pltpu.VMEM((m, width), BF16)] * count
        + [pltpu.VMEM(right.shape, BF16)] * keep_right,
        scratch_shapes=[pltpu.SemaphoreType.DMA((count + keep_right,))],
        compiler_params=PRODUCT,
        cost_estimate=products(count, m, width, rank),
    )(place, in_hbm(activations), (in_hbm if keep_right else resident)(right))


def load_forward(place, activations, right):
    two, one, a2, a1, right = load_part(place, activations, right, (2, 1), (BF16, BF16), True)
    three, own, a3, a0 = load_part(place, activations, right, (3, 0), (BF16, F32), False)
    return (one, two, three, own), (a0, a1, a2, a3)


def forward_kernel(place, mine, other, *refs):
    count = len(refs) // 2
    half = mine.shape[1]
    here = pl.ds(pl.multiple_of(place[1] * half, half), half)
    there = pl.ds(pl.multiple_of((1 - place[1]) * half, half), half)
    for kept, out in zip(refs[:count], refs[count:]):
        part = lax.dot_general(kept[:, here], mine[...], LAST, preferred_element_type=F32)
        part += lax.dot_general(kept[:, there], other[...], LAST, preferred_element_type=F32)
        out[...] = part.astype(out.dtype)


def forward_part(place, kept, mine, other, types):
    m, width = kept[0].shape
    rank = mine.shape[0]
    return pl.pallas_call(
        forward_kernel,
        in_specs=[SMEM] + [VMEM] * (2 + len(kept)),
        out_specs=[VMEM] * len(types),
        out_shape=[jax.ShapeDtypeStruct((m, rank), t) for t in types],
        compiler_params=PRODUCT,
        cost_estimate=products(len(kept), m, width, rank),
    )(place, mine, other, *map(resident, kept))


def forward(place, kept, mine, other):
    two, one = forward_part(place, (kept[2], kept[1]), mine, other, (BF16, BF16))
    three, own = forward_part(place, (kept[3], kept[0]), mine, other, (BF16, F32))
    return one, two, three, own


def back_kernel(count, first, final, with_gram, place, *refs):
    sums = 2 if with_gram else 1
    kept, images, refs = refs[:count], refs[count : 2 * count], refs[2 * count :]
    before = None
    if not first:
        before, refs = refs[:sums], refs[sums:]
    totals = refs[len(refs) - sums :]
    for i, image in enumerate(images):
        value = image[...]
        parts = [lax.dot_general(value, kept[i][...], FIRST, preferred_element_type=F32)]
        if with_gram:
            parts.append(lax.dot_general(value, value, FIRST, preferred_element_type=F32))
        for j, part in enumerate(parts):
            if i > 0:
                part += totals[j][...]
            elif not first:
                part += before[j][...]
            totals[j][...] = part
    if final:
        for j in range(sums):
            total, mine, other = totals[j], refs[2 * j], refs[2 * j + 1]
            half = mine.shape[1]
            mine[...] = total[:, pl.ds(pl.multiple_of(place[1] * half, half), half)]
            there = pl.ds(pl.multiple_of((1 - place[1]) * half, half), half)
            other[...] = total[:, there].astype(other.dtype)


def back_part(place, kept, images, before, final, with_gram):
    m, width = kept[0].shape
    rank = images[0].shape[1]
    sums = [(rank, width)] + ([(rank, rank)] if with_gram else [])
    if final:
        shapes = [
            jax.ShapeDtypeStruct((rank, w // NC), t)
            for (_, w), types in zip(sums, ((F32, BF16), (F32, F32)))
            for t in types
        ]
    else:
        shapes = [pltpu.VMEM(shape, F32) for shape in sums]
    return pl.pallas_call(
        functools.partial(back_kernel, len(images), not before, final, with_gram),
        in_specs=[SMEM] + [VMEM] * (2 * len(images) + len(before)),
        out_specs=[VMEM] * len(shapes),
        out_shape=shapes,
        scratch_shapes=[pltpu.VMEM(shape, F32) for shape in sums] if final else [],
        compiler_params=PRODUCT,
        cost_estimate=products(len(images), m, width, rank),
    )(place, *map(resident, kept), *images, *map(resident, before))


def back(place, kept, images, with_gram):
    own, on, far, behind = images
    total = back_part(place, kept[:1], (own,), (), False, with_gram)
    total = back_part(place, (kept[1], kept[3]), (on, behind), total, False, with_gram)
    return back_part(place, kept[2:3], (far,), total, True, with_gram)


def small_inverse(block, block_at):
    rows = lax.broadcasted_iota(jnp.int32, (8, 128), 0)
    e = list(block)
    for group in range(4):
        c = {}
        for j in range(8):
            lane = block_at + 8 * group + j
            for g in range(group, 4):
                c[j, g] = jnp.broadcast_to(e[g][:, lane : lane + 1], (8, 128))
        for k in range(8):
            root = lax.rsqrt(jnp.broadcast_to(c[k, group][k : k + 1, :], (8, 128)))
            col = {g: c[k, g] * root for g in range(group, 4)}
            row = jnp.broadcast_to(e[group][k : k + 1, :], (8, 128)) * root
            below = jnp.where(rows > k, col[group], 0.0)
            for j in range(k + 1, 8):
                times = jnp.broadcast_to(col[group][j : j + 1, :], (8, 128))
                c[j, group] = c[j, group] - below * times
                for g in range(group + 1, 4):
                    c[j, g] = c[j, g] - col[g] * times
            e[group] = jnp.where(rows == k, row, e[group] - below * row)
            for g in range(group + 1, 4):
                e[g] = e[g] - col[g] * row
    return e


def eliminate(m, n):
    lanes = lax.broadcasted_iota(jnp.int32, (8, 128), 1)
    rows = lax.broadcasted_iota(jnp.int32, (8, 128), 0)
    wide = lax.broadcasted_iota(jnp.int32, (32, 128), 1)
    for k0 in range(0, n, 32):
        tile = 128 * (k0 // 128)
        off = k0 - tile
        at = (off + 32) % 128
        groups = []
        for g in range(4):
            v = pltpu.roll(m[k0 + 8 * g : k0 + 8 * g + 8, tile : tile + 128], 32, 1)
            eye = jnp.where(lanes - off == rows + 8 * g, 1.0, 0.0)
            groups.append(jnp.where((lanes >= at) & (lanes < at + 32), v, eye))
        e = jnp.concatenate(small_inverse(groups, at), axis=0)
        e = jnp.where((wide >= off) & (wide < off + 32), e, 0.0)
        lo, hi = (0, n + 128) if k0 < 128 else (128, 2 * n)
        panel = jnp.dot(e, m[tile : tile + 128, lo:hi], precision=EXACT, preferred_element_type=F32)
        m[k0 : k0 + 32, lo:hi] = panel
        done = k0 + 32
        if done < n:
            first = 0 if done < 128 else 128
            left = panel[:, first - lo : n - lo]
            update = lax.dot_general(left, panel, FIRST, precision=EXACT, preferred_element_type=F32)
            m[done:, lo:hi] = m[done:, lo:hi] - update[done - first :]


def inverse_kernel(scale, start, place, gathered, swapped, out, m):
    n = out.shape[0]
    half = n // NC
    for at, source, first in ((place[1], gathered, start), (1 - place[1], swapped, 0)):
        high = source[:, first : first + half].astype(F32)
        low = source[:, first + half : first + n].astype(F32)
        m[:, pl.ds(pl.multiple_of(at * half, half), half)] = (high + low) * scale
    r = lax.broadcasted_iota(jnp.int32, (n, n), 0)
    c = lax.broadcasted_iota(jnp.int32, (n, n), 1)
    m[:, n:] = jnp.where(r == c, 1.0, 0.0)
    eliminate(m, n)
    out[...] = m[:, n:]


def factor_inverse(place, gathered, start, swapped, scale):
    n = gathered.shape[0]
    return pl.pallas_call(
        functools.partial(inverse_kernel, scale, start),
        in_specs=[SMEM, VMEM, VMEM],
        out_specs=VMEM,
        out_shape=jax.ShapeDtypeStruct((n, n), F32),
        scratch_shapes=[pltpu.VMEM((n, 2 * n), F32)],
        compiler_params=PRODUCT,
        cost_estimate=pl.CostEstimate(flops=10**10, bytes_accessed=2**20, transcendentals=0),
    )(place, gathered, swapped)


def last_kernel(inverse_root, place, inverse, power, gathered, other, basis, projected):
    basis[...] = lax.dot_general(
        power[...], inverse[...], LAST, precision=EXACT, preferred_element_type=F32
    ).astype(BF16)
    scaled = inverse[...] * inverse_root
    high = scaled.astype(BF16)
    low = (scaled - high.astype(F32)).astype(BF16)
    half = other.shape[1]
    for at, source in ((place[1], gathered), (1 - place[1], other)):
        value = source[:, :half]
        projected[:, pl.ds(pl.multiple_of(at * half, half), half)] = jnp.dot(
            high, value, preferred_element_type=F32
        ) + jnp.dot(low, value, preferred_element_type=F32)


def last(place, inverse, power, gathered, other, inverse_root):
    m, rank = power.shape
    return pl.pallas_call(
        functools.partial(last_kernel, inverse_root),
        in_specs=[SMEM] + [VMEM] * 4,
        out_specs=[VMEM] * 2,
        out_shape=[
            jax.ShapeDtypeStruct((m, rank), BF16),
            jax.ShapeDtypeStruct((rank, NC * other.shape[1]), F32),
        ],
        compiler_params=PRODUCT,
    )(place, inverse, power, gathered, other)


def sum_over_y(one, two, three, own):
    got = [from_y(two, 2), from_y(one, 1), from_y(three, 3)]
    return own + got[0].astype(F32) + got[1].astype(F32) + got[2].astype(F32)


def gather_over_y(mine):
    far, on, behind = from_y(mine, 2), from_y(mine, 3), from_y(mine, 1)
    return mine, on, far, behind


def sum_over_plane(value):
    rows, width = value.shape
    got = exchange(value)
    return jnp.sum(got.reshape(PLANE, rows // PLANE, width).astype(F32), axis=0)


def gather_over_plane(mine):
    return exchange(jnp.tile(mine, (PLANE, 1)))


def split(value):
    high = value.astype(BF16)
    return high, (value - high.astype(F32)).astype(BF16)


def per_device(activations, sketch):
    token_count = activations.shape[0] * lax.axis_size("rows")
    place = jnp.stack([lax.axis_index("cols"), lax.axis_index("rows") % NC]).astype(jnp.int32)

    pieces, kept = load_forward(place, activations, sketch)
    image = sum_over_y(*pieces).astype(BF16)
    mine, other = back(place, kept, gather_over_y(image), False)
    back_image = sum_over_plane((mine + from_core(other).astype(F32)).astype(BF16))
    back_image = gather_over_plane(back_image.astype(BF16))

    power = sum_over_y(*forward(place, kept, back_image, from_core(back_image)))
    mine, other, gram, gram_other = back(place, kept, gather_over_y(power.astype(BF16)), True)
    gram = gram + from_core(gram_other)
    mine = (mine + from_core(other).astype(F32)).astype(BF16)
    slab = sum_over_plane(jnp.concatenate([mine, *split(gram)], axis=1))
    half, columns = mine.shape[1], gram.shape[1]
    gram = slab[:, half : half + columns] + slab[:, half + columns :]
    gathered = gather_over_plane(
        jnp.concatenate([slab[:, :half].astype(BF16), *split(gram)], axis=1)
    )
    swapped = from_core(gathered[:, half:])
    inverse = factor_inverse(place, gathered, half, swapped, 1.0 / token_count)
    other = from_core(gathered[:, :half])
    return last(place, inverse, power, gathered, other, 1.0 / math.sqrt(token_count))


def solution(mesh):
    placed = (P("rows", "cols"), P("cols", None))
    return jax.shard_map(
        per_device,
        mesh=mesh,
        in_specs=placed,
        out_specs=(P(("rows", "cols"), None), P(None, "cols")),
        check_vma=False,
    )
```

time: 223 us -> 200 us (0.90)
  waiting for transfers between devices: 69.2 us -> 35.3 us
  blocking collectives: 70.9 us -> 93 us
  starting transfers between devices: 39 us -> 32.7 us
  Pallas kernels: 39.8 us -> 35.6 us
    all_to_all x3 -> x4, blocking collectives: 70.9 us -> 93 us  [exchange(): lax.all_to_all(value, 'rows', 0, 0, tiled=True, axis_index_groups=PLANES)]
    all_to_all x1 -> x0, waiting for transfers between devices: 17.6 us -> none  [exchange(): lax.all_to_all(value, 'rows', 0, 0, tiled=True, axis_index_groups=PLANES)]
    ppermute x15 -> x12, waiting for transfers between devices: 46.8 us -> 30 us  [from_y(): return lax.ppermute(value, 'cols', Y_SHIFT[k])]
    all_to_all x1 -> x0, starting transfers between devices: 4.27 us -> none  [exchange(): lax.all_to_all(value, 'rows', 0, 0, tiled=True, axis_index_groups=PLANES)]
    pallas_call x6 -> x12, Pallas kernels: 39.8 us -> 35.6 us  [the longest x1 12.1 us: factor_inverse(): pl.pallas_call(functools.partial(inverse_kernel, scale, start), in_specs=...]
    ppermute x15 -> x12, starting transfers between devices: 21.9 us -> 19.9 us  [from_y(): return lax.ppermute(value, 'cols', Y_SHIFT[k])]
    ppermute x5 -> x6, waiting for transfers between devices: 4.8 us -> 5.31 us  [from_core(): return lax.ppermute(value, 'rows', CORE_SWAP)]
    ppermute x5 -> x6, starting transfers between devices: 12.8 us -> 12.8 us  [from_core(): return lax.ppermute(value, 'rows', CORE_SWAP)]
  transfers between devices with their start and end apart: 21 -> 18, of which waited for: 16 -> 12; matrix products, arithmetic and copies ran while one was open for 0% -> 0% of each run, Pallas kernels for 5% -> 12%
where the time goes in v2:
time: 200 us
  blocking collectives  93 us (46%)
  Pallas kernels  35.6 us (18%)
  waiting for transfers between devices  35.3 us (18%)
  starting transfers between devices  32.7 us (16%)
    all_to_all x4, blocking collectives, exchange(): lax.all_to_all(value, 'rows', 0, 0, tiled=True, axis_index_groups=PLANES)  93 us
    ppermute x12, waiting for transfers between devices, from_y(): return lax.ppermute(value, 'cols', Y_SHIFT[k])  30 us
    ppermute x12, starting transfers between devices, from_y(): return lax.ppermute(value, 'cols', Y_SHIFT[k])  19.9 us
    ppermute x6, starting transfers between devices, from_core(): return lax.ppermute(value, 'rows', CORE_SWAP)  12.8 us
    pallas_call x1, Pallas kernels, factor_inverse(): pl.pallas_call(functools.partial(inverse_kernel, scale, start), in_specs=...  12.1 us
    pallas_call x6, Pallas kernels, back_part(): pl.pallas_call(functools.partial(back_kernel, len(images), not before, fi...  9.29 us
    pallas_call x2, Pallas kernels, load_part(): pl.pallas_call(functools.partial(load_kernel, quarters, keep_right), in_s...  7.51 us
    ppermute x6, waiting for transfers between devices, from_core(): return lax.ppermute(value, 'rows', CORE_SWAP)  5.31 us
  transfers between devices with their start and end apart: 18, of which 12 were waited for; matrix products, arithmetic and copies ran while one was open for 0% of the time, Pallas kernels for 12%

profile of v2, /device:TPU:1, one launch (start us, length us, event | category | flops | bytes accessed | tf_op | source)
XLA Modules:
  0.0 200.1 jit_solution(5957753661680498699)
XLA Ops:
  0.7 3.9 %shard_map.41 = (bf16[512,256]{1,0:T(8,128)(2,1)S(1)}, bf16[512,256]{1,0:T(8,128)(2,1)S(1)}, bf16[512,2048]{1,0:T(8,128)(2,1)S(1)}, bf16[512,2048]{1,0:T(8,128)(2,1)S(1)}, bf16[2048,256]{1,0:T(8,128)(2,1)S(1)}) custom-call(s32[2]{0:T(128)S(1)} %pad_add_fusion.place, bf16[2048,2048]{1,0:T(8,128)(2,1)} %a.3, bf16[2048,256]{1,0:T(8,128)(2,1)} %right.1), custom_call_target="tpu_custom_call" | custom-call | flops 1073741824 | bytes 4194304 | tf_op jit(solution)/shard_map/pallas_call | solution.py:87
  4.7 3.8 %collective-permute-start = (bf16[512,256]{1,0:T(8,128)(2,1)S(1)}, bf16[512,256]{1,0:T(8,128)(2,1)S(1)}, u32[]{:S(2)}, u32[]{:S(2)}) collective-permute-start(bf16[512,256]{1,0:T(8,128)(2,1)S(1)} %get-tuple-element.28), channel_id=1, source_target_pairs={{0,2},{1,3},{2,0},{3,1},{4,6},{5,7},{6,4},{7,5},{8,10},{9,11},{10,... | collective-permute-start | bytes 786440 | tf_op jit(solution)/shard_map/ppermute | solution.py:30
  8.9 3.6 %shard_map.42 = (bf16[512,256]{1,0:T(8,128)(2,1)S(1)}, f32[512,256]{1,0:T(8,128)S(1)}, bf16[512,2048]{1,0:T(8,128)(2,1)S(1)}, bf16[512,2048]{1,0:T(8,128)(2,1)S(1)}) custom-call(s32[2]{0:T(128)S(1)} %pad_add_fusion.place, bf16[2048,2048]{1,0:T(8,128)(2,1)} %a.3, bf16[2048,256]{1,0:T(8,128)(2,1)S(1)} %get-tuple-element.26.right), custom_call_target="tpu_custom_call" | custom-call | flops 1073741824 | bytes 4194304 | tf_op jit(solution)/shard_map/pallas_call | solution.py:87
  12.5 2.4 %collective-permute-start.2 = (bf16[512,256]{1,0:T(8,128)(2,1)S(1)}, bf16[512,256]{1,0:T(8,128)(2,1)S(1)}, u32[]{:S(2)}, u32[]{:S(2)}) collective-permute-start(bf16[512,256]{1,0:T(8,128)(2,1)S(1)} %get-tuple-element.30), channel_id=1, source_target_pairs={{0,3},{1,0},{2,1},{3,2},{4,7},{5,4},{6,5},{7,6},{8,11},{9,8},{10,9... | collective-permute-start | bytes 786440 | tf_op jit(solution)/shard_map/ppermute | solution.py:30
  14.9 5.3 %collective-permute-done.1 = bf16[512,256]{1,0:T(8,128)(2,1)S(1)} collective-permute-done((bf16[512,256]{1,0:T(8,128)(2,1)S(1)}, bf16[512,256]{1,0:T(8,128)(2,1)S(1)}, u32[]{:S(2)}, u32[]{:S(2)}) %collective-permute-start.1) | collective-permute-done | bytes 262176 | tf_op jit(solution)/shard_map/ppermute | solution.py:30
  25.3 2.5 %collective-permute-done.5.refs_3_ = bf16[512,256]{1,0:T(8,128)(2,1)S(1)} collective-permute-done((bf16[512,256]{1,0:T(8,128)(2,1)S(1)}, bf16[512,256]{1,0:T(8,128)(2,1)S(1)}, u32[]{:S(2)}, u32[]{:S(2)}) %collective-permute-start.5) | collective-permute-done | bytes 262176 | tf_op jit(solution)/shard_map/ppermute | solution.py:30
  27.8 1.8 shard_map.44.refs_2_
  29.6 4.2 %collective-permute-done.3.refs_1_ = bf16[512,256]{1,0:T(8,128)(2,1)S(1)} collective-permute-done((bf16[512,256]{1,0:T(8,128)(2,1)S(1)}, bf16[512,256]{1,0:T(8,128)(2,1)S(1)}, u32[]{:S(2)}, u32[]{:S(2)}) %collective-permute-start.3) | collective-permute-done | bytes 262176 | tf_op jit(solution)/shard_map/ppermute | solution.py:30
  35.2 3.4 %collective-permute-start.6 = (bf16[256,1024]{1,0:T(8,128)(2,1)S(1)}, bf16[256,1024]{1,0:T(8,128)(2,1)S(1)}, u32[]{:S(2)}, u32[]{:S(2)}) collective-permute-start(bf16[256,1024]{1,0:T(8,128)(2,1)S(1)} %get-tuple-element.35), channel_id=1, source_target_pairs={{0,4},{4,0},{8,12},{12,8},{16,20},{20,16},{24,28},{28,24},{32,36},... | collective-permute-start | bytes 1572872 | tf_op jit(solution)/shard_map/ppermute | solution.py:34
  38.6 1.5 collective-permute-done.6
  40.3 27.2 %all_to_all.34 = bf16[32,8,1024]{2,1,0:T(8,128)(2,1)S(1)} all-to-all(bf16[32,8,1024]{2,1,0:T(8,128)(2,1)S(1)} %fusion), channel_id=1, replica_groups={{0,8,16,24,32,40,48,56,64,72,80,88,96,104,112,120,128,136,144,152,160,1..., dimensions={0} | all-to-all | bytes 1048576 | tf_op jit(solution)/shard_map/all_to_all | solution.py:38
  67.6 20.1 %all_to_all.35 = bf16[32,8,1024]{2,1,0:T(8,128)(2,1)S(1)} all-to-all(bf16[32,8,1024]{2,1,0:T(8,128)(2,1)S(1)} %tile.4), channel_id=1, replica_groups={{0,8,16,24,32,40,48,56,64,72,80,88,96,104,112,120,128,136,144,152,160,1..., dimensions={0} | all-to-all | bytes 1048576 | tf_op jit(solution)/shard_map/all_to_all | solution.py:38
  87.7 3.6 %collective-permute-start.7 = (bf16[256,1024]{1,0:T(8,128)(2,1)S(1)}, bf16[256,1024]{1,0:T(8,128)(2,1)S(1)}, u32[]{:S(2)}, u32[]{:S(2)}) collective-permute-start(bf16[256,1024]{1,0:T(8,128)(2,1)S(1)} %bitcast.12), channel_id=1, source_target_pairs={{0,4},{4,0},{8,12},{12,8},{16,20},{20,16},{24,28},{28,24},{32,36},... | collective-permute-start | bytes 1572872 | tf_op jit(solution)/shard_map/ppermute | solution.py:34
  91.3 1.5 collective-permute-done.7.other
  92.8 1.6 copy-done.3
  94.4 1.8 shard_map.47
  96.2 1.7 collective-permute-start.8
  97.9 3.5 %collective-permute-start.9 = (bf16[512,256]{1,0:T(8,128)(2,1)S(1)}, bf16[512,256]{1,0:T(8,128)(2,1)S(1)}, u32[]{:S(2)}, u32[]{:S(2)}) collective-permute-start(bf16[512,256]{1,0:T(8,128)(2,1)S(1)} %get-tuple-element.38), channel_id=1, source_target_pairs={{0,1},{1,2},{2,3},{3,0},{4,5},{5,6},{6,7},{7,4},{8,9},{9,10},{10,1... | collective-permute-start | bytes 786440 | tf_op jit(solution)/shard_map/ppermute | solution.py:30
  101.4 1.8 shard_map.46
  103.3 2.2 %collective-permute-done.8 = bf16[512,256]{1,0:T(8,128)(2,1)S(1)} collective-permute-done((bf16[512,256]{1,0:T(8,128)(2,1)S(1)}, bf16[512,256]{1,0:T(8,128)(2,1)S(1)}, u32[]{:S(2)}, u32[]{:S(2)}) %collective-permute-start.8) | collective-permute-done | bytes 262176 | tf_op jit(solution)/shard_map/ppermute | solution.py:30
  105.6 6.3 %collective-permute-done.9 = bf16[512,256]{1,0:T(8,128)(2,1)S(1)} collective-permute-done((bf16[512,256]{1,0:T(8,128)(2,1)S(1)}, bf16[512,256]{1,0:T(8,128)(2,1)S(1)}, u32[]{:S(2)}, u32[]{:S(2)}) %collective-permute-start.9) | collective-permute-done | bytes 262176 | tf_op jit(solution)/shard_map/ppermute | solution.py:30
  114.0 2.5 %collective-permute-start.12 = (bf16[512,256]{1,0:T(8,128)(2,1)S(1)}, bf16[512,256]{1,0:T(8,128)(2,1)S(1)}, u32[]{:S(2)}, u32[]{:S(2)}) collective-permute-start(bf16[512,256]{1,0:T(8,128)(2,1)S(1)} %get-tuple-element.50.refs_1_), channel_id=1, source_target_pairs={{0,3},{1,0},{2,1},{3,2},{4,7},{5,4},{6,5},{7,6},{8,11},{9,8},{10,9... | collective-permute-start | bytes 786440 | tf_op jit(solution)/shard_map/ppermute | solution.py:30
  118.9 3.0 %collective-permute-done.13.refs_3_ = bf16[512,256]{1,0:T(8,128)(2,1)S(1)} collective-permute-done((bf16[512,256]{1,0:T(8,128)(2,1)S(1)}, bf16[512,256]{1,0:T(8,128)(2,1)S(1)}, u32[]{:S(2)}, u32[]{:S(2)}) %collective-permute-start.13) | collective-permute-done | bytes 262176 | tf_op jit(solution)/shard_map/ppermute | solution.py:30
  121.9 2.0 shard_map.49
  123.9 5.2 %collective-permute-done.11.refs_1_ = bf16[512,256]{1,0:T(8,128)(2,1)S(1)} collective-permute-done((bf16[512,256]{1,0:T(8,128)(2,1)S(1)}, bf16[512,256]{1,0:T(8,128)(2,1)S(1)}, u32[]{:S(2)}, u32[]{:S(2)}) %collective-permute-start.11) | collective-permute-done | bytes 262176 | tf_op jit(solution)/shard_map/ppermute | solution.py:30
  130.6 1.6 collective-permute-start.14
  132.3 1.6 collective-permute-done.15
  134.2 22.8 %all_to_all.36 = bf16[32,8,1280]{2,1,0:T(8,128)(2,1)S(1)} all-to-all(bf16[32,8,1280]{2,1,0:T(8,128)(2,1)S(1)} %maximum_bitcast_fusion), channel_id=1, replica_groups={{0,8,16,24,32,40,48,56,64,72,80,88,96,104,112,120,128,136,144,152,160,1..., dimensions={0} | all-to-all | bytes 1310720 | tf_op jit(solution)/shard_map/all_to_all | solution.py:38
  157.2 22.9 %all_to_all.37 = bf16[32,8,1280]{2,1,0:T(8,128)(2,1)S(1)} all-to-all(bf16[32,8,1280]{2,1,0:T(8,128)(2,1)S(1)} %tile.5), channel_id=1, replica_groups={{0,8,16,24,32,40,48,56,64,72,80,88,96,104,112,120,128,136,144,152,160,1..., dimensions={0} | all-to-all | bytes 1310720 | tf_op jit(solution)/shard_map/all_to_all | solution.py:38
  180.2 3.8 %collective-permute-start.16 = (bf16[256,256]{1,0:T(8,128)(2,1)S(1)}, bf16[256,256]{1,0:T(8,128)(2,1)S(1)}, u32[]{:S(2)}, u32[]{:S(2)}) collective-permute-start(bf16[256,256]{1,0:T(8,128)(2,1)S(1)} %slice.24), channel_id=1, source_target_pairs={{0,4},{4,0},{8,12},{12,8},{16,20},{20,16},{24,28},{28,24},{32,36},... | collective-permute-start | bytes 393224 | tf_op jit(solution)/shard_map/ppermute | solution.py:34
  185.0 12.1 %shard_map.51.inverse = f32[256,256]{1,0:T(8,128)S(1)} custom-call(s32[2]{0:T(128)S(1)} %pad_add_fusion.place, bf16[256,1280]{1,0:T(8,128)(2,1)S(1)} %bitcast.10, bf16[256,256]{1,0:T(8,128)(2,1)S(1)} %collective-permute-done.16.swapped), custom_call_target="tpu_custom_call" | custom-call | flops 10000000000 | bytes 1048576 | tf_op jit(solution)/shard_map/pallas_call | solution.py:260
  197.1 3.0 %shard_map.52 = (bf16[512,256]{1,0:T(8,128)(2,1)}, f32[256,2048]{1,0:T(8,128)}) custom-call(s32[2]{0:T(128)S(1)} %pad_add_fusion.place, f32[256,256]{1,0:T(8,128)S(1)} %shard_map.51.inverse, f32[512,256]{1,0:T(8,128)S(1)} %get-tuple-element.51.power, bf16[256,1280]{1,0:T(8,128)(2,1)S(1)} %bitcast.11, bf16[256,1024]{1,0:T(8,128)(2,1)S(1)} %collective-permute-done.17.other), custom_call_target="tpu_custom_call" | custom-call | tf_op jit(solution)/shard_map/pallas_call | solution.py:288
  (50 shorter events, 14.9 us)
Async XLA Ops:
  4.7 29.2 %copy-start.2 = (bf16[512,2048]{1,0:T(8,128)(2,1)}, bf16[512,2048]{1,0:T(8,128)(2,1)S(1)}, u32[]{:S(2)}) copy-start(bf16[512,2048]{1,0:T(8,128)(2,1)S(1)} %get-tuple-element.25.refs_0_) | copy-start | bytes 6291460
  4.7 10.2 %collective-permute-start = (bf16[512,256]{1,0:T(8,128)(2,1)S(1)}, bf16[512,256]{1,0:T(8,128)(2,1)S(1)}, u32[]{:S(2)}, u32[]{:S(2)}) collective-permute-start(bf16[512,256]{1,0:T(8,128)(2,1)S(1)} %get-tuple-element.28), channel_id=1, source_target_pairs={{0,2},{1,3},{2,0},{3,1},{4,6},{5,7},{6,4},{7,5},{8,10},{9,11},{10,... | collective-permute-start | bytes 786440 | tf_op jit(solution)/shard_map/ppermute | solution.py:30
  8.5 11.7 %collective-permute-start.1 = (bf16[512,256]{1,0:T(8,128)(2,1)S(1)}, bf16[512,256]{1,0:T(8,128)(2,1)S(1)}, u32[]{:S(2)}, u32[]{:S(2)}) collective-permute-start(bf16[512,256]{1,0:T(8,128)(2,1)S(1)} %get-tuple-element.29), channel_id=1, source_target_pairs={{0,1},{1,2},{2,3},{3,0},{4,5},{5,6},{6,7},{7,4},{8,9},{9,10},{10,1... | collective-permute-start | bytes 786440 | tf_op jit(solution)/shard_map/ppermute | solution.py:30
  12.5 12.8 %copy-start.5 = (bf16[512,2048]{1,0:T(8,128)(2,1)}, bf16[512,2048]{1,0:T(8,128)(2,1)S(1)}, u32[]{:S(2)}) copy-start(bf16[512,2048]{1,0:T(8,128)(2,1)S(1)} %get-tuple-element.33.refs_0_.refs_1_) | copy-start | bytes 6291460
  12.5 15.3 %copy-start = (bf16[512,2048]{1,0:T(8,128)(2,1)}, bf16[512,2048]{1,0:T(8,128)(2,1)S(1)}, u32[]{:S(2)}) copy-start(bf16[512,2048]{1,0:T(8,128)(2,1)S(1)} %get-tuple-element.32.refs_1_.refs_0_) | copy-start | bytes 6291460
  12.5 7.7 %collective-permute-start.2 = (bf16[512,256]{1,0:T(8,128)(2,1)S(1)}, bf16[512,256]{1,0:T(8,128)(2,1)S(1)}, u32[]{:S(2)}, u32[]{:S(2)}) collective-permute-start(bf16[512,256]{1,0:T(8,128)(2,1)S(1)} %get-tuple-element.30), channel_id=1, source_target_pairs={{0,3},{1,0},{2,1},{3,2},{4,7},{5,4},{6,5},{7,6},{8,11},{9,8},{10,9... | collective-permute-start | bytes 786440 | tf_op jit(solution)/shard_map/ppermute | solution.py:30
  20.3 7.4 %collective-permute-start.5 = (bf16[512,256]{1,0:T(8,128)(2,1)S(1)}, bf16[512,256]{1,0:T(8,128)(2,1)S(1)}, u32[]{:S(2)}, u32[]{:S(2)}) collective-permute-start(bf16[512,256]{1,0:T(8,128)(2,1)S(1)} %add_convert_fusion.2.refs_1_), channel_id=1, source_target_pairs={{0,1},{1,2},{2,3},{3,0},{4,5},{5,6},{6,7},{7,4},{8,9},{9,10},{10,1... | collective-permute-start | bytes 786440 | tf_op jit(solution)/shard_map/ppermute | solution.py:30
  21.6 6.2 %collective-permute-start.4 = (bf16[512,256]{1,0:T(8,128)(2,1)S(1)}, bf16[512,256]{1,0:T(8,128)(2,1)S(1)}, u32[]{:S(2)}, u32[]{:S(2)}) collective-permute-start(bf16[512,256]{1,0:T(8,128)(2,1)S(1)} %add_convert_fusion.2.refs_1_), channel_id=1, source_target_pairs={{0,3},{1,0},{2,1},{3,2},{4,7},{5,4},{6,5},{7,6},{8,11},{9,8},{10,9... | collective-permute-start | bytes 786440 | tf_op jit(solution)/shard_map/ppermute | solution.py:30
  23.1 10.7 %collective-permute-start.3 = (bf16[512,256]{1,0:T(8,128)(2,1)S(1)}, bf16[512,256]{1,0:T(8,128)(2,1)S(1)}, u32[]{:S(2)}, u32[]{:S(2)}) collective-permute-start(bf16[512,256]{1,0:T(8,128)(2,1)S(1)} %add_convert_fusion.2.refs_1_), channel_id=1, source_target_pairs={{0,2},{1,3},{2,0},{3,1},{4,6},{5,7},{6,4},{7,5},{8,10},{9,11},{10,... | collective-permute-start | bytes 786440 | tf_op jit(solution)/shard_map/ppermute | solution.py:30
  35.2 4.9 %collective-permute-start.6 = (bf16[256,1024]{1,0:T(8,128)(2,1)S(1)}, bf16[256,1024]{1,0:T(8,128)(2,1)S(1)}, u32[]{:S(2)}, u32[]{:S(2)}) collective-permute-start(bf16[256,1024]{1,0:T(8,128)(2,1)S(1)} %get-tuple-element.35), channel_id=1, source_target_pairs={{0,4},{4,0},{8,12},{12,8},{16,20},{20,16},{24,28},{28,24},{32,36},... | collective-permute-start | bytes 1572872 | tf_op jit(solution)/shard_map/ppermute | solution.py:34
  87.7 13.7 %copy-start.1 = (bf16[512,2048]{1,0:T(8,128)(2,1)S(1)}, bf16[512,2048]{1,0:T(8,128)(2,1)}, u32[]{:S(2)}) copy-start(bf16[512,2048]{1,0:T(8,128)(2,1)} %copy-done) | copy-start | bytes 6291460
  87.7 5.1 %collective-permute-start.7 = (bf16[256,1024]{1,0:T(8,128)(2,1)S(1)}, bf16[256,1024]{1,0:T(8,128)(2,1)S(1)}, u32[]{:S(2)}, u32[]{:S(2)}) collective-permute-start(bf16[256,1024]{1,0:T(8,128)(2,1)S(1)} %bitcast.12), channel_id=1, source_target_pairs={{0,4},{4,0},{8,12},{12,8},{16,20},{20,16},{24,28},{28,24},{32,36},... | collective-permute-start | bytes 1572872 | tf_op jit(solution)/shard_map/ppermute | solution.py:34
  92.8 1.6 copy-start.3
  94.4 7.0 %copy-start.6 = (bf16[512,2048]{1,0:T(8,128)(2,1)S(1)}, bf16[512,2048]{1,0:T(8,128)(2,1)}, u32[]{:S(2)}) copy-start(bf16[512,2048]{1,0:T(8,128)(2,1)} %copy-done.5) | copy-start | bytes 6291460
  96.2 9.3 %collective-permute-start.8 = (bf16[512,256]{1,0:T(8,128)(2,1)S(1)}, bf16[512,256]{1,0:T(8,128)(2,1)S(1)}, u32[]{:S(2)}, u32[]{:S(2)}) collective-permute-start(bf16[512,256]{1,0:T(8,128)(2,1)S(1)} %get-tuple-element.37), channel_id=1, source_target_pairs={{0,2},{1,3},{2,0},{3,1},{4,6},{5,7},{6,4},{7,5},{8,10},{9,11},{10,... | collective-permute-start | bytes 786440 | tf_op jit(solution)/shard_map/ppermute | solution.py:30
  97.9 14.0 %collective-permute-start.9 = (bf16[512,256]{1,0:T(8,128)(2,1)S(1)}, bf16[512,256]{1,0:T(8,128)(2,1)S(1)}, u32[]{:S(2)}, u32[]{:S(2)}) collective-permute-start(bf16[512,256]{1,0:T(8,128)(2,1)S(1)} %get-tuple-element.38), channel_id=1, source_target_pairs={{0,1},{1,2},{2,3},{3,0},{4,5},{5,6},{6,7},{7,4},{8,9},{9,10},{10,1... | collective-permute-start | bytes 786440 | tf_op jit(solution)/shard_map/ppermute | solution.py:30
  103.2 9.9 %collective-permute-start.10 = (bf16[512,256]{1,0:T(8,128)(2,1)S(1)}, bf16[512,256]{1,0:T(8,128)(2,1)S(1)}, u32[]{:S(2)}, u32[]{:S(2)}) collective-permute-start(bf16[512,256]{1,0:T(8,128)(2,1)S(1)} %get-tuple-element.39), channel_id=1, source_target_pairs={{0,3},{1,0},{2,1},{3,2},{4,7},{5,4},{6,5},{7,6},{8,11},{9,8},{10,9... | collective-permute-start | bytes 786440 | tf_op jit(solution)/shard_map/ppermute | solution.py:30
  113.2 8.7 %collective-permute-start.13 = (bf16[512,256]{1,0:T(8,128)(2,1)S(1)}, bf16[512,256]{1,0:T(8,128)(2,1)S(1)}, u32[]{:S(2)}, u32[]{:S(2)}) collective-permute-start(bf16[512,256]{1,0:T(8,128)(2,1)S(1)} %get-tuple-element.50.refs_1_), channel_id=1, source_target_pairs={{0,1},{1,2},{2,3},{3,0},{4,5},{5,6},{6,7},{7,4},{8,9},{9,10},{10,1... | collective-permute-start | bytes 786440 | tf_op jit(solution)/shard_map/ppermute | solution.py:30
  114.0 7.9 %collective-permute-start.12 = (bf16[512,256]{1,0:T(8,128)(2,1)S(1)}, bf16[512,256]{1,0:T(8,128)(2,1)S(1)}, u32[]{:S(2)}, u32[]{:S(2)}) collective-permute-start(bf16[512,256]{1,0:T(8,128)(2,1)S(1)} %get-tuple-element.50.refs_1_), channel_id=1, source_target_pairs={{0,3},{1,0},{2,1},{3,2},{4,7},{5,4},{6,5},{7,6},{8,11},{9,8},{10,9... | collective-permute-start | bytes 786440 | tf_op jit(solution)/shard_map/ppermute | solution.py:30
  116.5 12.6 %collective-permute-start.11 = (bf16[512,256]{1,0:T(8,128)(2,1)S(1)}, bf16[512,256]{1,0:T(8,128)(2,1)S(1)}, u32[]{:S(2)}, u32[]{:S(2)}) collective-permute-start(bf16[512,256]{1,0:T(8,128)(2,1)S(1)} %get-tuple-element.50.refs_1_), channel_id=1, source_target_pairs={{0,2},{1,3},{2,0},{3,1},{4,6},{5,7},{6,4},{7,5},{8,10},{9,11},{10,... | collective-permute-start | bytes 786440 | tf_op jit(solution)/shard_map/ppermute | solution.py:30
  121.9 7.2 %copy-start.4 = (bf16[512,2048]{1,0:T(8,128)(2,1)S(1)}, bf16[512,2048]{1,0:T(8,128)(2,1)}, u32[]{:S(2)}) copy-start(bf16[512,2048]{1,0:T(8,128)(2,1)} %copy-done.2) | copy-start | bytes 6291460
  130.6 3.4 %collective-permute-start.14 = (bf16[256,1024]{1,0:T(8,128)(2,1)S(1)}, bf16[256,1024]{1,0:T(8,128)(2,1)S(1)}, u32[]{:S(2)}, u32[]{:S(2)}) collective-permute-start(bf16[256,1024]{1,0:T(8,128)(2,1)S(1)} %get-tuple-element.45), channel_id=1, source_target_pairs={{0,4},{4,0},{8,12},{12,8},{16,20},{20,16},{24,28},{28,24},{32,36},... | collective-permute-start | bytes 1572872 | tf_op jit(solution)/shard_map/ppermute | solution.py:34
  132.2 1.7 collective-permute-start.15
  180.2 4.8 %collective-permute-start.16 = (bf16[256,256]{1,0:T(8,128)(2,1)S(1)}, bf16[256,256]{1,0:T(8,128)(2,1)S(1)}, u32[]{:S(2)}, u32[]{:S(2)}) collective-permute-start(bf16[256,256]{1,0:T(8,128)(2,1)S(1)} %slice.24), channel_id=1, source_target_pairs={{0,4},{4,0},{8,12},{12,8},{16,20},{20,16},{24,28},{28,24},{32,36},... | collective-permute-start | bytes 393224 | tf_op jit(solution)/shard_map/ppermute | solution.py:34
  184.1 13.0 %collective-permute-start.17 = (bf16[256,1024]{1,0:T(8,128)(2,1)S(1)}, bf16[256,1024]{1,0:T(8,128)(2,1)S(1)}, u32[]{:S(2)}, u32[]{:S(2)}) collective-permute-start(bf16[256,1024]{1,0:T(8,128)(2,1)S(1)} %slice.25), channel_id=1, source_target_pairs={{0,4},{4,0},{8,12},{12,8},{16,20},{20,16},{24,28},{28,24},{32,36},... | collective-permute-start | bytes 1572872 | tf_op jit(solution)/shard_map/ppermute | solution.py:34

commit v3 on v2

v3 whole, which is shorter than its diff:
```python
import functools
import math

import jax
import jax.numpy as jnp
from jax import lax
from jax.experimental import pallas as pl
from jax.experimental.pallas import tpu as pltpu
from jax.sharding import PartitionSpec as P

NZ, NX, NC, NY = 8, 4, 2, 4
PLANE = NZ * NX
F32, BF16 = jnp.float32, jnp.bfloat16
EXACT = lax.Precision.HIGHEST
FIRST = (((0,), (0,)), ((), ()))
LAST = (((1,), (1,)), ((), ()))
PLAIN = (((1,), (0,)), ((), ()))
PRODUCT = pltpu.CompilerParams(vmem_limit_bytes=16 * 2**20)


def row_index(z, x, c):
    return (z * NX + x) * NC + c


Y_SHIFT = {k: [(i, (i + k) % NY) for i in range(NY)] for k in range(1, NY)}
CORE_SWAP = [(i, i ^ 1) for i in range(NZ * NX * NC)]
PLANES = [[row_index(z, x, c) for z in range(NZ) for x in range(NX)] for c in range(NC)]


def from_y(value, k):
    return lax.ppermute(value, "cols", Y_SHIFT[k])


def from_core(value):
    return lax.ppermute(value, "rows", CORE_SWAP)


def exchange(value):
    return lax.all_to_all(value, "rows", 0, 0, tiled=True, axis_index_groups=PLANES)


VMEM = pl.BlockSpec(memory_space=pltpu.VMEM)
SMEM = pl.BlockSpec(memory_space=pltpu.SMEM)
HBM = pl.BlockSpec(memory_space=pltpu.HBM)


def resident(value):
    return pltpu.with_memory_space_constraint(value, pltpu.VMEM)


def in_hbm(value):
    return pltpu.with_memory_space_constraint(value, pltpu.HBM)


def products(steps, rows, width, rank):
    return pl.CostEstimate(
        flops=2 * steps * rows * width * rank, bytes_accessed=steps * rows * width * 2, transcendentals=0
    )


def load_kernel(quarters, keep_right, place, a, right, *refs):
    count = len(quarters)
    outs, kept, refs = refs[:count], refs[count : 2 * count], refs[2 * count :]
    sems = refs[-1]
    m = outs[0].shape[0]
    copies = []
    if keep_right:
        copies.append(pltpu.make_async_copy(right, refs[0], sems.at[count]))
        right = refs[0]
    for i, k in enumerate(quarters):
        rows = pl.ds(pl.multiple_of(lax.rem(place[0] + k, NY) * m, m), m)
        copies.append(pltpu.make_async_copy(a.at[rows, :], kept[i], sems.at[i]))
    for copy in copies:
        copy.start()
    if keep_right:
        copies.pop(0).wait()
    for i, out in enumerate(outs):
        @pl.when(place[0] >= 0)
        def _(i=i, out=out):
            copies[i].wait()
            part = jnp.dot(kept[i][...], right[...], preferred_element_type=F32)
            out[...] = part.astype(out.dtype)


def load_part(place, activations, right, quarters, types, keep_right):
    rows, width = activations.shape
    count, m, rank = len(quarters), rows // NY, right.shape[1]
    return pl.pallas_call(
        functools.partial(load_kernel, quarters, keep_right),
        in_specs=[SMEM, HBM, HBM if keep_right else VMEM],
        out_specs=[VMEM] * (2 * count + keep_right),
        out_shape=[jax.ShapeDtypeStruct((m, rank), t) for t in types]
        + [pltpu.VMEM((m, width), BF16)] * count
        + [pltpu.VMEM(right.shape, BF16)] * keep_right,
        scratch_shapes=[pltpu.SemaphoreType.DMA((count + keep_right,))],
        compiler_params=PRODUCT,
        cost_estimate=products(count, m, width, rank),
    )(place, in_hbm(activations), (in_hbm if keep_right else resident)(right))


def load_forward(place, activations, right):
    two, one, a2, a1, right = load_part(place, activations, right, (2, 1), (BF16, BF16), True)
    three, own, a3, a0 = load_part(place, activations, right, (3, 0), (BF16, F32), False)
    return (one, two, three, own), (a0, a1, a2, a3)


def forward_kernel(side, count, place, image, *refs):
    kept, refs = refs[:count], refs[count:]
    before, outs = refs[: len(refs) - count], refs[len(refs) - count :]
    half = image.shape[1]
    at = (place[1] if side == 0 else 1 - place[1]) * half
    columns = pl.ds(pl.multiple_of(at, half), half)
    for i, out in enumerate(outs):
        part = lax.dot_general(kept[i][:, columns], image[...], LAST, preferred_element_type=F32)
        if before:
            part += before[i][...]
        out[...] = part.astype(out.dtype)


def forward_part(place, kept, image, side, before, types):
    m = kept[0].shape[0]
    rank, half = image.shape
    count = len(kept)
    last = [jax.ShapeDtypeStruct((m, rank), t) for t in types]
    return pl.pallas_call(
        functools.partial(forward_kernel, side, count),
        in_specs=[SMEM] + [VMEM] * (1 + count + len(before)),
        out_specs=[VMEM] * count,
        out_shape=last if before else [pltpu.VMEM((m, rank), t) for t in types],
        compiler_params=PRODUCT,
        cost_estimate=products(count, m, half, rank),
    )(place, image, *map(resident, kept), *map(resident, before))


def forward(place, kept, image):
    parts = forward_part(place, kept, image, 0, (), (F32,) * NY)
    own, one, two, three = forward_part(
        place, kept, from_core(image), 1, parts, (F32, BF16, BF16, BF16)
    )
    return one, two, three, own


def back_kernel(image, kept, out):
    out[...] = lax.dot_general(image[...], kept[...], FIRST, preferred_element_type=F32)


def back_own(kept, image):
    m, width = kept.shape
    rank = image.shape[1]
    return pl.pallas_call(
        back_kernel,
        in_specs=[VMEM] * 2,
        out_specs=VMEM,
        out_shape=pltpu.VMEM((rank, width), F32),
        compiler_params=PRODUCT,
        cost_estimate=products(1, m, width, rank),
    )(image, resident(kept))


def back_half_kernel(side, count, place, before, *refs):
    kept, images, out, total = refs[:count], refs[count : 2 * count], refs[-2], refs[-1]
    half = out.shape[1]
    at = (place[1] if side == 0 else 1 - place[1]) * half
    columns = pl.ds(pl.multiple_of(at, half), half)
    part = before[:, columns]
    for i, image in enumerate(images):
        part += lax.dot_general(image[...], kept[i][:, columns], FIRST, preferred_element_type=F32)
        if i + 1 < count:
            total[...] = part
            part = total[...]
    out[...] = part.astype(out.dtype)


def back_half(place, before, kept, images, side, dtype):
    m, width = kept[0].shape
    rank, half = images[0].shape[1], width // NC
    count = len(images)
    return pl.pallas_call(
        functools.partial(back_half_kernel, side, count),
        in_specs=[SMEM] + [VMEM] * (1 + 2 * count),
        out_specs=VMEM,
        out_shape=jax.ShapeDtypeStruct((rank, half), dtype),
        scratch_shapes=[pltpu.VMEM((rank, half), F32)],
        compiler_params=PRODUCT,
        cost_estimate=products(count, m, half, rank),
    )(place, resident(before), *map(resident, kept), *images)


def back(place, kept, images):
    total = back_own(kept[0], images[0])
    rest = (place, total, (kept[1], kept[3], kept[2]), (images[1], images[3], images[2]))
    other = from_core(back_half(*rest, 1, BF16))
    return (back_half(*rest, 0, F32) + other.astype(F32)).astype(BF16)


def gram_kernel(place, one, two, three, four, mine, other, total):
    for i, image in enumerate((one, two, three, four)):
        value = image[...]
        part = lax.dot_general(value, value, FIRST, preferred_element_type=F32)
        total[...] = part if i == 0 else total[...] + part
    half = mine.shape[1]
    first = place[1] == 0
    mine[...] = jnp.where(first, total[:, :half], total[:, half:])
    other[...] = jnp.where(first, total[:, half:], total[:, :half])


def gram_part(place, images):
    m, rank = images[0].shape
    shape = jax.ShapeDtypeStruct((rank, rank // NC), F32)
    return pl.pallas_call(
        gram_kernel,
        in_specs=[SMEM] + [VMEM] * NY,
        out_specs=[VMEM] * 2,
        out_shape=[shape] * 2,
        scratch_shapes=[pltpu.VMEM((rank, rank), F32)],
        compiler_params=PRODUCT,
        cost_estimate=products(NY, m, rank, rank),
    )(place, *images)


def small_inverse(block, block_at):
    rows = lax.broadcasted_iota(jnp.int32, (8, 128), 0)
    e = list(block)
    groups = len(e)
    for group in range(groups):
        c = {}
        for j in range(8):
            lane = block_at + 8 * group + j
            for g in range(group, groups):
                c[j, g] = jnp.broadcast_to(e[g][:, lane : lane + 1], (8, 128))
        for k in range(8):
            root = lax.rsqrt(jnp.broadcast_to(c[k, group][k : k + 1, :], (8, 128)))
            col = {g: c[k, g] * root for g in range(group, groups)}
            row = jnp.broadcast_to(e[group][k : k + 1, :], (8, 128)) * root
            below = jnp.where(rows > k, col[group], 0.0)
            for j in range(k + 1, 8):
                times = jnp.broadcast_to(col[group][j : j + 1, :], (8, 128))
                c[j, group] = c[j, group] - below * times
                for g in range(group + 1, groups):
                    c[j, g] = c[j, g] - col[g] * times
            e[group] = jnp.where(rows == k, row, e[group] - below * row)
            for g in range(group + 1, groups):
                e[g] = e[g] - col[g] * row
    return e


def invert_block(m):
    n = m.shape[0]
    r = lax.broadcasted_iota(jnp.int32, (n, n), 0)
    c = lax.broadcasted_iota(jnp.int32, (n, n), 1)
    m[:, n:] = jnp.where(r == c, 1.0, 0.0)
    lanes = lax.broadcasted_iota(jnp.int32, (8, n), 1)
    rows = lax.broadcasted_iota(jnp.int32, (8, n), 0)
    size = n // 2
    wide = lax.broadcasted_iota(jnp.int32, (size, n), 1)
    for k0 in range(0, n, size):
        at = (k0 + size) % n
        groups = []
        for g in range(size // 8):
            v = pltpu.roll(m[k0 + 8 * g : k0 + 8 * g + 8, :n], size, 1)
            eye = jnp.where(lanes - k0 == rows + 8 * g, 1.0, 0.0)
            groups.append(jnp.where((lanes >= at) & (lanes < at + size), v, eye))
        e = jnp.concatenate(small_inverse(groups, at), axis=0)
        e = jnp.where((wide >= k0) & (wide < k0 + size), e, 0.0)
        panel = exact(e, m[...], PLAIN)
        m[k0 : k0 + size, :] = panel
        done = k0 + size
        if done < n:
            update = exact(panel[:, :n], panel, FIRST)
            m[done:, :] = m[done:, :] - update[done:]


def exact(a, b, dims):
    return lax.dot_general(a, b, dims, precision=EXACT, preferred_element_type=F32)


def inverse_kernel(scale, start, place, gathered, swapped, out, gram, m):
    n = out.shape[0]
    half = n // NC
    for at, source, first in ((place[1], gathered, start), (1 - place[1], swapped, 0)):
        high = source[:, first : first + half].astype(F32)
        low = source[:, first + half : first + n].astype(F32)
        gram[:, pl.ds(pl.multiple_of(at * half, half), half)] = (high + low) * scale
    m[:, :half] = gram[:half, :half]
    invert_block(m)
    one = m[:, half:]
    cross = exact(one, gram[:half, half:], PLAIN)
    m[:, :half] = gram[half:, half:] - exact(cross, cross, FIRST)
    invert_block(m)
    two = m[:, half:]
    out[:half, :half] = one
    out[:half, half:] = jnp.zeros_like(one)
    out[half:, :half] = -exact(two, exact(cross, one, FIRST), PLAIN)
    out[half:, half:] = two


def factor_inverse(place, gathered, start, swapped, scale):
    n = gathered.shape[0]
    return pl.pallas_call(
        functools.partial(inverse_kernel, scale, start),
        in_specs=[SMEM, VMEM, VMEM],
        out_specs=VMEM,
        out_shape=jax.ShapeDtypeStruct((n, n), F32),
        scratch_shapes=[pltpu.VMEM((n, n), F32), pltpu.VMEM((n // 2, n), F32)],
        compiler_params=PRODUCT,
        cost_estimate=pl.CostEstimate(flops=10**10, bytes_accessed=2**20, transcendentals=0),
    )(place, gathered, swapped)


def halves_product(a, b, dims):
    a, b = split(a), split(b)
    terms = [
        lax.dot_general(x, y, dims, preferred_element_type=F32)
        for x, y in ((a[0], b[0]), (a[0], b[1]), (a[1], b[0]))
    ]
    return terms[0] + (terms[1] + terms[2])


def last_kernel(inverse_root, place, inverse, power, gathered, other, basis, projected, rows, wide, sems):
    half = other.shape[1]
    scaled = inverse[...] * inverse_root
    high = scaled.astype(BF16)
    low = (scaled - high.astype(F32)).astype(BF16)
    copies = []
    for i, (at, source) in enumerate(((place[1], gathered), (1 - place[1], other))):
        columns = pl.ds(pl.multiple_of(at * half, half), half)
        copies.append(pltpu.make_async_copy(wide.at[i], projected.at[:, columns], sems.at[i]))

        @pl.when(place[0] >= 0)
        def _(i=i, source=source):
            value = source[:, :half]
            wide[i] = jnp.dot(high, value, preferred_element_type=F32) + jnp.dot(
                low, value, preferred_element_type=F32
            )
            copies[i].start()

    copies.append(pltpu.make_async_copy(rows, basis, sems.at[2]))
    rows[...] = halves_product(power[...], inverse[...], LAST).astype(BF16)
    copies[2].start()
    for copy in copies:
        copy.wait()


def last(place, inverse, power, gathered, other, inverse_root):
    m, rank = power.shape
    half = other.shape[1]
    return pl.pallas_call(
        functools.partial(last_kernel, inverse_root),
        in_specs=[SMEM] + [VMEM] * 4,
        out_specs=[HBM] * 2,
        out_shape=[
            jax.ShapeDtypeStruct((m, rank), BF16),
            jax.ShapeDtypeStruct((rank, NC * half), F32),
        ],
        scratch_shapes=[
            pltpu.VMEM((m, rank), BF16),
            pltpu.VMEM((NC, rank, half), F32),
            pltpu.SemaphoreType.DMA((3,)),
        ],
        compiler_params=PRODUCT,
    )(place, inverse, power, gathered, other)


def sum_over_y(one, two, three, own):
    got = [from_y(two, 2), from_y(one, 1), from_y(three, 3)]
    return own + got[0].astype(F32) + got[1].astype(F32) + got[2].astype(F32)


def gather_over_y(mine):
    far, on, behind = from_y(mine, 2), from_y(mine, 3), from_y(mine, 1)
    return mine, on, far, behind


def spread_kernel(gram_at, got, out):
    rows = 2 * out.shape[0] // PLANE
    total = None
    for at in range(0, got.shape[0], rows):
        pair = got[at : at + rows, :].astype(F32)
        pair = pair[: rows // 2] + pair[rows // 2 :]
        total = pair if total is None else total + pair
    mine = total.astype(BF16)
    if gram_at:
        columns = (total.shape[1] - gram_at) // 2
        gram = total[:, gram_at : gram_at + columns] + total[:, gram_at + columns :]
        mine = jnp.concatenate([total[:, :gram_at].astype(BF16), *split(gram)], axis=1)
    pair = jnp.concatenate([mine, mine], axis=0)
    for at in range(0, got.shape[0], rows):
        out[at : at + rows, :] = pair


def all_sum_over_plane(value, gram_at=0):
    spread = pl.pallas_call(
        functools.partial(spread_kernel, gram_at),
        in_specs=[VMEM],
        out_specs=VMEM,
        out_shape=jax.ShapeDtypeStruct(value.shape, BF16),
        compiler_params=PRODUCT,
    )(exchange(value))
    return exchange(spread)


def split(value):
    high = value.astype(BF16)
    return high, (value - high.astype(F32)).astype(BF16)


def per_device(activations, sketch):
    token_count = activations.shape[0] * lax.axis_size("rows")
    place = jnp.stack([lax.axis_index("cols"), lax.axis_index("rows") % NC]).astype(jnp.int32)

    pieces, kept = load_forward(place, activations, sketch)
    image = sum_over_y(*pieces).astype(BF16)
    back_image = all_sum_over_plane(back(place, kept, gather_over_y(image)))

    power = sum_over_y(*forward(place, kept, back_image))
    images = gather_over_y(power.astype(BF16))
    wide = back(place, kept, images)
    mine, other = gram_part(place, images)
    gram = mine + from_core(other)
    half = wide.shape[1]
    gathered = all_sum_over_plane(jnp.concatenate([wide, *split(gram)], axis=1), half)
    swapped = from_core(gathered[:, half:])
    inverse = factor_inverse(place, gathered, half, swapped, 1.0 / token_count)
    other = from_core(gathered[:, :half])
    return last(place, inverse, power, gathered, other, 1.0 / math.sqrt(token_count))


def solution(mesh):
    placed = (P("rows", "cols"), P("cols", None))
    return jax.shard_map(
        per_device,
        mesh=mesh,
        in_specs=placed,
        out_specs=(P(("rows", "cols"), None), P(None, "cols")),
        check_vma=False,
    )
```

time: 200 us -> 195 us (0.975)
  starting transfers between devices: 32.7 us -> 29.3 us
  Pallas kernels: 35.6 us -> 32.8 us
    ppermute x12, waiting for transfers between devices: 30 us -> 36.4 us  [from_y(): return lax.ppermute(value, 'cols', Y_SHIFT[k])]
    ppermute x6, waiting for transfers between devices: 5.31 us -> 0.62 us  [from_core(): return lax.ppermute(value, 'rows', CORE_SWAP)]
    ppermute x6, starting transfers between devices: 12.8 us -> 8.98 us  [from_core(): return lax.ppermute(value, 'rows', CORE_SWAP)]
    pallas_call x8 -> x11, Pallas kernels: 12.9 us -> 12.5 us  [the longest x4 6.16 us: back_half(): pl.pallas_call(functools.partial(back_half_kernel, side, count), in_specs...]
  transfers between devices with their start and end apart: 18 -> 18, of which waited for: 12 -> 8; matrix products, arithmetic and copies ran while one was open for 0% -> 0% of each run, Pallas kernels for 12% -> 11%
where the time goes in v3:
time: 195 us
  blocking collectives  93.9 us (48%)
  waiting for transfers between devices  37 us (19%)
  Pallas kernels  32.8 us (17%)
  starting transfers between devices  29.3 us (15%)
    all_to_all x4, blocking collectives, exchange(): lax.all_to_all(value, 'rows', 0, 0, tiled=True, axis_index_groups=PLANES)  93.9 us
    ppermute x12, waiting for transfers between devices, from_y(): return lax.ppermute(value, 'cols', Y_SHIFT[k])  36.4 us
    ppermute x12, starting transfers between devices, from_y(): return lax.ppermute(value, 'cols', Y_SHIFT[k])  20.3 us
    pallas_call x1, Pallas kernels, factor_inverse(): pl.pallas_call(functools.partial(inverse_kernel, scale, start), in_specs=...  10.2 us
    ppermute x6, starting transfers between devices, from_core(): return lax.ppermute(value, 'rows', CORE_SWAP)  8.98 us
    pallas_call x2, Pallas kernels, load_part(): pl.pallas_call(functools.partial(load_kernel, quarters, keep_right), in_s...  7.5 us
    pallas_call x4, Pallas kernels, back_half(): pl.pallas_call(functools.partial(back_half_kernel, side, count), in_specs...  6.16 us
  transfers between devices with their start and end apart: 18, of which 8 were waited for; matrix products, arithmetic and copies ran while one was open for 0% of the time, Pallas kernels for 11%

profile of v3, /device:TPU:1, one launch (start us, length us, event | category | flops | bytes accessed | tf_op | source)
XLA Modules:
  0.0 194.9 jit_solution(7371179099600662603)
XLA Ops:
  0.7 3.9 %shard_map.41 = (bf16[512,256]{1,0:T(8,128)(2,1)S(1)}, bf16[512,256]{1,0:T(8,128)(2,1)S(1)}, bf16[512,2048]{1,0:T(8,128)(2,1)S(1)}, bf16[512,2048]{1,0:T(8,128)(2,1)S(1)}, bf16[2048,256]{1,0:T(8,128)(2,1)S(1)}) custom-call(s32[2]{0:T(128)S(1)} %pad_add_fusion.place, bf16[2048,2048]{1,0:T(8,128)(2,1)} %a.3, bf16[2048,256]{1,0:T(8,128)(2,1)} %right.1), custom_call_target="tpu_custom_call" | custom-call | flops 1073741824 | bytes 4194304 | tf_op jit(solution)/shard_map/pallas_call | solution.py:88
  4.6 3.8 %collective-permute-start = (bf16[512,256]{1,0:T(8,128)(2,1)S(1)}, bf16[512,256]{1,0:T(8,128)(2,1)S(1)}, u32[]{:S(2)}, u32[]{:S(2)}) collective-permute-start(bf16[512,256]{1,0:T(8,128)(2,1)S(1)} %get-tuple-element.23), channel_id=1, source_target_pairs={{0,2},{1,3},{2,0},{3,1},{4,6},{5,7},{6,4},{7,5},{8,10},{9,11},{10,... | collective-permute-start | bytes 786440 | tf_op jit(solution)/shard_map/ppermute | solution.py:31
  8.9 3.6 %shard_map.42 = (bf16[512,256]{1,0:T(8,128)(2,1)S(1)}, f32[512,256]{1,0:T(8,128)S(1)}, bf16[512,2048]{1,0:T(8,128)(2,1)S(1)}, bf16[512,2048]{1,0:T(8,128)(2,1)S(1)}) custom-call(s32[2]{0:T(128)S(1)} %pad_add_fusion.place, bf16[2048,2048]{1,0:T(8,128)(2,1)} %a.3, bf16[2048,256]{1,0:T(8,128)(2,1)S(1)} %get-tuple-element.21.right), custom_call_target="tpu_custom_call" | custom-call | flops 1073741824 | bytes 4194304 | tf_op jit(solution)/shard_map/pallas_call | solution.py:88
  12.5 2.4 %collective-permute-start.2 = (bf16[512,256]{1,0:T(8,128)(2,1)S(1)}, bf16[512,256]{1,0:T(8,128)(2,1)S(1)}, u32[]{:S(2)}, u32[]{:S(2)}) collective-permute-start(bf16[512,256]{1,0:T(8,128)(2,1)S(1)} %get-tuple-element.25), channel_id=1, source_target_pairs={{0,3},{1,0},{2,1},{3,2},{4,7},{5,4},{6,5},{7,6},{8,11},{9,8},{10,9... | collective-permute-start | bytes 786440 | tf_op jit(solution)/shard_map/ppermute | solution.py:31
  14.8 5.4 %collective-permute-done.1 = bf16[512,256]{1,0:T(8,128)(2,1)S(1)} collective-permute-done((bf16[512,256]{1,0:T(8,128)(2,1)S(1)}, bf16[512,256]{1,0:T(8,128)(2,1)S(1)}, u32[]{:S(2)}, u32[]{:S(2)}) %collective-permute-start.1) | collective-permute-done | bytes 262176 | tf_op jit(solution)/shard_map/ppermute | solution.py:31
  20.3 2.1 %collective-permute-start.5 = (bf16[512,256]{1,0:T(8,128)(2,1)S(1)}, bf16[512,256]{1,0:T(8,128)(2,1)S(1)}, u32[]{:S(2)}, u32[]{:S(2)}) collective-permute-start(bf16[512,256]{1,0:T(8,128)(2,1)S(1)} %add_convert_fusion.2.image), channel_id=1, source_target_pairs={{0,2},{1,3},{2,0},{3,1},{4,6},{5,7},{6,4},{7,5},{8,10},{9,11},{10,... | collective-permute-start | bytes 786440 | tf_op jit(solution)/shard_map/ppermute | solution.py:31
  23.4 1.7 collective-permute-start.3
  25.8 2.3 %collective-permute-done.5.refs_5_ = bf16[512,256]{1,0:T(8,128)(2,1)S(1)} collective-permute-done((bf16[512,256]{1,0:T(8,128)(2,1)S(1)}, bf16[512,256]{1,0:T(8,128)(2,1)S(1)}, u32[]{:S(2)}, u32[]{:S(2)}) %collective-permute-start.5) | collective-permute-done | bytes 262176 | tf_op jit(solution)/shard_map/ppermute | solution.py:31
  28.1 7.5 %collective-permute-done.4.refs_4_ = bf16[512,256]{1,0:T(8,128)(2,1)S(1)} collective-permute-done((bf16[512,256]{1,0:T(8,128)(2,1)S(1)}, bf16[512,256]{1,0:T(8,128)(2,1)S(1)}, u32[]{:S(2)}, u32[]{:S(2)}) %collective-permute-start.4) | collective-permute-done | bytes 262176 | tf_op jit(solution)/shard_map/ppermute | solution.py:31
  35.7 1.5 shard_map.45
  37.9 1.5 shard_map.44
  39.6 28.1 %all_to_all.44 = bf16[32,8,1024]{2,1,0:T(8,128)(2,1)S(1)} all-to-all(bf16[32,8,1024]{2,1,0:T(8,128)(2,1)S(1)} %fusion), channel_id=1, replica_groups={{0,8,16,24,32,40,48,56,64,72,80,88,96,104,112,120,128,136,144,152,160,1..., dimensions={0} | all-to-all | bytes 1048576 | tf_op jit(solution)/shard_map/all_to_all | solution.py:39
  67.8 20.1 %all_to_all.45 = bf16[32,8,1024]{2,1,0:T(8,128)(2,1)S(1)} all-to-all(bf16[32,8,1024]{2,1,0:T(8,128)(2,1)S(1)} %bitcast.21), channel_id=1, replica_groups={{0,8,16,24,32,40,48,56,64,72,80,88,96,104,112,120,128,136,144,152,160,1..., dimensions={0} | all-to-all | bytes 1048576 | tf_op jit(solution)/shard_map/all_to_all | solution.py:39
  87.9 3.6 %collective-permute-start.7 = (bf16[256,1024]{1,0:T(8,128)(2,1)S(1)}, bf16[256,1024]{1,0:T(8,128)(2,1)S(1)}, u32[]{:S(2)}, u32[]{:S(2)}) collective-permute-start(bf16[256,1024]{1,0:T(8,128)(2,1)S(1)} %bitcast.18), channel_id=1, source_target_pairs={{0,4},{4,0},{8,12},{12,8},{16,20},{20,16},{24,28},{28,24},{32,36},... | collective-permute-start | bytes 1572872 | tf_op jit(solution)/shard_map/ppermute | solution.py:35
  91.5 1.8 shard_map.47
  93.3 1.8 shard_map.48
  95.1 2.0 %collective-permute-start.8 = (bf16[512,256]{1,0:T(8,128)(2,1)S(1)}, bf16[512,256]{1,0:T(8,128)(2,1)S(1)}, u32[]{:S(2)}, u32[]{:S(2)}) collective-permute-start(bf16[512,256]{1,0:T(8,128)(2,1)S(1)} %get-tuple-element.35), channel_id=1, source_target_pairs={{0,2},{1,3},{2,0},{3,1},{4,6},{5,7},{6,4},{7,5},{8,10},{9,11},{10,... | collective-permute-start | bytes 786440 | tf_op jit(solution)/shard_map/ppermute | solution.py:31
  97.5 2.4 %collective-permute-start.10 = (bf16[512,256]{1,0:T(8,128)(2,1)S(1)}, bf16[512,256]{1,0:T(8,128)(2,1)S(1)}, u32[]{:S(2)}, u32[]{:S(2)}) collective-permute-start(bf16[512,256]{1,0:T(8,128)(2,1)S(1)} %get-tuple-element.37), channel_id=1, source_target_pairs={{0,3},{1,0},{2,1},{3,2},{4,7},{5,4},{6,5},{7,6},{8,11},{9,8},{10,9... | collective-permute-start | bytes 786440 | tf_op jit(solution)/shard_map/ppermute | solution.py:31
  99.8 4.8 %collective-permute-done.8 = bf16[512,256]{1,0:T(8,128)(2,1)S(1)} collective-permute-done((bf16[512,256]{1,0:T(8,128)(2,1)S(1)}, bf16[512,256]{1,0:T(8,128)(2,1)S(1)}, u32[]{:S(2)}, u32[]{:S(2)}) %collective-permute-start.8) | collective-permute-done | bytes 262176 | tf_op jit(solution)/shard_map/ppermute | solution.py:31
  104.7 6.0 %collective-permute-done.9 = bf16[512,256]{1,0:T(8,128)(2,1)S(1)} collective-permute-done((bf16[512,256]{1,0:T(8,128)(2,1)S(1)}, bf16[512,256]{1,0:T(8,128)(2,1)S(1)}, u32[]{:S(2)}, u32[]{:S(2)}) %collective-permute-start.9) | collective-permute-done | bytes 262176 | tf_op jit(solution)/shard_map/ppermute | solution.py:31
  110.7 1.6 collective-permute-start.13
  113.0 2.0 %collective-permute-start.11 = (bf16[512,256]{1,0:T(8,128)(2,1)S(1)}, bf16[512,256]{1,0:T(8,128)(2,1)S(1)}, u32[]{:S(2)}, u32[]{:S(2)}) collective-permute-start(bf16[512,256]{1,0:T(8,128)(2,1)S(1)} %get-tuple-element.40.image.one), channel_id=1, source_target_pairs={{0,3},{1,0},{2,1},{3,2},{4,7},{5,4},{6,5},{7,6},{8,11},{9,8},{10,9... | collective-permute-start | bytes 786440 | tf_op jit(solution)/shard_map/ppermute | solution.py:31
  115.8 4.0 %collective-permute-done.13.refs_5_.three = bf16[512,256]{1,0:T(8,128)(2,1)S(1)} collective-permute-done((bf16[512,256]{1,0:T(8,128)(2,1)S(1)}, bf16[512,256]{1,0:T(8,128)(2,1)S(1)}, u32[]{:S(2)}, u32[]{:S(2)}) %collective-permute-start.13) | collective-permute-done | bytes 262176 | tf_op jit(solution)/shard_map/ppermute | solution.py:31
  119.8 6.4 %collective-permute-done.12.refs_4_.four = bf16[512,256]{1,0:T(8,128)(2,1)S(1)} collective-permute-done((bf16[512,256]{1,0:T(8,128)(2,1)S(1)}, bf16[512,256]{1,0:T(8,128)(2,1)S(1)}, u32[]{:S(2)}, u32[]{:S(2)}) %collective-permute-start.12) | collective-permute-done | bytes 262176 | tf_op jit(solution)/shard_map/ppermute | solution.py:31
  126.2 1.5 shard_map.51
  128.3 1.0 shard_map.52
  129.4 1.5 shard_map.50
  131.3 22.7 %all_to_all.46 = bf16[32,8,1280]{2,1,0:T(8,128)(2,1)S(1)} all-to-all(bf16[32,8,1280]{2,1,0:T(8,128)(2,1)S(1)} %maximum_bitcast_fusion), channel_id=1, replica_groups={{0,8,16,24,32,40,48,56,64,72,80,88,96,104,112,120,128,136,144,152,160,1..., dimensions={0} | all-to-all | bytes 1310720 | tf_op jit(solution)/shard_map/all_to_all | solution.py:39
  154.1 23.0 %all_to_all.47 = bf16[32,8,1280]{2,1,0:T(8,128)(2,1)S(1)} all-to-all(bf16[32,8,1280]{2,1,0:T(8,128)(2,1)S(1)} %bitcast.17), channel_id=1, replica_groups={{0,8,16,24,32,40,48,56,64,72,80,88,96,104,112,120,128,136,144,152,160,1..., dimensions={0} | all-to-all | bytes 1310720 | tf_op jit(solution)/shard_map/all_to_all | solution.py:39
  177.1 3.7 %collective-permute-start.16 = (bf16[256,256]{1,0:T(8,128)(2,1)S(1)}, bf16[256,256]{1,0:T(8,128)(2,1)S(1)}, u32[]{:S(2)}, u32[]{:S(2)}) collective-permute-start(bf16[256,256]{1,0:T(8,128)(2,1)S(1)} %slice.8), channel_id=1, source_target_pairs={{0,4},{4,0},{8,12},{12,8},{16,20},{20,16},{24,28},{28,24},{32,36},... | collective-permute-start | bytes 393224 | tf_op jit(solution)/shard_map/ppermute | solution.py:35
  181.9 10.2 %shard_map.54.inverse = f32[256,256]{1,0:T(8,128)S(1)} custom-call(s32[2]{0:T(128)S(1)} %pad_add_fusion.place, bf16[256,1280]{1,0:T(8,128)(2,1)S(1)} %bitcast.14, bf16[256,256]{1,0:T(8,128)(2,1)S(1)} %collective-permute-done.16.swapped), custom_call_target="tpu_custom_call" | custom-call | flops 10000000000 | bytes 1048576 | tf_op jit(solution)/shard_map/pallas_call | solution.py:299
  192.1 2.6 %shard_map.55 = (bf16[512,256]{1,0:T(8,128)(2,1)}, f32[256,2048]{1,0:T(8,128)}) custom-call(s32[2]{0:T(128)S(1)} %pad_add_fusion.place, f32[256,256]{1,0:T(8,128)S(1)} %shard_map.54.inverse, f32[512,256]{1,0:T(8,128)S(1)} %get-tuple-element.41.power, bf16[256,1280]{1,0:T(8,128)(2,1)S(1)} %bitcast.15, bf16[256,1024]{1,0:T(8,128)(2,1)S(1)} %collective-permute-done.17.other), custom_call_target="tpu_custom_call" | custom-call | tf_op jit(solution)/shard_map/pallas_call | solution.py:347
  (32 shorter events, 7.1 us)
Async XLA Ops:
  4.6 10.2 %collective-permute-start = (bf16[512,256]{1,0:T(8,128)(2,1)S(1)}, bf16[512,256]{1,0:T(8,128)(2,1)S(1)}, u32[]{:S(2)}, u32[]{:S(2)}) collective-permute-start(bf16[512,256]{1,0:T(8,128)(2,1)S(1)} %get-tuple-element.23), channel_id=1, source_target_pairs={{0,2},{1,3},{2,0},{3,1},{4,6},{5,7},{6,4},{7,5},{8,10},{9,11},{10,... | collective-permute-start | bytes 786440 | tf_op jit(solution)/shard_map/ppermute | solution.py:31
  8.5 11.7 %collective-permute-start.1 = (bf16[512,256]{1,0:T(8,128)(2,1)S(1)}, bf16[512,256]{1,0:T(8,128)(2,1)S(1)}, u32[]{:S(2)}, u32[]{:S(2)}) collective-permute-start(bf16[512,256]{1,0:T(8,128)(2,1)S(1)} %get-tuple-element.24), channel_id=1, source_target_pairs={{0,1},{1,2},{2,3},{3,0},{4,5},{5,6},{6,7},{7,4},{8,9},{9,10},{10,1... | collective-permute-start | bytes 786440 | tf_op jit(solution)/shard_map/ppermute | solution.py:31
  12.5 7.7 %collective-permute-start.2 = (bf16[512,256]{1,0:T(8,128)(2,1)S(1)}, bf16[512,256]{1,0:T(8,128)(2,1)S(1)}, u32[]{:S(2)}, u32[]{:S(2)}) collective-permute-start(bf16[512,256]{1,0:T(8,128)(2,1)S(1)} %get-tuple-element.25), channel_id=1, source_target_pairs={{0,3},{1,0},{2,1},{3,2},{4,7},{5,4},{6,5},{7,6},{8,11},{9,8},{10,9... | collective-permute-start | bytes 786440 | tf_op jit(solution)/shard_map/ppermute | solution.py:31
  20.3 7.9 %collective-permute-start.5 = (bf16[512,256]{1,0:T(8,128)(2,1)S(1)}, bf16[512,256]{1,0:T(8,128)(2,1)S(1)}, u32[]{:S(2)}, u32[]{:S(2)}) collective-permute-start(bf16[512,256]{1,0:T(8,128)(2,1)S(1)} %add_convert_fusion.2.image), channel_id=1, source_target_pairs={{0,2},{1,3},{2,0},{3,1},{4,6},{5,7},{6,4},{7,5},{8,10},{9,11},{10,... | collective-permute-start | bytes 786440 | tf_op jit(solution)/shard_map/ppermute | solution.py:31
  22.4 13.3 %collective-permute-start.4 = (bf16[512,256]{1,0:T(8,128)(2,1)S(1)}, bf16[512,256]{1,0:T(8,128)(2,1)S(1)}, u32[]{:S(2)}, u32[]{:S(2)}) collective-permute-start(bf16[512,256]{1,0:T(8,128)(2,1)S(1)} %add_convert_fusion.2.image), channel_id=1, source_target_pairs={{0,1},{1,2},{2,3},{3,0},{4,5},{5,6},{6,7},{7,4},{8,9},{9,10},{10,1... | collective-permute-start | bytes 786440 | tf_op jit(solution)/shard_map/ppermute | solution.py:31
  23.4 12.3 %collective-permute-start.3 = (bf16[512,256]{1,0:T(8,128)(2,1)S(1)}, bf16[512,256]{1,0:T(8,128)(2,1)S(1)}, u32[]{:S(2)}, u32[]{:S(2)}) collective-permute-start(bf16[512,256]{1,0:T(8,128)(2,1)S(1)} %add_convert_fusion.2.image), channel_id=1, source_target_pairs={{0,3},{1,0},{2,1},{3,2},{4,7},{5,4},{6,5},{7,6},{8,11},{9,8},{10,9... | collective-permute-start | bytes 786440 | tf_op jit(solution)/shard_map/ppermute | solution.py:31
  37.2 2.2 %collective-permute-start.6 = (bf16[256,1024]{1,0:T(8,128)(2,1)S(1)}, bf16[256,1024]{1,0:T(8,128)(2,1)S(1)}, u32[]{:S(2)}, u32[]{:S(2)}) collective-permute-start(bf16[256,1024]{1,0:T(8,128)(2,1)S(1)} %shard_map.45), channel_id=1, source_target_pairs={{0,4},{4,0},{8,12},{12,8},{16,20},{20,16},{24,28},{28,24},{32,36},... | collective-permute-start | bytes 1572872 | tf_op jit(solution)/shard_map/ppermute | solution.py:35
  87.9 5.4 %collective-permute-start.7 = (bf16[256,1024]{1,0:T(8,128)(2,1)S(1)}, bf16[256,1024]{1,0:T(8,128)(2,1)S(1)}, u32[]{:S(2)}, u32[]{:S(2)}) collective-permute-start(bf16[256,1024]{1,0:T(8,128)(2,1)S(1)} %bitcast.18), channel_id=1, source_target_pairs={{0,4},{4,0},{8,12},{12,8},{16,20},{20,16},{24,28},{28,24},{32,36},... | collective-permute-start | bytes 1572872 | tf_op jit(solution)/shard_map/ppermute | solution.py:35
  95.1 9.5 %collective-permute-start.8 = (bf16[512,256]{1,0:T(8,128)(2,1)S(1)}, bf16[512,256]{1,0:T(8,128)(2,1)S(1)}, u32[]{:S(2)}, u32[]{:S(2)}) collective-permute-start(bf16[512,256]{1,0:T(8,128)(2,1)S(1)} %get-tuple-element.35), channel_id=1, source_target_pairs={{0,2},{1,3},{2,0},{3,1},{4,6},{5,7},{6,4},{7,5},{8,10},{9,11},{10,... | collective-permute-start | bytes 786440 | tf_op jit(solution)/shard_map/ppermute | solution.py:31
  97.2 13.4 %collective-permute-start.9 = (bf16[512,256]{1,0:T(8,128)(2,1)S(1)}, bf16[512,256]{1,0:T(8,128)(2,1)S(1)}, u32[]{:S(2)}, u32[]{:S(2)}) collective-permute-start(bf16[512,256]{1,0:T(8,128)(2,1)S(1)} %get-tuple-element.36), channel_id=1, source_target_pairs={{0,1},{1,2},{2,3},{3,0},{4,5},{5,6},{6,7},{7,4},{8,9},{9,10},{10,1... | collective-permute-start | bytes 786440 | tf_op jit(solution)/shard_map/ppermute | solution.py:31
  97.5 13.1 %collective-permute-start.10 = (bf16[512,256]{1,0:T(8,128)(2,1)S(1)}, bf16[512,256]{1,0:T(8,128)(2,1)S(1)}, u32[]{:S(2)}, u32[]{:S(2)}) collective-permute-start(bf16[512,256]{1,0:T(8,128)(2,1)S(1)} %get-tuple-element.37), channel_id=1, source_target_pairs={{0,3},{1,0},{2,1},{3,2},{4,7},{5,4},{6,5},{7,6},{8,11},{9,8},{10,9... | collective-permute-start | bytes 786440 | tf_op jit(solution)/shard_map/ppermute | solution.py:31
  110.7 9.0 %collective-permute-start.13 = (bf16[512,256]{1,0:T(8,128)(2,1)S(1)}, bf16[512,256]{1,0:T(8,128)(2,1)S(1)}, u32[]{:S(2)}, u32[]{:S(2)}) collective-permute-start(bf16[512,256]{1,0:T(8,128)(2,1)S(1)} %get-tuple-element.40.image.one), channel_id=1, source_target_pairs={{0,2},{1,3},{2,0},{3,1},{4,6},{5,7},{6,4},{7,5},{8,10},{9,11},{10,... | collective-permute-start | bytes 786440 | tf_op jit(solution)/shard_map/ppermute | solution.py:31
  112.3 13.8 %collective-permute-start.12 = (bf16[512,256]{1,0:T(8,128)(2,1)S(1)}, bf16[512,256]{1,0:T(8,128)(2,1)S(1)}, u32[]{:S(2)}, u32[]{:S(2)}) collective-permute-start(bf16[512,256]{1,0:T(8,128)(2,1)S(1)} %get-tuple-element.40.image.one), channel_id=1, source_target_pairs={{0,1},{1,2},{2,3},{3,0},{4,5},{5,6},{6,7},{7,4},{8,9},{9,10},{10,1... | collective-permute-start | bytes 786440 | tf_op jit(solution)/shard_map/ppermute | solution.py:31
  113.0 13.1 %collective-permute-start.11 = (bf16[512,256]{1,0:T(8,128)(2,1)S(1)}, bf16[512,256]{1,0:T(8,128)(2,1)S(1)}, u32[]{:S(2)}, u32[]{:S(2)}) collective-permute-start(bf16[512,256]{1,0:T(8,128)(2,1)S(1)} %get-tuple-element.40.image.one), channel_id=1, source_target_pairs={{0,3},{1,0},{2,1},{3,2},{4,7},{5,4},{6,5},{7,6},{8,11},{9,8},{10,9... | collective-permute-start | bytes 786440 | tf_op jit(solution)/shard_map/ppermute | solution.py:31
  127.7 3.3 %collective-permute-start.14 = (bf16[256,1024]{1,0:T(8,128)(2,1)S(1)}, bf16[256,1024]{1,0:T(8,128)(2,1)S(1)}, u32[]{:S(2)}, u32[]{:S(2)}) collective-permute-start(bf16[256,1024]{1,0:T(8,128)(2,1)S(1)} %shard_map.51), channel_id=1, source_target_pairs={{0,4},{4,0},{8,12},{12,8},{16,20},{20,16},{24,28},{28,24},{32,36},... | collective-permute-start | bytes 1572872 | tf_op jit(solution)/shard_map/ppermute | solution.py:35
  129.3 1.7 collective-permute-start.15
  177.1 4.7 %collective-permute-start.16 = (bf16[256,256]{1,0:T(8,128)(2,1)S(1)}, bf16[256,256]{1,0:T(8,128)(2,1)S(1)}, u32[]{:S(2)}, u32[]{:S(2)}) collective-permute-start(bf16[256,256]{1,0:T(8,128)(2,1)S(1)} %slice.8), channel_id=1, source_target_pairs={{0,4},{4,0},{8,12},{12,8},{16,20},{20,16},{24,28},{28,24},{32,36},... | collective-permute-start | bytes 393224 | tf_op jit(solution)/shard_map/ppermute | solution.py:35
  180.9 11.1 %collective-permute-start.17 = (bf16[256,1024]{1,0:T(8,128)(2,1)S(1)}, bf16[256,1024]{1,0:T(8,128)(2,1)S(1)}, u32[]{:S(2)}, u32[]{:S(2)}) collective-permute-start(bf16[256,1024]{1,0:T(8,128)(2,1)S(1)} %slice.9), channel_id=1, source_target_pairs={{0,4},{4,0},{8,12},{12,8},{16,20},{20,16},{24,28},{28,24},{32,36},... | collective-permute-start | bytes 1572872 | tf_op jit(solution)/shard_map/ppermute | solution.py:35

commit v4 on v3

--- a/solution.py
+++ b/solution.py
@@ -29,6 +29,18 @@
 
 def from_y(value, k):
     return lax.ppermute(value, "cols", Y_SHIFT[k])
+
+
+def from_x(value, k):
+    to = [(row_index(z, x, c), row_index(z, (x + k) % NX, c)) for z in range(NZ) for x in range(NX) for c in range(NC)]
+    return lax.ppermute(value, "rows", to)
+
+
+COLUMNS = [[row_index(z, x, c) for z in range(NZ)] for x in range(NX) for c in range(NC)]
+
+
+def exchange_z(value):
+    return lax.all_to_all(value, "rows", 0, 0, tiled=True, axis_index_groups=COLUMNS)
 
 
 def from_core(value):
@@ -190,7 +202,7 @@
     total = back_own(kept[0], images[0])
     rest = (place, total, (kept[1], kept[3], kept[2]), (images[1], images[3], images[2]))
     other = from_core(back_half(*rest, 1, BF16))
-    return (back_half(*rest, 0, F32) + other.astype(F32)).astype(BF16)
+    return back_half(*rest, 0, F32), other
 
 
 def gram_kernel(place, one, two, three, four, mine, other, total):
@@ -198,15 +210,15 @@
         value = image[...]
         part = lax.dot_general(value, value, FIRST, preferred_element_type=F32)
         total[...] = part if i == 0 else total[...] + part
-    half = mine.shape[1]
-    first = place[1] == 0
-    mine[...] = jnp.where(first, total[:, :half], total[:, half:])
-    other[...] = jnp.where(first, total[:, half:], total[:, :half])
+    m, half = mine.shape
+    rows = pl.ds(pl.multiple_of(place[0] * m, m), m)
+    mine[...] = total[rows, pl.ds(pl.multiple_of(place[1] * half, half), half)]
+    other[...] = total[rows, pl.ds(pl.multiple_of((1 - place[1]) * half, half), half)]
 
 
 def gram_part(place, images):
     m, rank = images[0].shape
-    shape = jax.ShapeDtypeStruct((rank, rank // NC), F32)
+    shape = jax.ShapeDtypeStruct((rank // NY, rank // NC), F32)
     return pl.pallas_call(
         gram_kernel,
         in_specs=[SMEM] + [VMEM] * NY,
@@ -274,13 +286,14 @@
     return lax.dot_general(a, b, dims, precision=EXACT, preferred_element_type=F32)
 
 
-def inverse_kernel(scale, start, place, gathered, swapped, out, gram, m):
+def inverse_kernel(scale, place, own, swapped, out, gram, m):
     n = out.shape[0]
-    half = n // NC
-    for at, source, first in ((place[1], gathered, start), (1 - place[1], swapped, 0)):
-        high = source[:, first : first + half].astype(F32)
-        low = source[:, first + half : first + n].astype(F32)
-        gram[:, pl.ds(pl.multiple_of(at * half, half), half)] = (high + low) * scale
+    half, quarter = n // NC, n // NY
+    for at, source in ((place[1], own), (1 - place[1], swapped)):
+        for k in range(NY):
+            rows = pl.ds(pl.multiple_of(lax.rem(place[0] + k, NY) * quarter, quarter), quarter)
+            value = source[k * quarter : (k + 1) * quarter, :] * scale
+            gram[rows, pl.ds(pl.multiple_of(at * half, half), half)] = value
     m[:, :half] = gram[:half, :half]
     invert_block(m)
     one = m[:, half:]
@@ -294,17 +307,17 @@
     out[half:, half:] = two
 
 
-def factor_inverse(place, gathered, start, swapped, scale):
-    n = gathered.shape[0]
-    return pl.pallas_call(
-        functools.partial(inverse_kernel, scale, start),
+def factor_inverse(place, own, swapped, scale):
+    n = own.shape[0]
+    return pl.pallas_call(
+        functools.partial(inverse_kernel, scale),
         in_specs=[SMEM, VMEM, VMEM],
         out_specs=VMEM,
         out_shape=jax.ShapeDtypeStruct((n, n), F32),
         scratch_shapes=[pltpu.VMEM((n, n), F32), pltpu.VMEM((n // 2, n), F32)],
         compiler_params=PRODUCT,
-        cost_estimate=pl.CostEstimate(flops=10**10, bytes_accessed=2**20, transcendentals=0),
-    )(place, gathered, swapped)
+        cost_estimate=pl.CostEstimate(flops=10**9, bytes_accessed=2**20, transcendentals=0),
+    )(place, own, swapped)
 
 
 def halves_product(a, b, dims):
@@ -371,26 +384,28 @@
     return mine, on, far, behind
 
 
-def spread_kernel(gram_at, got, out):
-    rows = 2 * out.shape[0] // PLANE
+def piece_sum(got, width):
     total = None
-    for at in range(0, got.shape[0], rows):
-        pair = got[at : at + rows, :].astype(F32)
-        pair = pair[: rows // 2] + pair[rows // 2 :]
+    for at in range(0, got.shape[0], 16):
+        pair = got[at : at + 16, :width].astype(F32)
+        pair = pair[:8] + pair[8:]
         total = pair if total is None else total + pair
-    mine = total.astype(BF16)
-    if gram_at:
-        columns = (total.shape[1] - gram_at) // 2
-        gram = total[:, gram_at : gram_at + columns] + total[:, gram_at + columns :]
-        mine = jnp.concatenate([total[:, :gram_at].astype(BF16), *split(gram)], axis=1)
-    pair = jnp.concatenate([mine, mine], axis=0)
-    for at in range(0, got.shape[0], rows):
-        out[at : at + rows, :] = pair
-
-
-def all_sum_over_plane(value, gram_at=0):
+    return total
+
+
+def spread_to(out, value):
+    pair = jnp.concatenate([value, value], axis=0)
+    for at in range(0, out.shape[0], 16):
+        out[at : at + 16, :] = pair
+
+
+def spread_kernel(got, out):
+    spread_to(out, piece_sum(got, out.shape[1]).astype(BF16))
+
+
+def all_sum_over_plane(value):
     spread = pl.pallas_call(
-        functools.partial(spread_kernel, gram_at),
+        spread_kernel,
         in_specs=[VMEM],
         out_specs=VMEM,
         out_shape=jax.ShapeDtypeStruct(value.shape, BF16),
@@ -399,6 +414,85 @@
     return exchange(spread)
 
 
+def cut_kernel(place, mine, other, gram, own, one, two, three, total):
+    total[...] = mine[...] + other[...].astype(F32)
+    width = total.shape[1]
+    high, low = split(gram[...])
+    own[:, width:] = high.astype(F32) + low.astype(F32)
+    for out in (one, two, three):
+        out[:, width:] = jnp.concatenate([high, low], axis=1)
+    for k, out in enumerate((own, one, two, three)):
+        x = lax.rem(place[2] + k, NX)
+        for z in range(0, NZ, 2):
+            blocks = [
+                total[pl.ds(pl.multiple_of(8 * (NX * (z + i) + x), 8), 8), :] for i in range(2)
+            ]
+            out[8 * z : 8 * z + 16, :width] = jnp.concatenate(blocks, axis=0).astype(out.dtype)
+
+
+def cut(place, mine, other, gram):
+    rows, width = mine.shape
+    m, size = gram.shape
+    return pl.pallas_call(
+        cut_kernel,
+        in_specs=[SMEM] + [VMEM] * 3,
+        out_specs=[VMEM] * NX,
+        out_shape=[jax.ShapeDtypeStruct((m, width + size), F32)]
+        + [jax.ShapeDtypeStruct((m, width + 2 * size), BF16)] * (NX - 1),
+        scratch_shapes=[pltpu.VMEM((rows, width), F32)],
+        compiler_params=PRODUCT,
+    )(place, mine, other, gram)
+
+
+def pack_kernel(width, own, one, two, three, out):
+    size = own.shape[1] - width
+    pieces = [piece[...].astype(F32) for piece in (one, two, three)]
+    total = own[:, :width] + pieces[0][:, :width] + pieces[1][:, :width] + pieces[2][:, :width]
+    out[:, :width] = total.astype(BF16)
+    grams = [piece[:, width : width + size] + piece[:, width + size :] for piece in pieces]
+    gram = (own[:, width:] + grams[1]) + (grams[0] + grams[2])
+    flat = jnp.concatenate([gram[8 * i : 8 * i + 8] for i in range(gram.shape[0] // 8)], axis=1)
+    flat = jnp.concatenate(split(flat), axis=1)
+    flat = jnp.concatenate([flat, flat], axis=0)
+    for at in range(0, out.shape[0], 16):
+        out[at : at + 16, width:] = flat
+
+
+def pack(width, own, *pieces):
+    rows = own.shape[0]
+    size = own.shape[1] - width
+    return pl.pallas_call(
+        functools.partial(pack_kernel, width),
+        in_specs=[VMEM] * NX,
+        out_specs=VMEM,
+        out_shape=jax.ShapeDtypeStruct((rows, width + 2 * rows // 8 * size), BF16),
+        compiler_params=PRODUCT,
+    )(own, *pieces)
+
+
+def unpack_kernel(got, out, gram):
+    width, size = out.shape[1], gram.shape[1]
+    total = piece_sum(got, got.shape[1])
+    spread_to(out, total[:, :width].astype(BF16))
+    count = gram.shape[0] // 8
+    flat = total[:, width : width + count * size] + total[:, width + count * size :]
+    for i in range(count):
+        gram[8 * i : 8 * i + 8, :] = flat[:, i * size : (i + 1) * size]
+
+
+def unpack(got, width, shape):
+    return pl.pallas_call(
+        unpack_kernel,
+        in_specs=[VMEM],
+        out_specs=[VMEM] * 2,
+        out_shape=[
+            jax.ShapeDtypeStruct((8 * PLANE, width), BF16),
+            jax.ShapeDtypeStruct(shape, F32),
+        ],
+        compiler_params=PRODUCT,
+    )(got)
+
+
 def split(value):
     high = value.astype(BF16)
     return high, (value - high.astype(F32)).astype(BF16)
@@ -406,23 +500,28 @@
 
 def per_device(activations, sketch):
     token_count = activations.shape[0] * lax.axis_size("rows")
-    place = jnp.stack([lax.axis_index("cols"), lax.axis_index("rows") % NC]).astype(jnp.int32)
+    row = lax.axis_index("rows")
+    place = jnp.stack([lax.axis_index("cols"), row % NC, row // NC % NX]).astype(jnp.int32)
 
     pieces, kept = load_forward(place, activations, sketch)
     image = sum_over_y(*pieces).astype(BF16)
-    back_image = all_sum_over_plane(back(place, kept, gather_over_y(image)))
+    mine, other = back(place, kept, gather_over_y(image))
+    back_image = all_sum_over_plane((mine + other.astype(F32)).astype(BF16))
 
     power = sum_over_y(*forward(place, kept, back_image))
     images = gather_over_y(power.astype(BF16))
-    wide = back(place, kept, images)
-    mine, other = gram_part(place, images)
-    gram = mine + from_core(other)
-    half = wide.shape[1]
-    gathered = all_sum_over_plane(jnp.concatenate([wide, *split(gram)], axis=1), half)
-    swapped = from_core(gathered[:, half:])
-    inverse = factor_inverse(place, gathered, half, swapped, 1.0 / token_count)
-    other = from_core(gathered[:, :half])
-    return last(place, inverse, power, gathered, other, 1.0 / math.sqrt(token_count))
+    mine, other = back(place, kept, images)
+    gram, gram_other = gram_part(place, images)
+    gram = gram + from_core(gram_other)
+    own, one, two, three = cut(place, mine, other, gram)
+    half = mine.shape[1]
+    packed = pack(half, own, from_x(one, 1), from_x(two, 2), from_x(three, 3))
+    wide, gram = unpack(exchange_z(packed), half, gram.shape)
+    wide = exchange(wide)
+    gram = jnp.concatenate([gram, from_y(gram, 3), from_y(gram, 2), from_y(gram, 1)], axis=0)
+    inverse = factor_inverse(place, gram, from_core(gram), 1.0 / token_count)
+    wide, inverse = lax.optimization_barrier((wide, inverse))
+    return last(place, inverse, power, wide, from_core(wide), 1.0 / math.sqrt(token_count))
 
 
 def solution(mesh):

time: 195 us -> 191 us (0.979)
  blocking collectives: 93.9 us -> 63.1 us
  starting transfers between devices: 29.3 us -> 44.4 us
  waiting for transfers between devices: 37 us -> 47.1 us
    all_to_all x4 -> x2, blocking collectives: 93.9 us -> 48.2 us  [exchange(): lax.all_to_all(value, 'rows', 0, 0, tiled=True, axis_index_groups=PLANES)]
    all_to_all x0 -> x1, blocking collectives: none -> 14.9 us  [exchange_z(): lax.all_to_all(value, 'rows', 0, 0, tiled=True, axis_index_groups=COLUMNS)]
    all_to_all x0 -> x1, starting transfers between devices: none -> 7.6 us  [exchange(): lax.all_to_all(value, 'rows', 0, 0, tiled=True, axis_index_groups=PLANES)]
    ppermute x0 -> x3, waiting for transfers between devices: none -> 6.24 us  [from_x(): return lax.ppermute(value, 'rows', to)]
    ppermute x0 -> x3, starting transfers between devices: none -> 4.15 us  [from_x(): return lax.ppermute(value, 'rows', to)]
    ppermute x12 -> x15, starting transfers between devices: 20.3 us -> 24.4 us  [from_y(): return lax.ppermute(value, 'cols', Y_SHIFT[k])]
    ppermute x12 -> x15, waiting for transfers between devices: 36.4 us -> 38.3 us  [from_y(): return lax.ppermute(value, 'cols', Y_SHIFT[k])]
    pallas_call x3 -> x5, Pallas kernels: 10.4 us -> 12 us  [the longest x1 10.2 us: factor_inverse(): pl.pallas_call(functools.partial(inverse_kernel, scale), in_specs=[SMEM,...]
  transfers between devices with their start and end apart: 18 -> 25, of which waited for: 8 -> 13; matrix products, arithmetic and copies ran while one was open for 0% -> 0% of each run, Pallas kernels for 11% -> 11%
where the time goes in v4:
time: 191 us; the launch traced here: 190 us
  blocking collectives  63.1 us (33%)
  waiting for transfers between devices  47.1 us (25%)
  starting transfers between devices  44.4 us (23%)
  Pallas kernels  34.4 us (18%)
    all_to_all x2, blocking collectives, exchange(): lax.all_to_all(value, 'rows', 0, 0, tiled=True, axis_index_groups=PLANES)  48.2 us
    ppermute x15, waiting for transfers between devices, from_y(): return lax.ppermute(value, 'cols', Y_SHIFT[k])  38.3 us
    ppermute x15, starting transfers between devices, from_y(): return lax.ppermute(value, 'cols', Y_SHIFT[k])  24.4 us
    all_to_all x1, blocking collectives, exchange_z(): lax.all_to_all(value, 'rows', 0, 0, tiled=True, axis_index_groups=COLUMNS)  14.9 us
    pallas_call x1, Pallas kernels, factor_inverse(): pl.pallas_call(functools.partial(inverse_kernel, scale), in_specs=[SMEM,...  10.2 us
    ppermute x6, starting transfers between devices, from_core(): return lax.ppermute(value, 'rows', CORE_SWAP)  8.17 us
    all_to_all x1, starting transfers between devices, exchange(): lax.all_to_all(value, 'rows', 0, 0, tiled=True, axis_index_groups=PLANES)  7.6 us
    pallas_call x2, Pallas kernels, load_part(): pl.pallas_call(functools.partial(load_kernel, quarters, keep_right), in_s...  7.5 us
  transfers between devices with their start and end apart: 25, of which 13 were waited for; matrix products, arithmetic and copies ran while one was open for 0% of the time, Pallas kernels for 11%

profile of v4, /device:TPU:1, one launch (start us, length us, event | category | flops | bytes accessed | tf_op | source)
XLA Modules:
  0.0 190.5 jit_solution(276442695578379438)
XLA Ops:
  0.7 3.9 %shard_map.41 = (bf16[512,256]{1,0:T(8,128)(2,1)S(1)}, bf16[512,256]{1,0:T(8,128)(2,1)S(1)}, bf16[512,2048]{1,0:T(8,128)(2,1)S(1)}, bf16[512,2048]{1,0:T(8,128)(2,1)S(1)}, bf16[2048,256]{1,0:T(8,128)(2,1)S(1)}) custom-call(s32[3]{0:T(128)S(1)} %pad_add_fusion.place, bf16[2048,2048]{1,0:T(8,128)(2,1)} %a.3, bf16[2048,256]{1,0:T(8,128)(2,1)} %right.1), custom_call_target="tpu_custom_call" | custom-call | flops 1073741824 | bytes 4194304 | tf_op jit(solution)/shard_map/pallas_call | solution.py:100
  4.7 3.8 %collective-permute-start = (bf16[512,256]{1,0:T(8,128)(2,1)S(1)}, bf16[512,256]{1,0:T(8,128)(2,1)S(1)}, u32[]{:S(2)}, u32[]{:S(2)}) collective-permute-start(bf16[512,256]{1,0:T(8,128)(2,1)S(1)} %get-tuple-element.31), channel_id=1, source_target_pairs={{0,2},{1,3},{2,0},{3,1},{4,6},{5,7},{6,4},{7,5},{8,10},{9,11},{10,... | collective-permute-start | bytes 786440 | tf_op jit(solution)/shard_map/ppermute | solution.py:31
  8.9 3.6 %shard_map.42 = (bf16[512,256]{1,0:T(8,128)(2,1)S(1)}, f32[512,256]{1,0:T(8,128)S(1)}, bf16[512,2048]{1,0:T(8,128)(2,1)S(1)}, bf16[512,2048]{1,0:T(8,128)(2,1)S(1)}) custom-call(s32[3]{0:T(128)S(1)} %pad_add_fusion.place, bf16[2048,2048]{1,0:T(8,128)(2,1)} %a.3, bf16[2048,256]{1,0:T(8,128)(2,1)S(1)} %get-tuple-element.29.right), custom_call_target="tpu_custom_call" | custom-call | flops 1073741824 | bytes 4194304 | tf_op jit(solution)/shard_map/pallas_call | solution.py:100
  12.5 2.4 %collective-permute-start.2 = (bf16[512,256]{1,0:T(8,128)(2,1)S(1)}, bf16[512,256]{1,0:T(8,128)(2,1)S(1)}, u32[]{:S(2)}, u32[]{:S(2)}) collective-permute-start(bf16[512,256]{1,0:T(8,128)(2,1)S(1)} %get-tuple-element.33), channel_id=1, source_target_pairs={{0,3},{1,0},{2,1},{3,2},{4,7},{5,4},{6,5},{7,6},{8,11},{9,8},{10,9... | collective-permute-start | bytes 786440 | tf_op jit(solution)/shard_map/ppermute | solution.py:31
  14.8 5.4 %collective-permute-done.1 = bf16[512,256]{1,0:T(8,128)(2,1)S(1)} collective-permute-done((bf16[512,256]{1,0:T(8,128)(2,1)S(1)}, bf16[512,256]{1,0:T(8,128)(2,1)S(1)}, u32[]{:S(2)}, u32[]{:S(2)}) %collective-permute-start.1) | collective-permute-done | bytes 262176 | tf_op jit(solution)/shard_map/ppermute | solution.py:31
  20.3 2.1 %collective-permute-start.5 = (bf16[512,256]{1,0:T(8,128)(2,1)S(1)}, bf16[512,256]{1,0:T(8,128)(2,1)S(1)}, u32[]{:S(2)}, u32[]{:S(2)}) collective-permute-start(bf16[512,256]{1,0:T(8,128)(2,1)S(1)} %add_convert_fusion.1.image), channel_id=1, source_target_pairs={{0,2},{1,3},{2,0},{3,1},{4,6},{5,7},{6,4},{7,5},{8,10},{9,11},{10,... | collective-permute-start | bytes 786440 | tf_op jit(solution)/shard_map/ppermute | solution.py:31
  23.4 1.7 collective-permute-start.3
  25.8 2.3 %collective-permute-done.5.refs_5_ = bf16[512,256]{1,0:T(8,128)(2,1)S(1)} collective-permute-done((bf16[512,256]{1,0:T(8,128)(2,1)S(1)}, bf16[512,256]{1,0:T(8,128)(2,1)S(1)}, u32[]{:S(2)}, u32[]{:S(2)}) %collective-permute-start.5) | collective-permute-done | bytes 262176 | tf_op jit(solution)/shard_map/ppermute | solution.py:31
  28.2 7.5 %collective-permute-done.4.refs_4_ = bf16[512,256]{1,0:T(8,128)(2,1)S(1)} collective-permute-done((bf16[512,256]{1,0:T(8,128)(2,1)S(1)}, bf16[512,256]{1,0:T(8,128)(2,1)S(1)}, u32[]{:S(2)}, u32[]{:S(2)}) %collective-permute-start.4) | collective-permute-done | bytes 262176 | tf_op jit(solution)/shard_map/ppermute | solution.py:31
  39.6 28.1 %all_to_all.45 = bf16[32,8,1024]{2,1,0:T(8,128)(2,1)S(1)} all-to-all(bf16[32,8,1024]{2,1,0:T(8,128)(2,1)S(1)} %fusion), channel_id=1, replica_groups={{0,8,16,24,32,40,48,56,64,72,80,88,96,104,112,120,128,136,144,152,160,1..., dimensions={0} | all-to-all | bytes 1048576 | tf_op jit(solution)/shard_map/all_to_all | solution.py:51
  67.9 20.1 %all_to_all.46 = bf16[32,8,1024]{2,1,0:T(8,128)(2,1)S(1)} all-to-all(bf16[32,8,1024]{2,1,0:T(8,128)(2,1)S(1)} %bitcast.15), channel_id=1, replica_groups={{0,8,16,24,32,40,48,56,64,72,80,88,96,104,112,120,128,136,144,152,160,1..., dimensions={0} | all-to-all | bytes 1048576 | tf_op jit(solution)/shard_map/all_to_all | solution.py:51
  87.9 3.6 %collective-permute-start.7 = (bf16[256,1024]{1,0:T(8,128)(2,1)S(1)}, bf16[256,1024]{1,0:T(8,128)(2,1)S(1)}, u32[]{:S(2)}, u32[]{:S(2)}) collective-permute-start(bf16[256,1024]{1,0:T(8,128)(2,1)S(1)} %bitcast.12), channel_id=1, source_target_pairs={{0,4},{4,0},{8,12},{12,8},{16,20},{20,16},{24,28},{28,24},{32,36},... | collective-permute-start | bytes 1572872 | tf_op jit(solution)/shard_map/ppermute | solution.py:47
  91.5 1.8 shard_map.47
  93.4 1.8 shard_map.48
  95.2 2.0 %collective-permute-start.8 = (bf16[512,256]{1,0:T(8,128)(2,1)S(1)}, bf16[512,256]{1,0:T(8,128)(2,1)S(1)}, u32[]{:S(2)}, u32[]{:S(2)}) collective-permute-start(bf16[512,256]{1,0:T(8,128)(2,1)S(1)} %get-tuple-element.43), channel_id=1, source_target_pairs={{0,2},{1,3},{2,0},{3,1},{4,6},{5,7},{6,4},{7,5},{8,10},{9,11},{10,... | collective-permute-start | bytes 786440 | tf_op jit(solution)/shard_map/ppermute | solution.py:31
  97.5 2.4 %collective-permute-start.10 = (bf16[512,256]{1,0:T(8,128)(2,1)S(1)}, bf16[512,256]{1,0:T(8,128)(2,1)S(1)}, u32[]{:S(2)}, u32[]{:S(2)}) collective-permute-start(bf16[512,256]{1,0:T(8,128)(2,1)S(1)} %get-tuple-element.45), channel_id=1, source_target_pairs={{0,3},{1,0},{2,1},{3,2},{4,7},{5,4},{6,5},{7,6},{8,11},{9,8},{10,9... | collective-permute-start | bytes 786440 | tf_op jit(solution)/shard_map/ppermute | solution.py:31
  99.9 4.8 %collective-permute-done.8 = bf16[512,256]{1,0:T(8,128)(2,1)S(1)} collective-permute-done((bf16[512,256]{1,0:T(8,128)(2,1)S(1)}, bf16[512,256]{1,0:T(8,128)(2,1)S(1)}, u32[]{:S(2)}, u32[]{:S(2)}) %collective-permute-start.8) | collective-permute-done | bytes 262176 | tf_op jit(solution)/shard_map/ppermute | solution.py:31
  104.7 6.0 %collective-permute-done.9 = bf16[512,256]{1,0:T(8,128)(2,1)S(1)} collective-permute-done((bf16[512,256]{1,0:T(8,128)(2,1)S(1)}, bf16[512,256]{1,0:T(8,128)(2,1)S(1)}, u32[]{:S(2)}, u32[]{:S(2)}) %collective-permute-start.9) | collective-permute-done | bytes 262176 | tf_op jit(solution)/shard_map/ppermute | solution.py:31
  110.8 1.6 collective-permute-start.13
  113.1 2.0 %collective-permute-start.11 = (bf16[512,256]{1,0:T(8,128)(2,1)S(1)}, bf16[512,256]{1,0:T(8,128)(2,1)S(1)}, u32[]{:S(2)}, u32[]{:S(2)}) collective-permute-start(bf16[512,256]{1,0:T(8,128)(2,1)S(1)} %get-tuple-element.56.image.one), channel_id=1, source_target_pairs={{0,3},{1,0},{2,1},{3,2},{4,7},{5,4},{6,5},{7,6},{8,11},{9,8},{10,9... | collective-permute-start | bytes 786440 | tf_op jit(solution)/shard_map/ppermute | solution.py:31
  115.8 4.0 %collective-permute-done.13.refs_5_.three = bf16[512,256]{1,0:T(8,128)(2,1)S(1)} collective-permute-done((bf16[512,256]{1,0:T(8,128)(2,1)S(1)}, bf16[512,256]{1,0:T(8,128)(2,1)S(1)}, u32[]{:S(2)}, u32[]{:S(2)}) %collective-permute-start.13) | collective-permute-done | bytes 262176 | tf_op jit(solution)/shard_map/ppermute | solution.py:31
  119.8 6.4 %collective-permute-done.12.refs_4_.four = bf16[512,256]{1,0:T(8,128)(2,1)S(1)} collective-permute-done((bf16[512,256]{1,0:T(8,128)(2,1)S(1)}, bf16[512,256]{1,0:T(8,128)(2,1)S(1)}, u32[]{:S(2)}, u32[]{:S(2)}) %collective-permute-start.12) | collective-permute-done | bytes 262176 | tf_op jit(solution)/shard_map/ppermute | solution.py:31
  132.4 2.4 %collective-permute-start.17 = (bf16[64,1280]{1,0:T(8,128)(2,1)S(1)}, bf16[64,1280]{1,0:T(8,128)(2,1)S(1)}, u32[]{:S(2)}, u32[]{:S(2)}) collective-permute-start(bf16[64,1280]{1,0:T(8,128)(2,1)S(1)} %get-tuple-element.50), channel_id=1, source_target_pairs={{0,16},{4,20},{8,24},{12,28},{16,0},{20,4},{24,8},{28,12},{32,48},... | collective-permute-start | bytes 491528 | tf_op jit(solution)/shard_map/ppermute | solution.py:36
  136.0 2.4 %collective-permute-done.16.one = bf16[64,1280]{1,0:T(8,128)(2,1)S(1)} collective-permute-done((bf16[64,1280]{1,0:T(8,128)(2,1)S(1)}, bf16[64,1280]{1,0:T(8,128)(2,1)S(1)}, u32[]{:S(2)}, u32[]{:S(2)}) %collective-permute-start.16) | collective-permute-done | bytes 163872 | tf_op jit(solution)/shard_map/ppermute | solution.py:36
  138.4 3.7 %collective-permute-done.17.two = bf16[64,1280]{1,0:T(8,128)(2,1)S(1)} collective-permute-done((bf16[64,1280]{1,0:T(8,128)(2,1)S(1)}, bf16[64,1280]{1,0:T(8,128)(2,1)S(1)}, u32[]{:S(2)}, u32[]{:S(2)}) %collective-permute-start.17) | collective-permute-done | bytes 163872 | tf_op jit(solution)/shard_map/ppermute | solution.py:36
  142.3 14.9 %all_to_all.47 = bf16[8,8,3072]{2,1,0:T(8,128)(2,1)S(1)} all-to-all(bf16[8,8,3072]{2,1,0:T(8,128)(2,1)S(1)} %bitcast.19), channel_id=1, replica_groups={{0,32,64,96,128,160,192,224},{4,36,68,100,132,164,196,228},{8,40,72,104..., dimensions={0} | all-to-all | bytes 786432 | tf_op jit(solution)/shard_map/all_to_all | solution.py:43
  158.1 7.6 %all-to-all-start.3 = ((bf16[32,8,1024]{2,1,0:T(8,128)(2,1)}), bf16[32,8,1024]{2,1,0:T(8,128)(2,1)S(1)}, u32[]{:S(2)}, u32[]{:S(2)}) async-start(bf16[32,8,1024]{2,1,0:T(8,128)(2,1)} %bitcast.9), calls=%async_computation.3 | async-start | bytes 1048576 | tf_op jit(solution)/shard_map/all_to_all | solution.py:51
  167.1 1.5 collective-permute-start.20
  169.8 1.9 collective-permute-done.19
  171.7 2.8 %collective-permute-start.22 = (f32[256,128]{1,0:T(8,128)S(1)}, f32[256,128]{1,0:T(8,128)S(1)}, u32[]{:S(2)}, u32[]{:S(2)}) collective-permute-start(f32[256,128]{1,0:T(8,128)S(1)} %constant_dynamic-update-slice_fusion.own), channel_id=1, source_target_pairs={{0,4},{4,0},{8,12},{12,8},{16,20},{20,16},{24,28},{28,24},{32,36},... | collective-permute-start | bytes 393224 | tf_op jit(solution)/shard_map/ppermute | solution.py:47
  175.5 10.2 %shard_map.56.inverse = f32[256,256]{1,0:T(8,128)S(1)} custom-call(s32[3]{0:T(128)S(1)} %pad_add_fusion.place, f32[256,128]{1,0:T(8,128)S(1)} %constant_dynamic-update-slice_fusion.own, f32[256,128]{1,0:T(8,128)S(1)} %collective-permute-done.22.swapped), custom_call_target="tpu_custom_call" | custom-call | flops 1000000000 | bytes 1048576 | tf_op jit(solution)/shard_map/pallas_call | solution.py:312
  187.7 2.6 %shard_map.57 = (bf16[512,256]{1,0:T(8,128)(2,1)}, f32[256,2048]{1,0:T(8,128)}) custom-call(s32[3]{0:T(128)S(1)} %pad_add_fusion.place, f32[256,256]{1,0:T(8,128)S(1)} %shard_map.56.inverse, f32[512,256]{1,0:T(8,128)S(1)} %get-tuple-element.57.power, bf16[256,1024]{1,0:T(8,128)(2,1)S(1)} %bitcast.17, bf16[256,1024]{1,0:T(8,128)(2,1)S(1)} %collective-permute-done.23.other), custom_call_target="tpu_custom_call" | custom-call | tf_op jit(solution)/shard_map/pallas_call | solution.py:360
  (47 shorter events, 22.1 us)
Async XLA Ops:
  4.7 10.2 %collective-permute-start = (bf16[512,256]{1,0:T(8,128)(2,1)S(1)}, bf16[512,256]{1,0:T(8,128)(2,1)S(1)}, u32[]{:S(2)}, u32[]{:S(2)}) collective-permute-start(bf16[512,256]{1,0:T(8,128)(2,1)S(1)} %get-tuple-element.31), channel_id=1, source_target_pairs={{0,2},{1,3},{2,0},{3,1},{4,6},{5,7},{6,4},{7,5},{8,10},{9,11},{10,... | collective-permute-start | bytes 786440 | tf_op jit(solution)/shard_map/ppermute | solution.py:31
  8.5 11.7 %collective-permute-start.1 = (bf16[512,256]{1,0:T(8,128)(2,1)S(1)}, bf16[512,256]{1,0:T(8,128)(2,1)S(1)}, u32[]{:S(2)}, u32[]{:S(2)}) collective-permute-start(bf16[512,256]{1,0:T(8,128)(2,1)S(1)} %get-tuple-element.32), channel_id=1, source_target_pairs={{0,1},{1,2},{2,3},{3,0},{4,5},{5,6},{6,7},{7,4},{8,9},{9,10},{10,1... | collective-permute-start | bytes 786440 | tf_op jit(solution)/shard_map/ppermute | solution.py:31
  12.5 7.7 %collective-permute-start.2 = (bf16[512,256]{1,0:T(8,128)(2,1)S(1)}, bf16[512,256]{1,0:T(8,128)(2,1)S(1)}, u32[]{:S(2)}, u32[]{:S(2)}) collective-permute-start(bf16[512,256]{1,0:T(8,128)(2,1)S(1)} %get-tuple-element.33), channel_id=1, source_target_pairs={{0,3},{1,0},{2,1},{3,2},{4,7},{5,4},{6,5},{7,6},{8,11},{9,8},{10,9... | collective-permute-start | bytes 786440 | tf_op jit(solution)/shard_map/ppermute | solution.py:31
  20.3 7.9 %collective-permute-start.5 = (bf16[512,256]{1,0:T(8,128)(2,1)S(1)}, bf16[512,256]{1,0:T(8,128)(2,1)S(1)}, u32[]{:S(2)}, u32[]{:S(2)}) collective-permute-start(bf16[512,256]{1,0:T(8,128)(2,1)S(1)} %add_convert_fusion.1.image), channel_id=1, source_target_pairs={{0,2},{1,3},{2,0},{3,1},{4,6},{5,7},{6,4},{7,5},{8,10},{9,11},{10,... | collective-permute-start | bytes 786440 | tf_op jit(solution)/shard_map/ppermute | solution.py:31
  22.4 13.3 %collective-permute-start.4 = (bf16[512,256]{1,0:T(8,128)(2,1)S(1)}, bf16[512,256]{1,0:T(8,128)(2,1)S(1)}, u32[]{:S(2)}, u32[]{:S(2)}) collective-permute-start(bf16[512,256]{1,0:T(8,128)(2,1)S(1)} %add_convert_fusion.1.image), channel_id=1, source_target_pairs={{0,1},{1,2},{2,3},{3,0},{4,5},{5,6},{6,7},{7,4},{8,9},{9,10},{10,1... | collective-permute-start | bytes 786440 | tf_op jit(solution)/shard_map/ppermute | solution.py:31
  23.4 12.3 %collective-permute-start.3 = (bf16[512,256]{1,0:T(8,128)(2,1)S(1)}, bf16[512,256]{1,0:T(8,128)(2,1)S(1)}, u32[]{:S(2)}, u32[]{:S(2)}) collective-permute-start(bf16[512,256]{1,0:T(8,128)(2,1)S(1)} %add_convert_fusion.1.image), channel_id=1, source_target_pairs={{0,3},{1,0},{2,1},{3,2},{4,7},{5,4},{6,5},{7,6},{8,11},{9,8},{10,9... | collective-permute-start | bytes 786440 | tf_op jit(solution)/shard_map/ppermute | solution.py:31
  37.3 2.2 %collective-permute-start.6 = (bf16[256,1024]{1,0:T(8,128)(2,1)S(1)}, bf16[256,1024]{1,0:T(8,128)(2,1)S(1)}, u32[]{:S(2)}, u32[]{:S(2)}) collective-permute-start(bf16[256,1024]{1,0:T(8,128)(2,1)S(1)} %shard_map.45), channel_id=1, source_target_pairs={{0,4},{4,0},{8,12},{12,8},{16,20},{20,16},{24,28},{28,24},{32,36},... | collective-permute-start | bytes 1572872 | tf_op jit(solution)/shard_map/ppermute | solution.py:47
  87.9 5.4 %collective-permute-start.7 = (bf16[256,1024]{1,0:T(8,128)(2,1)S(1)}, bf16[256,1024]{1,0:T(8,128)(2,1)S(1)}, u32[]{:S(2)}, u32[]{:S(2)}) collective-permute-start(bf16[256,1024]{1,0:T(8,128)(2,1)S(1)} %bitcast.12), channel_id=1, source_target_pairs={{0,4},{4,0},{8,12},{12,8},{16,20},{20,16},{24,28},{28,24},{32,36},... | collective-permute-start | bytes 1572872 | tf_op jit(solution)/shard_map/ppermute | solution.py:47
  95.2 9.5 %collective-permute-start.8 = (bf16[512,256]{1,0:T(8,128)(2,1)S(1)}, bf16[512,256]{1,0:T(8,128)(2,1)S(1)}, u32[]{:S(2)}, u32[]{:S(2)}) collective-permute-start(bf16[512,256]{1,0:T(8,128)(2,1)S(1)} %get-tuple-element.43), channel_id=1, source_target_pairs={{0,2},{1,3},{2,0},{3,1},{4,6},{5,7},{6,4},{7,5},{8,10},{9,11},{10,... | collective-permute-start | bytes 786440 | tf_op jit(solution)/shard_map/ppermute | solution.py:31
  97.2 13.4 %collective-permute-start.9 = (bf16[512,256]{1,0:T(8,128)(2,1)S(1)}, bf16[512,256]{1,0:T(8,128)(2,1)S(1)}, u32[]{:S(2)}, u32[]{:S(2)}) collective-permute-start(bf16[512,256]{1,0:T(8,128)(2,1)S(1)} %get-tuple-element.44), channel_id=1, source_target_pairs={{0,1},{1,2},{2,3},{3,0},{4,5},{5,6},{6,7},{7,4},{8,9},{9,10},{10,1... | collective-permute-start | bytes 786440 | tf_op jit(solution)/shard_map/ppermute | solution.py:31
  97.5 13.1 %collective-permute-start.10 = (bf16[512,256]{1,0:T(8,128)(2,1)S(1)}, bf16[512,256]{1,0:T(8,128)(2,1)S(1)}, u32[]{:S(2)}, u32[]{:S(2)}) collective-permute-start(bf16[512,256]{1,0:T(8,128)(2,1)S(1)} %get-tuple-element.45), channel_id=1, source_target_pairs={{0,3},{1,0},{2,1},{3,2},{4,7},{5,4},{6,5},{7,6},{8,11},{9,8},{10,9... | collective-permute-start | bytes 786440 | tf_op jit(solution)/shard_map/ppermute | solution.py:31
  110.8 9.0 %collective-permute-start.13 = (bf16[512,256]{1,0:T(8,128)(2,1)S(1)}, bf16[512,256]{1,0:T(8,128)(2,1)S(1)}, u32[]{:S(2)}, u32[]{:S(2)}) collective-permute-start(bf16[512,256]{1,0:T(8,128)(2,1)S(1)} %get-tuple-element.56.image.one), channel_id=1, source_target_pairs={{0,2},{1,3},{2,0},{3,1},{4,6},{5,7},{6,4},{7,5},{8,10},{9,11},{10,... | collective-permute-start | bytes 786440 | tf_op jit(solution)/shard_map/ppermute | solution.py:31
  112.4 13.8 %collective-permute-start.12 = (bf16[512,256]{1,0:T(8,128)(2,1)S(1)}, bf16[512,256]{1,0:T(8,128)(2,1)S(1)}, u32[]{:S(2)}, u32[]{:S(2)}) collective-permute-start(bf16[512,256]{1,0:T(8,128)(2,1)S(1)} %get-tuple-element.56.image.one), channel_id=1, source_target_pairs={{0,1},{1,2},{2,3},{3,0},{4,5},{5,6},{6,7},{7,4},{8,9},{9,10},{10,1... | collective-permute-start | bytes 786440 | tf_op jit(solution)/shard_map/ppermute | solution.py:31
  113.1 13.1 %collective-permute-start.11 = (bf16[512,256]{1,0:T(8,128)(2,1)S(1)}, bf16[512,256]{1,0:T(8,128)(2,1)S(1)}, u32[]{:S(2)}, u32[]{:S(2)}) collective-permute-start(bf16[512,256]{1,0:T(8,128)(2,1)S(1)} %get-tuple-element.56.image.one), channel_id=1, source_target_pairs={{0,3},{1,0},{2,1},{3,2},{4,7},{5,4},{6,5},{7,6},{8,11},{9,8},{10,9... | collective-permute-start | bytes 786440 | tf_op jit(solution)/shard_map/ppermute | solution.py:31
  127.8 3.3 %collective-permute-start.14 = (bf16[256,1024]{1,0:T(8,128)(2,1)S(1)}, bf16[256,1024]{1,0:T(8,128)(2,1)S(1)}, u32[]{:S(2)}, u32[]{:S(2)}) collective-permute-start(bf16[256,1024]{1,0:T(8,128)(2,1)S(1)} %shard_map.51), channel_id=1, source_target_pairs={{0,4},{4,0},{8,12},{12,8},{16,20},{20,16},{24,28},{28,24},{32,36},... | collective-permute-start | bytes 1572872 | tf_op jit(solution)/shard_map/ppermute | solution.py:47
  129.4 1.7 collective-permute-start.15
  131.8 6.6 %collective-permute-start.16 = (bf16[64,1280]{1,0:T(8,128)(2,1)S(1)}, bf16[64,1280]{1,0:T(8,128)(2,1)S(1)}, u32[]{:S(2)}, u32[]{:S(2)}) collective-permute-start(bf16[64,1280]{1,0:T(8,128)(2,1)S(1)} %get-tuple-element.49), channel_id=1, source_target_pairs={{0,8},{4,12},{8,16},{12,20},{16,24},{20,28},{24,0},{28,4},{32,40},... | collective-permute-start | bytes 491528 | tf_op jit(solution)/shard_map/ppermute | solution.py:36
  132.4 9.7 %collective-permute-start.17 = (bf16[64,1280]{1,0:T(8,128)(2,1)S(1)}, bf16[64,1280]{1,0:T(8,128)(2,1)S(1)}, u32[]{:S(2)}, u32[]{:S(2)}) collective-permute-start(bf16[64,1280]{1,0:T(8,128)(2,1)S(1)} %get-tuple-element.50), channel_id=1, source_target_pairs={{0,16},{4,20},{8,24},{12,28},{16,0},{20,4},{24,8},{28,12},{32,48},... | collective-permute-start | bytes 491528 | tf_op jit(solution)/shard_map/ppermute | solution.py:36
  134.8 7.4 %collective-permute-start.18 = (bf16[64,1280]{1,0:T(8,128)(2,1)S(1)}, bf16[64,1280]{1,0:T(8,128)(2,1)S(1)}, u32[]{:S(2)}, u32[]{:S(2)}) collective-permute-start(bf16[64,1280]{1,0:T(8,128)(2,1)S(1)} %get-tuple-element.51), channel_id=1, source_target_pairs={{0,24},{4,28},{8,0},{12,4},{16,8},{20,12},{24,16},{28,20},{32,56},... | collective-permute-start | bytes 491528 | tf_op jit(solution)/shard_map/ppermute | solution.py:36
  158.1 27.6 %all-to-all-start.3 = ((bf16[32,8,1024]{2,1,0:T(8,128)(2,1)}), bf16[32,8,1024]{2,1,0:T(8,128)(2,1)S(1)}, u32[]{:S(2)}, u32[]{:S(2)}) async-start(bf16[32,8,1024]{2,1,0:T(8,128)(2,1)} %bitcast.9), calls=%async_computation.3 | async-start | bytes 1048576 | tf_op jit(solution)/shard_map/all_to_all | solution.py:51
  165.7 6.0 %collective-permute-start.21 = (f32[64,128]{1,0:T(8,128)S(1)}, f32[64,128]{1,0:T(8,128)S(1)}, u32[]{:S(2)}, u32[]{:S(2)}) collective-permute-start(f32[64,128]{1,0:T(8,128)S(1)} %get-tuple-element.53), channel_id=1, source_target_pairs={{0,1},{1,2},{2,3},{3,0},{4,5},{5,6},{6,7},{7,4},{8,9},{9,10},{10,1... | collective-permute-start | bytes 98312 | tf_op jit(solution)/shard_map/ppermute | solution.py:31
  167.1 4.6 %collective-permute-start.20 = (f32[64,128]{1,0:T(8,128)S(1)}, f32[64,128]{1,0:T(8,128)S(1)}, u32[]{:S(2)}, u32[]{:S(2)}) collective-permute-start(f32[64,128]{1,0:T(8,128)S(1)} %get-tuple-element.53), channel_id=1, source_target_pairs={{0,2},{1,3},{2,0},{3,1},{4,6},{5,7},{6,4},{7,5},{8,10},{9,11},{10,... | collective-permute-start | bytes 98312 | tf_op jit(solution)/shard_map/ppermute | solution.py:31
  168.6 3.1 %collective-permute-start.19 = (f32[64,128]{1,0:T(8,128)S(1)}, f32[64,128]{1,0:T(8,128)S(1)}, u32[]{:S(2)}, u32[]{:S(2)}) collective-permute-start(f32[64,128]{1,0:T(8,128)S(1)} %get-tuple-element.53), channel_id=1, source_target_pairs={{0,3},{1,0},{2,1},{3,2},{4,7},{5,4},{6,5},{7,6},{8,11},{9,8},{10,9... | collective-permute-start | bytes 98312 | tf_op jit(solution)/shard_map/ppermute | solution.py:31
  171.7 3.8 %collective-permute-start.22 = (f32[256,128]{1,0:T(8,128)S(1)}, f32[256,128]{1,0:T(8,128)S(1)}, u32[]{:S(2)}, u32[]{:S(2)}) collective-permute-start(f32[256,128]{1,0:T(8,128)S(1)} %constant_dynamic-update-slice_fusion.own), channel_id=1, source_target_pairs={{0,4},{4,0},{8,12},{12,8},{16,20},{20,16},{24,28},{28,24},{32,36},... | collective-permute-start | bytes 393224 | tf_op jit(solution)/shard_map/ppermute | solution.py:47
  185.7 2.0 %collective-permute-start.23 = (bf16[256,1024]{1,0:T(8,128)(2,1)S(1)}, bf16[256,1024]{1,0:T(8,128)(2,1)S(1)}, u32[]{:S(2)}, u32[]{:S(2)}) collective-permute-start(bf16[256,1024]{1,0:T(8,128)(2,1)S(1)} %bitcast.16), channel_id=1, source_target_pairs={{0,4},{4,0},{8,12},{12,8},{16,20},{20,16},{24,28},{28,24},{32,36},... | collective-permute-start | bytes 1572872 | tf_op jit(solution)/shard_map/ppermute | solution.py:47

commit v5 on v4

--- a/solution.py
+++ b/solution.py
@@ -329,49 +329,64 @@
     return terms[0] + (terms[1] + terms[2])
 
 
-def last_kernel(inverse_root, place, inverse, power, gathered, other, basis, projected, rows, wide, sems):
+def project(inverse, inverse_root, value):
+    scaled = inverse[...] * inverse_root
+    high, low = split(scaled)
+    return jnp.dot(high, value, preferred_element_type=F32) + jnp.dot(
+        low, value, preferred_element_type=F32
+    )
+
+
+def own_kernel(inverse_root, place, inverse, power, gathered, basis, projected, rows, wide, sems):
+    half = gathered.shape[1]
+    columns = pl.ds(pl.multiple_of(place[1] * half, half), half)
+    wide[...] = project(inverse, inverse_root, gathered[...])
+    first = pltpu.make_async_copy(wide, projected.at[:, columns], sems.at[0])
+    first.start()
+    rows[...] = halves_product(power[...], inverse[...], LAST).astype(BF16)
+    second = pltpu.make_async_copy(rows, basis, sems.at[1])
+    second.start()
+    first.wait()
+    second.wait()
+
+
+def other_kernel(inverse_root, place, inverse, other, before, projected, wide, sems):
     half = other.shape[1]
-    scaled = inverse[...] * inverse_root
-    high = scaled.astype(BF16)
-    low = (scaled - high.astype(F32)).astype(BF16)
-    copies = []
-    for i, (at, source) in enumerate(((place[1], gathered), (1 - place[1], other))):
-        columns = pl.ds(pl.multiple_of(at * half, half), half)
-        copies.append(pltpu.make_async_copy(wide.at[i], projected.at[:, columns], sems.at[i]))
-
-        @pl.when(place[0] >= 0)
-        def _(i=i, source=source):
-            value = source[:, :half]
-            wide[i] = jnp.dot(high, value, preferred_element_type=F32) + jnp.dot(
-                low, value, preferred_element_type=F32
-            )
-            copies[i].start()
-
-    copies.append(pltpu.make_async_copy(rows, basis, sems.at[2]))
-    rows[...] = halves_product(power[...], inverse[...], LAST).astype(BF16)
-    copies[2].start()
-    for copy in copies:
-        copy.wait()
-
-
-def last(place, inverse, power, gathered, other, inverse_root):
+    columns = pl.ds(pl.multiple_of((1 - place[1]) * half, half), half)
+    wide[...] = project(inverse, inverse_root, other[...])
+    copy = pltpu.make_async_copy(wide, projected.at[:, columns], sems.at[0])
+    copy.start()
+    copy.wait()
+
+
+def last(place, inverse, power, gathered, inverse_root):
     m, rank = power.shape
-    half = other.shape[1]
-    return pl.pallas_call(
-        functools.partial(last_kernel, inverse_root),
-        in_specs=[SMEM] + [VMEM] * 4,
+    half = gathered.shape[1]
+    projected = jax.ShapeDtypeStruct((rank, NC * half), F32)
+    other = from_core(gathered)
+    basis, partly = pl.pallas_call(
+        functools.partial(own_kernel, inverse_root),
+        in_specs=[SMEM] + [VMEM] * 3,
         out_specs=[HBM] * 2,
-        out_shape=[
-            jax.ShapeDtypeStruct((m, rank), BF16),
-            jax.ShapeDtypeStruct((rank, NC * half), F32),
-        ],
+        out_shape=[jax.ShapeDtypeStruct((m, rank), BF16), projected],
         scratch_shapes=[
             pltpu.VMEM((m, rank), BF16),
-            pltpu.VMEM((NC, rank, half), F32),
-            pltpu.SemaphoreType.DMA((3,)),
+            pltpu.VMEM((rank, half), F32),
+            pltpu.SemaphoreType.DMA((2,)),
         ],
         compiler_params=PRODUCT,
-    )(place, inverse, power, gathered, other)
+        cost_estimate=products(2, rank, half, rank),
+    )(place, inverse, power, gathered)
+    projected = pl.pallas_call(
+        functools.partial(other_kernel, inverse_root),
+        in_specs=[SMEM, VMEM, VMEM, HBM],
+        out_specs=HBM,
+        out_shape=projected,
+        scratch_shapes=[pltpu.VMEM((rank, half), F32), pltpu.SemaphoreType.DMA((1,))],
+        input_output_aliases={3: 0},
+        compiler_params=PRODUCT,
+    )(place, inverse, other, partly)
+    return basis, projected
 
 
 def sum_over_y(one, two, three, own):
@@ -521,7 +536,7 @@
     gram = jnp.concatenate([gram, from_y(gram, 3), from_y(gram, 2), from_y(gram, 1)], axis=0)
     inverse = factor_inverse(place, gram, from_core(gram), 1.0 / token_count)
     wide, inverse = lax.optimization_barrier((wide, inverse))
-    return last(place, inverse, power, wide, from_core(wide), 1.0 / math.sqrt(token_count))
+    return last(place, inverse, power, wide, 1.0 / math.sqrt(token_count))
 
 
 def solution(mesh):

time: 191 us -> 191 us (level)
    pallas_call x1 -> x2, Pallas kernels: 2.62 us -> 4.09 us  [the longest x1 2.12 us: last(): pl.pallas_call(functools.partial(own_kernel, inverse_root), in_specs=[SME...]
  transfers between devices with their start and end apart: 25 -> 25, of which waited for: 13 -> 12; matrix products, arithmetic and copies ran while one was open for 0% -> 0% of each run, Pallas kernels for 11% -> 12%
where the time goes in v5:
time: 191 us; the launch traced here: 190 us
  blocking collectives  63.1 us (33%)
  waiting for transfers between devices  45.5 us (24%)
  starting transfers between devices  44.4 us (23%)
  Pallas kernels  35.9 us (19%)
    all_to_all x2, blocking collectives, exchange(): lax.all_to_all(value, 'rows', 0, 0, tiled=True, axis_index_groups=PLANES)  48.2 us
    ppermute x15, waiting for transfers between devices, from_y(): return lax.ppermute(value, 'cols', Y_SHIFT[k])  38.3 us
    ppermute x15, starting transfers between devices, from_y(): return lax.ppermute(value, 'cols', Y_SHIFT[k])  24.4 us
    all_to_all x1, blocking collectives, exchange_z(): lax.all_to_all(value, 'rows', 0, 0, tiled=True, axis_index_groups=COLUMNS)  14.9 us
    pallas_call x1, Pallas kernels, factor_inverse(): pl.pallas_call(functools.partial(inverse_kernel, scale), in_specs=[SMEM,...  10.2 us
    ppermute x6, starting transfers between devices, from_core(): return lax.ppermute(value, 'rows', CORE_SWAP)  8.17 us
    all_to_all x1, starting transfers between devices, exchange(): lax.all_to_all(value, 'rows', 0, 0, tiled=True, axis_index_groups=PLANES)  7.6 us
    pallas_call x2, Pallas kernels, load_part(): pl.pallas_call(functools.partial(load_kernel, quarters, keep_right), in_s...  7.5 us
  transfers between devices with their start and end apart: 25, of which 12 were waited for; matrix products, arithmetic and copies ran while one was open for 0% of the time, Pallas kernels for 12%

profile of v5, /device:TPU:1, one launch (start us, length us, event | category | flops | bytes accessed | tf_op | source)
XLA Modules:
  0.0 190.4 jit_solution(4501083584822269157)
XLA Ops:
  0.7 3.9 %shard_map.41 = (bf16[512,256]{1,0:T(8,128)(2,1)S(1)}, bf16[512,256]{1,0:T(8,128)(2,1)S(1)}, bf16[512,2048]{1,0:T(8,128)(2,1)S(1)}, bf16[512,2048]{1,0:T(8,128)(2,1)S(1)}, bf16[2048,256]{1,0:T(8,128)(2,1)S(1)}) custom-call(s32[3]{0:T(128)S(1)} %pad_add_fusion.place, bf16[2048,2048]{1,0:T(8,128)(2,1)} %a.3, bf16[2048,256]{1,0:T(8,128)(2,1)} %right.1), custom_call_target="tpu_custom_call" | custom-call | flops 1073741824 | bytes 4194304 | tf_op jit(solution)/shard_map/pallas_call | solution.py:100
  4.7 3.8 %collective-permute-start = (bf16[512,256]{1,0:T(8,128)(2,1)S(1)}, bf16[512,256]{1,0:T(8,128)(2,1)S(1)}, u32[]{:S(2)}, u32[]{:S(2)}) collective-permute-start(bf16[512,256]{1,0:T(8,128)(2,1)S(1)} %get-tuple-element.33), channel_id=1, source_target_pairs={{0,2},{1,3},{2,0},{3,1},{4,6},{5,7},{6,4},{7,5},{8,10},{9,11},{10,... | collective-permute-start | bytes 786440 | tf_op jit(solution)/shard_map/ppermute | solution.py:31
  8.9 3.6 %shard_map.42 = (bf16[512,256]{1,0:T(8,128)(2,1)S(1)}, f32[512,256]{1,0:T(8,128)S(1)}, bf16[512,2048]{1,0:T(8,128)(2,1)S(1)}, bf16[512,2048]{1,0:T(8,128)(2,1)S(1)}) custom-call(s32[3]{0:T(128)S(1)} %pad_add_fusion.place, bf16[2048,2048]{1,0:T(8,128)(2,1)} %a.3, bf16[2048,256]{1,0:T(8,128)(2,1)S(1)} %get-tuple-element.31.right), custom_call_target="tpu_custom_call" | custom-call | flops 1073741824 | bytes 4194304 | tf_op jit(solution)/shard_map/pallas_call | solution.py:100
  12.5 2.4 %collective-permute-start.2 = (bf16[512,256]{1,0:T(8,128)(2,1)S(1)}, bf16[512,256]{1,0:T(8,128)(2,1)S(1)}, u32[]{:S(2)}, u32[]{:S(2)}) collective-permute-start(bf16[512,256]{1,0:T(8,128)(2,1)S(1)} %get-tuple-element.35), channel_id=1, source_target_pairs={{0,3},{1,0},{2,1},{3,2},{4,7},{5,4},{6,5},{7,6},{8,11},{9,8},{10,9... | collective-permute-start | bytes 786440 | tf_op jit(solution)/shard_map/ppermute | solution.py:31
  14.8 5.4 %collective-permute-done.1 = bf16[512,256]{1,0:T(8,128)(2,1)S(1)} collective-permute-done((bf16[512,256]{1,0:T(8,128)(2,1)S(1)}, bf16[512,256]{1,0:T(8,128)(2,1)S(1)}, u32[]{:S(2)}, u32[]{:S(2)}) %collective-permute-start.1) | collective-permute-done | bytes 262176 | tf_op jit(solution)/shard_map/ppermute | solution.py:31
  20.3 2.1 %collective-permute-start.5 = (bf16[512,256]{1,0:T(8,128)(2,1)S(1)}, bf16[512,256]{1,0:T(8,128)(2,1)S(1)}, u32[]{:S(2)}, u32[]{:S(2)}) collective-permute-start(bf16[512,256]{1,0:T(8,128)(2,1)S(1)} %add_convert_fusion.1.image), channel_id=1, source_target_pairs={{0,2},{1,3},{2,0},{3,1},{4,6},{5,7},{6,4},{7,5},{8,10},{9,11},{10,... | collective-permute-start | bytes 786440 | tf_op jit(solution)/shard_map/ppermute | solution.py:31
  23.4 1.7 collective-permute-start.3
  25.8 2.3 %collective-permute-done.5.refs_5_ = bf16[512,256]{1,0:T(8,128)(2,1)S(1)} collective-permute-done((bf16[512,256]{1,0:T(8,128)(2,1)S(1)}, bf16[512,256]{1,0:T(8,128)(2,1)S(1)}, u32[]{:S(2)}, u32[]{:S(2)}) %collective-permute-start.5) | collective-permute-done | bytes 262176 | tf_op jit(solution)/shard_map/ppermute | solution.py:31
  28.2 7.5 %collective-permute-done.4.refs_4_ = bf16[512,256]{1,0:T(8,128)(2,1)S(1)} collective-permute-done((bf16[512,256]{1,0:T(8,128)(2,1)S(1)}, bf16[512,256]{1,0:T(8,128)(2,1)S(1)}, u32[]{:S(2)}, u32[]{:S(2)}) %collective-permute-start.4) | collective-permute-done | bytes 262176 | tf_op jit(solution)/shard_map/ppermute | solution.py:31
  39.6 28.1 %all_to_all.45 = bf16[32,8,1024]{2,1,0:T(8,128)(2,1)S(1)} all-to-all(bf16[32,8,1024]{2,1,0:T(8,128)(2,1)S(1)} %fusion), channel_id=1, replica_groups={{0,8,16,24,32,40,48,56,64,72,80,88,96,104,112,120,128,136,144,152,160,1..., dimensions={0} | all-to-all | bytes 1048576 | tf_op jit(solution)/shard_map/all_to_all | solution.py:51
  67.9 20.1 %all_to_all.46 = bf16[32,8,1024]{2,1,0:T(8,128)(2,1)S(1)} all-to-all(bf16[32,8,1024]{2,1,0:T(8,128)(2,1)S(1)} %bitcast.17), channel_id=1, replica_groups={{0,8,16,24,32,40,48,56,64,72,80,88,96,104,112,120,128,136,144,152,160,1..., dimensions={0} | all-to-all | bytes 1048576 | tf_op jit(solution)/shard_map/all_to_all | solution.py:51
  87.9 3.6 %collective-permute-start.7 = (bf16[256,1024]{1,0:T(8,128)(2,1)S(1)}, bf16[256,1024]{1,0:T(8,128)(2,1)S(1)}, u32[]{:S(2)}, u32[]{:S(2)}) collective-permute-start(bf16[256,1024]{1,0:T(8,128)(2,1)S(1)} %bitcast.14), channel_id=1, source_target_pairs={{0,4},{4,0},{8,12},{12,8},{16,20},{20,16},{24,28},{28,24},{32,36},... | collective-permute-start | bytes 1572872 | tf_op jit(solution)/shard_map/ppermute | solution.py:47
  91.5 1.8 shard_map.47
  93.4 1.8 shard_map.48
  95.2 2.0 %collective-permute-start.8 = (bf16[512,256]{1,0:T(8,128)(2,1)S(1)}, bf16[512,256]{1,0:T(8,128)(2,1)S(1)}, u32[]{:S(2)}, u32[]{:S(2)}) collective-permute-start(bf16[512,256]{1,0:T(8,128)(2,1)S(1)} %get-tuple-element.45), channel_id=1, source_target_pairs={{0,2},{1,3},{2,0},{3,1},{4,6},{5,7},{6,4},{7,5},{8,10},{9,11},{10,... | collective-permute-start | bytes 786440 | tf_op jit(solution)/shard_map/ppermute | solution.py:31
  97.5 2.4 %collective-permute-start.10 = (bf16[512,256]{1,0:T(8,128)(2,1)S(1)}, bf16[512,256]{1,0:T(8,128)(2,1)S(1)}, u32[]{:S(2)}, u32[]{:S(2)}) collective-permute-start(bf16[512,256]{1,0:T(8,128)(2,1)S(1)} %get-tuple-element.47), channel_id=1, source_target_pairs={{0,3},{1,0},{2,1},{3,2},{4,7},{5,4},{6,5},{7,6},{8,11},{9,8},{10,9... | collective-permute-start | bytes 786440 | tf_op jit(solution)/shard_map/ppermute | solution.py:31
  99.9 4.8 %collective-permute-done.8 = bf16[512,256]{1,0:T(8,128)(2,1)S(1)} collective-permute-done((bf16[512,256]{1,0:T(8,128)(2,1)S(1)}, bf16[512,256]{1,0:T(8,128)(2,1)S(1)}, u32[]{:S(2)}, u32[]{:S(2)}) %collective-permute-start.8) | collective-permute-done | bytes 262176 | tf_op jit(solution)/shard_map/ppermute | solution.py:31
  104.7 6.0 %collective-permute-done.9 = bf16[512,256]{1,0:T(8,128)(2,1)S(1)} collective-permute-done((bf16[512,256]{1,0:T(8,128)(2,1)S(1)}, bf16[512,256]{1,0:T(8,128)(2,1)S(1)}, u32[]{:S(2)}, u32[]{:S(2)}) %collective-permute-start.9) | collective-permute-done | bytes 262176 | tf_op jit(solution)/shard_map/ppermute | solution.py:31
  110.8 1.6 collective-permute-start.13
  113.1 2.0 %collective-permute-start.11 = (bf16[512,256]{1,0:T(8,128)(2,1)S(1)}, bf16[512,256]{1,0:T(8,128)(2,1)S(1)}, u32[]{:S(2)}, u32[]{:S(2)}) collective-permute-start(bf16[512,256]{1,0:T(8,128)(2,1)S(1)} %get-tuple-element.60.image.one), channel_id=1, source_target_pairs={{0,3},{1,0},{2,1},{3,2},{4,7},{5,4},{6,5},{7,6},{8,11},{9,8},{10,9... | collective-permute-start | bytes 786440 | tf_op jit(solution)/shard_map/ppermute | solution.py:31
  115.8 4.0 %collective-permute-done.13.refs_5_.three = bf16[512,256]{1,0:T(8,128)(2,1)S(1)} collective-permute-done((bf16[512,256]{1,0:T(8,128)(2,1)S(1)}, bf16[512,256]{1,0:T(8,128)(2,1)S(1)}, u32[]{:S(2)}, u32[]{:S(2)}) %collective-permute-start.13) | collective-permute-done | bytes 262176 | tf_op jit(solution)/shard_map/ppermute | solution.py:31
  119.8 6.4 %collective-permute-done.12.refs_4_.four = bf16[512,256]{1,0:T(8,128)(2,1)S(1)} collective-permute-done((bf16[512,256]{1,0:T(8,128)(2,1)S(1)}, bf16[512,256]{1,0:T(8,128)(2,1)S(1)}, u32[]{:S(2)}, u32[]{:S(2)}) %collective-permute-start.12) | collective-permute-done | bytes 262176 | tf_op jit(solution)/shard_map/ppermute | solution.py:31
  132.4 2.4 %collective-permute-start.17 = (bf16[64,1280]{1,0:T(8,128)(2,1)S(1)}, bf16[64,1280]{1,0:T(8,128)(2,1)S(1)}, u32[]{:S(2)}, u32[]{:S(2)}) collective-permute-start(bf16[64,1280]{1,0:T(8,128)(2,1)S(1)} %get-tuple-element.52), channel_id=1, source_target_pairs={{0,16},{4,20},{8,24},{12,28},{16,0},{20,4},{24,8},{28,12},{32,48},... | collective-permute-start | bytes 491528 | tf_op jit(solution)/shard_map/ppermute | solution.py:36
  136.0 2.4 %collective-permute-done.16.one = bf16[64,1280]{1,0:T(8,128)(2,1)S(1)} collective-permute-done((bf16[64,1280]{1,0:T(8,128)(2,1)S(1)}, bf16[64,1280]{1,0:T(8,128)(2,1)S(1)}, u32[]{:S(2)}, u32[]{:S(2)}) %collective-permute-start.16) | collective-permute-done | bytes 163872 | tf_op jit(solution)/shard_map/ppermute | solution.py:36
  138.4 3.7 %collective-permute-done.17.two = bf16[64,1280]{1,0:T(8,128)(2,1)S(1)} collective-permute-done((bf16[64,1280]{1,0:T(8,128)(2,1)S(1)}, bf16[64,1280]{1,0:T(8,128)(2,1)S(1)}, u32[]{:S(2)}, u32[]{:S(2)}) %collective-permute-start.17) | collective-permute-done | bytes 163872 | tf_op jit(solution)/shard_map/ppermute | solution.py:36
  142.3 14.9 %all_to_all.47 = bf16[8,8,3072]{2,1,0:T(8,128)(2,1)S(1)} all-to-all(bf16[8,8,3072]{2,1,0:T(8,128)(2,1)S(1)} %bitcast.19), channel_id=1, replica_groups={{0,32,64,96,128,160,192,224},{4,36,68,100,132,164,196,228},{8,40,72,104..., dimensions={0} | all-to-all | bytes 786432 | tf_op jit(solution)/shard_map/all_to_all | solution.py:43
  158.1 7.6 %all-to-all-start.3 = ((bf16[32,8,1024]{2,1,0:T(8,128)(2,1)}), bf16[32,8,1024]{2,1,0:T(8,128)(2,1)S(1)}, u32[]{:S(2)}, u32[]{:S(2)}) async-start(bf16[32,8,1024]{2,1,0:T(8,128)(2,1)} %bitcast.9), calls=%async_computation.3 | async-start | bytes 1048576 | tf_op jit(solution)/shard_map/all_to_all | solution.py:51
  169.8 1.9 collective-permute-done.19
  171.7 2.8 %collective-permute-start.22 = (f32[256,128]{1,0:T(8,128)S(1)}, f32[256,128]{1,0:T(8,128)S(1)}, u32[]{:S(2)}, u32[]{:S(2)}) collective-permute-start(f32[256,128]{1,0:T(8,128)S(1)} %constant_dynamic-update-slice_fusion.own), channel_id=1, source_target_pairs={{0,4},{4,0},{8,12},{12,8},{16,20},{20,16},{24,28},{28,24},{32,36},... | collective-permute-start | bytes 393224 | tf_op jit(solution)/shard_map/ppermute | solution.py:47
  175.5 10.2 %shard_map.56.inverse = f32[256,256]{1,0:T(8,128)S(1)} custom-call(s32[3]{0:T(128)S(1)} %pad_add_fusion.place, f32[256,128]{1,0:T(8,128)S(1)} %constant_dynamic-update-slice_fusion.own, f32[256,128]{1,0:T(8,128)S(1)} %collective-permute-done.22.swapped), custom_call_target="tpu_custom_call" | custom-call | flops 1000000000 | bytes 1048576 | tf_op jit(solution)/shard_map/pallas_call | solution.py:312
  186.1 2.1 %shard_map.57 = (bf16[512,256]{1,0:T(8,128)(2,1)}, f32[256,2048]{1,0:T(8,128)}) custom-call(s32[3]{0:T(128)S(1)} %pad_add_fusion.place, f32[256,256]{1,0:T(8,128)S(1)} %shard_map.56.inverse, f32[512,256]{1,0:T(8,128)S(1)} %get-tuple-element.61.power, bf16[256,1024]{1,0:T(8,128)(2,1)S(1)} %bitcast.13), custom_call_target="tpu_custom_call" | custom-call | flops 268435456 | bytes 1048576 | tf_op jit(solution)/shard_map/pallas_call | solution.py:367
  188.3 2.0 %shard_map.58 = f32[256,2048]{1,0:T(8,128)} custom-call(s32[3]{0:T(128)S(1)} %pad_add_fusion.place, f32[256,256]{1,0:T(8,128)S(1)} %shard_map.56.inverse, bf16[256,1024]{1,0:T(8,128)(2,1)S(1)} %collective-permute-done.23.other, f32[256,2048]{1,0:T(8,128)} %get-tuple-element.59.before), custom_call_target="tpu_custom_call", output_to_operand_aliasing={{}: (3, {})} | custom-call | tf_op jit(solution)/shard_map/pallas_call | solution.py:380
  (48 shorter events, 22.1 us)
Async XLA Ops:
  4.7 10.2 %collective-permute-start = (bf16[512,256]{1,0:T(8,128)(2,1)S(1)}, bf16[512,256]{1,0:T(8,128)(2,1)S(1)}, u32[]{:S(2)}, u32[]{:S(2)}) collective-permute-start(bf16[512,256]{1,0:T(8,128)(2,1)S(1)} %get-tuple-element.33), channel_id=1, source_target_pairs={{0,2},{1,3},{2,0},{3,1},{4,6},{5,7},{6,4},{7,5},{8,10},{9,11},{10,... | collective-permute-start | bytes 786440 | tf_op jit(solution)/shard_map/ppermute | solution.py:31
  8.5 11.7 %collective-permute-start.1 = (bf16[512,256]{1,0:T(8,128)(2,1)S(1)}, bf16[512,256]{1,0:T(8,128)(2,1)S(1)}, u32[]{:S(2)}, u32[]{:S(2)}) collective-permute-start(bf16[512,256]{1,0:T(8,128)(2,1)S(1)} %get-tuple-element.34), channel_id=1, source_target_pairs={{0,1},{1,2},{2,3},{3,0},{4,5},{5,6},{6,7},{7,4},{8,9},{9,10},{10,1... | collective-permute-start | bytes 786440 | tf_op jit(solution)/shard_map/ppermute | solution.py:31
  12.5 7.7 %collective-permute-start.2 = (bf16[512,256]{1,0:T(8,128)(2,1)S(1)}, bf16[512,256]{1,0:T(8,128)(2,1)S(1)}, u32[]{:S(2)}, u32[]{:S(2)}) collective-permute-start(bf16[512,256]{1,0:T(8,128)(2,1)S(1)} %get-tuple-element.35), channel_id=1, source_target_pairs={{0,3},{1,0},{2,1},{3,2},{4,7},{5,4},{6,5},{7,6},{8,11},{9,8},{10,9... | collective-permute-start | bytes 786440 | tf_op jit(solution)/shard_map/ppermute | solution.py:31
  20.3 7.9 %collective-permute-start.5 = (bf16[512,256]{1,0:T(8,128)(2,1)S(1)}, bf16[512,256]{1,0:T(8,128)(2,1)S(1)}, u32[]{:S(2)}, u32[]{:S(2)}) collective-permute-start(bf16[512,256]{1,0:T(8,128)(2,1)S(1)} %add_convert_fusion.1.image), channel_id=1, source_target_pairs={{0,2},{1,3},{2,0},{3,1},{4,6},{5,7},{6,4},{7,5},{8,10},{9,11},{10,... | collective-permute-start | bytes 786440 | tf_op jit(solution)/shard_map/ppermute | solution.py:31
  22.4 13.3 %collective-permute-start.4 = (bf16[512,256]{1,0:T(8,128)(2,1)S(1)}, bf16[512,256]{1,0:T(8,128)(2,1)S(1)}, u32[]{:S(2)}, u32[]{:S(2)}) collective-permute-start(bf16[512,256]{1,0:T(8,128)(2,1)S(1)} %add_convert_fusion.1.image), channel_id=1, source_target_pairs={{0,1},{1,2},{2,3},{3,0},{4,5},{5,6},{6,7},{7,4},{8,9},{9,10},{10,1... | collective-permute-start | bytes 786440 | tf_op jit(solution)/shard_map/ppermute | solution.py:31
  23.4 12.3 %collective-permute-start.3 = (bf16[512,256]{1,0:T(8,128)(2,1)S(1)}, bf16[512,256]{1,0:T(8,128)(2,1)S(1)}, u32[]{:S(2)}, u32[]{:S(2)}) collective-permute-start(bf16[512,256]{1,0:T(8,128)(2,1)S(1)} %add_convert_fusion.1.image), channel_id=1, source_target_pairs={{0,3},{1,0},{2,1},{3,2},{4,7},{5,4},{6,5},{7,6},{8,11},{9,8},{10,9... | collective-permute-start | bytes 786440 | tf_op jit(solution)/shard_map/ppermute | solution.py:31
  37.3 2.2 %collective-permute-start.6 = (bf16[256,1024]{1,0:T(8,128)(2,1)S(1)}, bf16[256,1024]{1,0:T(8,128)(2,1)S(1)}, u32[]{:S(2)}, u32[]{:S(2)}) collective-permute-start(bf16[256,1024]{1,0:T(8,128)(2,1)S(1)} %shard_map.45), channel_id=1, source_target_pairs={{0,4},{4,0},{8,12},{12,8},{16,20},{20,16},{24,28},{28,24},{32,36},... | collective-permute-start | bytes 1572872 | tf_op jit(solution)/shard_map/ppermute | solution.py:47
  87.9 5.4 %collective-permute-start.7 = (bf16[256,1024]{1,0:T(8,128)(2,1)S(1)}, bf16[256,1024]{1,0:T(8,128)(2,1)S(1)}, u32[]{:S(2)}, u32[]{:S(2)}) collective-permute-start(bf16[256,1024]{1,0:T(8,128)(2,1)S(1)} %bitcast.14), channel_id=1, source_target_pairs={{0,4},{4,0},{8,12},{12,8},{16,20},{20,16},{24,28},{28,24},{32,36},... | collective-permute-start | bytes 1572872 | tf_op jit(solution)/shard_map/ppermute | solution.py:47
  95.2 9.5 %collective-permute-start.8 = (bf16[512,256]{1,0:T(8,128)(2,1)S(1)}, bf16[512,256]{1,0:T(8,128)(2,1)S(1)}, u32[]{:S(2)}, u32[]{:S(2)}) collective-permute-start(bf16[512,256]{1,0:T(8,128)(2,1)S(1)} %get-tuple-element.45), channel_id=1, source_target_pairs={{0,2},{1,3},{2,0},{3,1},{4,6},{5,7},{6,4},{7,5},{8,10},{9,11},{10,... | collective-permute-start | bytes 786440 | tf_op jit(solution)/shard_map/ppermute | solution.py:31
  97.2 13.4 %collective-permute-start.9 = (bf16[512,256]{1,0:T(8,128)(2,1)S(1)}, bf16[512,256]{1,0:T(8,128)(2,1)S(1)}, u32[]{:S(2)}, u32[]{:S(2)}) collective-permute-start(bf16[512,256]{1,0:T(8,128)(2,1)S(1)} %get-tuple-element.46), channel_id=1, source_target_pairs={{0,1},{1,2},{2,3},{3,0},{4,5},{5,6},{6,7},{7,4},{8,9},{9,10},{10,1... | collective-permute-start | bytes 786440 | tf_op jit(solution)/shard_map/ppermute | solution.py:31
  97.5 13.1 %collective-permute-start.10 = (bf16[512,256]{1,0:T(8,128)(2,1)S(1)}, bf16[512,256]{1,0:T(8,128)(2,1)S(1)}, u32[]{:S(2)}, u32[]{:S(2)}) collective-permute-start(bf16[512,256]{1,0:T(8,128)(2,1)S(1)} %get-tuple-element.47), channel_id=1, source_target_pairs={{0,3},{1,0},{2,1},{3,2},{4,7},{5,4},{6,5},{7,6},{8,11},{9,8},{10,9... | collective-permute-start | bytes 786440 | tf_op jit(solution)/shard_map/ppermute | solution.py:31
  110.8 9.0 %collective-permute-start.13 = (bf16[512,256]{1,0:T(8,128)(2,1)S(1)}, bf16[512,256]{1,0:T(8,128)(2,1)S(1)}, u32[]{:S(2)}, u32[]{:S(2)}) collective-permute-start(bf16[512,256]{1,0:T(8,128)(2,1)S(1)} %get-tuple-element.60.image.one), channel_id=1, source_target_pairs={{0,2},{1,3},{2,0},{3,1},{4,6},{5,7},{6,4},{7,5},{8,10},{9,11},{10,... | collective-permute-start | bytes 786440 | tf_op jit(solution)/shard_map/ppermute | solution.py:31
  112.4 13.8 %collective-permute-start.12 = (bf16[512,256]{1,0:T(8,128)(2,1)S(1)}, bf16[512,256]{1,0:T(8,128)(2,1)S(1)}, u32[]{:S(2)}, u32[]{:S(2)}) collective-permute-start(bf16[512,256]{1,0:T(8,128)(2,1)S(1)} %get-tuple-element.60.image.one), channel_id=1, source_target_pairs={{0,1},{1,2},{2,3},{3,0},{4,5},{5,6},{6,7},{7,4},{8,9},{9,10},{10,1... | collective-permute-start | bytes 786440 | tf_op jit(solution)/shard_map/ppermute | solution.py:31
  113.1 13.1 %collective-permute-start.11 = (bf16[512,256]{1,0:T(8,128)(2,1)S(1)}, bf16[512,256]{1,0:T(8,128)(2,1)S(1)}, u32[]{:S(2)}, u32[]{:S(2)}) collective-permute-start(bf16[512,256]{1,0:T(8,128)(2,1)S(1)} %get-tuple-element.60.image.one), channel_id=1, source_target_pairs={{0,3},{1,0},{2,1},{3,2},{4,7},{5,4},{6,5},{7,6},{8,11},{9,8},{10,9... | collective-permute-start | bytes 786440 | tf_op jit(solution)/shard_map/ppermute | solution.py:31
  127.8 3.3 %collective-permute-start.14 = (bf16[256,1024]{1,0:T(8,128)(2,1)S(1)}, bf16[256,1024]{1,0:T(8,128)(2,1)S(1)}, u32[]{:S(2)}, u32[]{:S(2)}) collective-permute-start(bf16[256,1024]{1,0:T(8,128)(2,1)S(1)} %shard_map.51), channel_id=1, source_target_pairs={{0,4},{4,0},{8,12},{12,8},{16,20},{20,16},{24,28},{28,24},{32,36},... | collective-permute-start | bytes 1572872 | tf_op jit(solution)/shard_map/ppermute | solution.py:47
  129.4 1.7 collective-permute-start.15
  131.8 6.6 %collective-permute-start.16 = (bf16[64,1280]{1,0:T(8,128)(2,1)S(1)}, bf16[64,1280]{1,0:T(8,128)(2,1)S(1)}, u32[]{:S(2)}, u32[]{:S(2)}) collective-permute-start(bf16[64,1280]{1,0:T(8,128)(2,1)S(1)} %get-tuple-element.51), channel_id=1, source_target_pairs={{0,8},{4,12},{8,16},{12,20},{16,24},{20,28},{24,0},{28,4},{32,40},... | collective-permute-start | bytes 491528 | tf_op jit(solution)/shard_map/ppermute | solution.py:36
  132.4 9.7 %collective-permute-start.17 = (bf16[64,1280]{1,0:T(8,128)(2,1)S(1)}, bf16[64,1280]{1,0:T(8,128)(2,1)S(1)}, u32[]{:S(2)}, u32[]{:S(2)}) collective-permute-start(bf16[64,1280]{1,0:T(8,128)(2,1)S(1)} %get-tuple-element.52), channel_id=1, source_target_pairs={{0,16},{4,20},{8,24},{12,28},{16,0},{20,4},{24,8},{28,12},{32,48},... | collective-permute-start | bytes 491528 | tf_op jit(solution)/shard_map/ppermute | solution.py:36
  134.8 7.4 %collective-permute-start.18 = (bf16[64,1280]{1,0:T(8,128)(2,1)S(1)}, bf16[64,1280]{1,0:T(8,128)(2,1)S(1)}, u32[]{:S(2)}, u32[]{:S(2)}) collective-permute-start(bf16[64,1280]{1,0:T(8,128)(2,1)S(1)} %get-tuple-element.53), channel_id=1, source_target_pairs={{0,24},{4,28},{8,0},{12,4},{16,8},{20,12},{24,16},{28,20},{32,56},... | collective-permute-start | bytes 491528 | tf_op jit(solution)/shard_map/ppermute | solution.py:36
  158.1 27.6 %all-to-all-start.3 = ((bf16[32,8,1024]{2,1,0:T(8,128)(2,1)}), bf16[32,8,1024]{2,1,0:T(8,128)(2,1)S(1)}, u32[]{:S(2)}, u32[]{:S(2)}) async-start(bf16[32,8,1024]{2,1,0:T(8,128)(2,1)} %bitcast.9), calls=%async_computation.3 | async-start | bytes 1048576 | tf_op jit(solution)/shard_map/all_to_all | solution.py:51
  165.7 6.0 %collective-permute-start.21 = (f32[64,128]{1,0:T(8,128)S(1)}, f32[64,128]{1,0:T(8,128)S(1)}, u32[]{:S(2)}, u32[]{:S(2)}) collective-permute-start(f32[64,128]{1,0:T(8,128)S(1)} %get-tuple-element.55), channel_id=1, source_target_pairs={{0,1},{1,2},{2,3},{3,0},{4,5},{5,6},{6,7},{7,4},{8,9},{9,10},{10,1... | collective-permute-start | bytes 98312 | tf_op jit(solution)/shard_map/ppermute | solution.py:31
  167.1 4.6 %collective-permute-start.20 = (f32[64,128]{1,0:T(8,128)S(1)}, f32[64,128]{1,0:T(8,128)S(1)}, u32[]{:S(2)}, u32[]{:S(2)}) collective-permute-start(f32[64,128]{1,0:T(8,128)S(1)} %get-tuple-element.55), channel_id=1, source_target_pairs={{0,2},{1,3},{2,0},{3,1},{4,6},{5,7},{6,4},{7,5},{8,10},{9,11},{10,... | collective-permute-start | bytes 98312 | tf_op jit(solution)/shard_map/ppermute | solution.py:31
  168.6 3.1 %collective-permute-start.19 = (f32[64,128]{1,0:T(8,128)S(1)}, f32[64,128]{1,0:T(8,128)S(1)}, u32[]{:S(2)}, u32[]{:S(2)}) collective-permute-start(f32[64,128]{1,0:T(8,128)S(1)} %get-tuple-element.55), channel_id=1, source_target_pairs={{0,3},{1,0},{2,1},{3,2},{4,7},{5,4},{6,5},{7,6},{8,11},{9,8},{10,9... | collective-permute-start | bytes 98312 | tf_op jit(solution)/shard_map/ppermute | solution.py:31
  171.7 3.8 %collective-permute-start.22 = (f32[256,128]{1,0:T(8,128)S(1)}, f32[256,128]{1,0:T(8,128)S(1)}, u32[]{:S(2)}, u32[]{:S(2)}) collective-permute-start(f32[256,128]{1,0:T(8,128)S(1)} %constant_dynamic-update-slice_fusion.own), channel_id=1, source_target_pairs={{0,4},{4,0},{8,12},{12,8},{16,20},{20,16},{24,28},{28,24},{32,36},... | collective-permute-start | bytes 393224 | tf_op jit(solution)/shard_map/ppermute | solution.py:47
  185.7 2.6 %collective-permute-start.23 = (bf16[256,1024]{1,0:T(8,128)(2,1)S(1)}, bf16[256,1024]{1,0:T(8,128)(2,1)S(1)}, u32[]{:S(2)}, u32[]{:S(2)}) collective-permute-start(bf16[256,1024]{1,0:T(8,128)(2,1)S(1)} %bitcast.12), channel_id=1, source_target_pairs={{0,4},{4,0},{8,12},{12,8},{16,20},{20,16},{24,28},{28,24},{32,36},... | collective-permute-start | bytes 1572872 | tf_op jit(solution)/shard_map/ppermute | solution.py:47
